TPU v7x, 32 devices: a whole 2x2x4 slice. The times are simulated.
32 devices in a mesh: dp: 8 (over y, x, core), rows: 4 (over z).
Axes of the slice: x: 2, y: 2, z: 4, core: 2. Of those that a mesh axis runs over, the one named last changes fastest.
Arguments:
- features: bfloat16 [8, 36, 48, 2048], P('dp', 'rows'), may hold values from -6 to 6
- extent: int32 [8, 2], P('dp'), may hold values from 18 to 48, as said below
- pointwise_weight: bfloat16 [2048, 256], P('dp', 'rows'), may hold values from -0.125 to 0.125
- pooling_weight: bfloat16 [2048, 256], P('dp', 'rows'), may hold values from -0.125 to 0.125
- dilated_weight: bfloat16 [55296, 256], P('dp', 'rows'), may hold values from -0.046875 to 0.046875
- projection_weight: bfloat16 [1280, 256], P('dp', 'rows'), may hold values from -0.15625 to 0.15625
- norm_gain: float32 [6, 256], replicated, may hold values from 0.5 to 1.5
- norm_bias: float32 [6, 256], replicated, may hold values from -3 to 3
- cotangent: bfloat16 [8, 36, 48, 256], P('dp', 'rows'), may hold values from -6 to 6
Outputs:
- output: bfloat16 [8, 36, 48, 256], P('dp', 'rows')
- feature_input_gradient: bfloat16 [8, 36, 48, 2048], P('dp', 'rows')
- pointwise_gradient: float32 [2048, 256], P('dp', 'rows')
- pooling_gradient: float32 [2048, 256], P('dp', 'rows')
- dilated_gradient: float32 [55296, 256], P('dp', 'rows')
- projection_gradient: float32 [1280, 256], P('dp', 'rows')
- norm_gain_gradient: float32 [6, 256], replicated
- norm_bias_gradient: float32 [6, 256], replicated
Inputs may be any that keep to these rules, and one draw needn't show every extreme that they name: `extent`: column 0 lies between 18 and 36, column 1 between 24 and 48; the first image fills its whole frame and the last has exactly 18 rows and 24 columns.
All inputs are finite; a program needn't handle non-finite values.
Results may differ from a plain program's by a relative error of at most 0.015.
Values may be sent and summed in bfloat16 or wider, within the bound.
No kernel may reach another device: no remote copies, remote signals or barrier semaphores. Data moves between devices by JAX's collectives and lax.ppermute only.
A program may use at most 384 MiB of HBM per device.

v0:
```python
import jax
import jax.numpy as jnp
from jax import lax
from jax.experimental import pallas as pl
from jax.experimental.pallas import tpu as pltpu
from jax.sharding import PartitionSpec as P

epsilon = 1e-05
dilations = (6, 12, 18)
LANES = 128
BLOCK_ROWS = 6
AXES = ("dp", "rows")
FULL, SHORT, PER_CHIP = 14, 13, 27
SLOTS = FULL + 2 + SHORT
FIRST = 14
CUT = 15
NT = (((1,), (1,)), ((), ()))
TN = (((0,), (0,)), ((), ()))
NN = (((1,), (0,)), ((), ()))


def dot(first, second, dims):
    return lax.dot_general(first, second, dims, preferred_element_type=jnp.float32)


def after(x, *first):
    return lax.optimization_barrier((x, first))[0]


def silu_slope(values):
    sigma = jax.nn.sigmoid(values)
    return sigma * (1.0 + values * (1.0 - sigma))


class Place:
    def __init__(self):
        self.nd, self.nr = lax.axis_size("dp"), lax.axis_size("rows")
        self.nzl = self.nr // 2
        d, z = lax.axis_index("dp"), lax.axis_index("rows")
        self.d, self.z = d, z
        self.m, self.c = d // 2, d % 2
        self.zh, self.zl = z // self.nzl, z % self.nzl
        self.part = self.c * self.nzl + self.zl
        self.image = 2 * self.m + self.zh

    def swap(self, x, m=0, c=0, zh=0, zl=0):
        nzl = self.nzl
        pairs = []
        for flat in range(self.nd * self.nr):
            d, z = divmod(flat, self.nr)
            pairs.append((flat, (d ^ (2 * m + c)) * self.nr + (z ^ (zh * nzl + zl))))
        return lax.ppermute(x, AXES, pairs)


def by_xor(items, index):
    items = list(items)
    bit = 1
    while bit < len(items):
        flip = (index & bit) != 0
        pick = lambda a, b: jnp.where(flip, a, b)
        items = [jax.tree.map(pick, items[k ^ bit], items[k]) for k in range(len(items))]
        bit *= 2
    return items


def tree(items):
    items = list(items)
    while len(items) > 1:
        items = [items[i] + items[i + 1] for i in range(0, len(items), 2)]
    return items[0]


def exchange_stages(place):
    return (
        [dict(c=1)],
        [dict(m=k) for k in range(1, place.nd // 2)],
        [dict(zh=k // place.nzl, zl=k % place.nzl) for k in range(1, place.nr)],
    )


def total(place, x):
    for stage in exchange_stages(place):
        x = tree([x] + [place.swap(x, **s) for s in stage])
    return x


def moments(place, sums, squares, count, extra=None):
    width = sums.shape[1]
    k = sums.shape[0]
    rows = [sums, squares, jnp.full((1, width), count, jnp.float32)]
    if extra is not None:
        rows.append(extra)
    x = jnp.concatenate(rows, axis=0)
    for stage in exchange_stages(place):
        xs = [x] + [place.swap(x, **s) for s in stage]
        whole = tree(xs)
        n = whole[2 * k : 2 * k + 1]
        mean = whole[:k] / jnp.maximum(n, 1.0)
        between = []
        for y in xs:
            own = y[2 * k : 2 * k + 1]
            gap = y[:k] / jnp.maximum(own, 1.0) - mean
            between.append(own * gap * gap)
        x = jnp.concatenate([whole[:k], whole[k : 2 * k] + tree(between), whole[2 * k :]], axis=0)
    n = x[2 * k : 2 * k + 1]
    return x[:k] / n, x[k : 2 * k] / n, n, x[2 * k + 1 :]


def local_moments(values, mask, count):
    sums = jnp.sum(values * mask, axis=0, keepdims=True)
    centred = (values - sums / jnp.maximum(count, 1.0)) * mask
    return sums, jnp.sum(centred * centred, axis=0, keepdims=True)


def line_pieces(place, dilated, pointwise, pooling):
    tiles = lambda w: jnp.transpose(w.T.reshape(w.shape[1], w.shape[0] // LANES, LANES), (1, 0, 2))
    dil, one, pool = tiles(dilated), tiles(pointwise), tiles(pooling)
    other = [dil[2 + r :: 4][:SHORT] for r in range(2)]
    got = place.swap(jnp.concatenate(other, axis=0), c=1)
    same = [jnp.concatenate([dil[r::4][:FULL], one[r : r + 1], pool[r : r + 1]], axis=0) for r in range(2)]
    whole = [jnp.concatenate([same[r], got[r * SHORT : (r + 1) * SHORT]], axis=0) for r in range(2)]
    return by_xor(whole, place.zl)


def plane_direct(place, half):
    return place.swap(half, m=1), place.swap(half, m=2)


def plane_diagonal(place, by_x, by_y):
    return place.swap(by_x[:CUT], m=2), place.swap(by_y[CUT:], m=1)


def add_low(first, *others):
    out = first.astype(jnp.float32)
    for o in others:
        out = out + o.astype(jnp.float32)
    return out.astype(jnp.bfloat16)


def plane_scatter_diagonal(place, pieces):
    return place.swap(pieces[3][0], m=2), place.swap(pieces[3][1], m=1)


def plane_scatter(place, pieces, first_d, second_d):
    to_x = jnp.stack([add_low(pieces[1][0], first_d), pieces[1][1]])
    to_y = jnp.stack([pieces[2][0], add_low(pieces[2][1], second_d)])
    by_x, by_y = place.swap(to_x, m=1), place.swap(to_y, m=2)
    return [add_low(pieces[0][q], by_x[q], by_y[q]) for q in range(2)]


def line_back(place, quarters, first):
    by_kl = by_xor(quarters, place.zl)
    by_part = by_xor([by_kl[0], after(place.swap(by_kl[1], zl=1), first)], place.zl)
    same = [p[: FULL + 2] for p in by_part]
    got = place.swap(jnp.concatenate([p[FULL + 2 :] for p in by_part], axis=0), c=1)
    other = [got[r * SHORT : (r + 1) * SHORT] for r in range(2)]
    gap = jnp.zeros((FULL - SHORT,) + other[0].shape[1:], other[0].dtype)
    dil = jnp.stack([s[:FULL] for s in same] + [jnp.concatenate([o, gap], axis=0) for o in other], axis=1)
    dil = dil.reshape((4 * FULL,) + dil.shape[2:])[: 2 * PER_CHIP]
    rows = lambda t: jnp.transpose(t, (1, 0, 2)).reshape(t.shape[1], t.shape[0] * LANES).astype(jnp.float32).T
    one = jnp.stack([s[FULL] for s in same])
    pool = jnp.stack([s[FULL + 1] for s in same])
    return rows(dil), rows(one), rows(pool)


def gathered_tiles(place, dilated, pointwise, pooling):
    whole = []
    for w in (dilated, pointwise, pooling):
        w = lax.all_gather(w, "rows", axis=1, tiled=True)
        w = lax.all_gather(w, "dp", axis=0, tiled=True)
        channels = pointwise.shape[0] * place.nd
        taps = w.shape[0] // channels
        w = w.reshape(taps, channels // (LANES * place.nr), place.nr, LANES, w.shape[1])
        w = lax.dynamic_index_in_dim(w, place.part, 2, keepdims=False)
        whole.append(jnp.transpose(w.reshape(taps, channels // place.nr, w.shape[-1]), (0, 2, 1)))
    return jnp.concatenate(whole, axis=0)


def scattered_tiles(place, gradients):
    outs = []
    taps, half, width = gradients.shape
    for g in (gradients[: taps - 2], gradients[taps - 2 : taps - 1], gradients[taps - 1 :]):
        g = jnp.transpose(g, (0, 2, 1)).reshape(g.shape[0], width // LANES, 1, LANES, half)
        spread = jnp.zeros((g.shape[0], width // LANES, place.nr, LANES, 2 * half), g.dtype)
        g = lax.dynamic_update_slice(spread, g, (0, 0, place.part, 0, place.zh * half)).reshape(-1, 2 * half)
        g = lax.psum_scatter(g, "dp", scatter_dimension=0, tiled=True)
        outs.append(lax.psum_scatter(g, "rows", scatter_dimension=1, tiled=True).astype(jnp.float32))
    return outs


def doubling(place):
    steps = []
    for name, index, size in (("zl", place.zl, place.nzl), ("zh", place.zh, 2), ("c", place.c, 2), ("m", place.m, place.nd // 2)):
        bit = 1
        while bit < size:
            steps.append(({name: bit}, (index & bit) != 0))
            bit *= 2
    return steps


def joined(place, x, step):
    swap, upper = step
    return jnp.stack(by_xor([x, place.swap(x, **swap)], upper.astype(jnp.int32)))


def halved(place, x, step):
    swap, upper = step
    mine = by_xor([x[0], x[1]], upper.astype(jnp.int32))
    return add_low(mine[0], place.swap(mine[1], **swap))


def m_halved(place, x, steps, first):
    for step in [step for step in steps if "m" in step[0]]:
        if (step[0]["m"] == 1) == (first == 1):
            x = x.reshape((-1, 2) + x.shape[1:])
            x = halved(place, [x[:, k] for k in range(2)], step)
    return x


class Shape:
    def __init__(self, band_rows, columns, nr, width, out, pieces):
        self.band_rows, self.columns, self.nr, self.width, self.out = band_rows, columns, nr, width, out
        self.rows = band_rows * nr
        self.band, self.pixels = band_rows * columns, band_rows * columns * nr
        self.block = BLOCK_ROWS * columns
        self.blocks = self.rows // BLOCK_ROWS
        self.pieces = pieces
        self.quarter = out // 4

    def regions(self, dilation):
        cuts = sorted({0, min(dilation, self.rows), max(self.rows - dilation, 0), self.rows})
        for lo, hi in zip(cuts, cuts[1:]):
            yield lo, hi, [r for r in range(3) if 0 <= lo + (r - 1) * dilation and hi + (r - 1) * dilation <= self.rows]


ANY = pl.BlockSpec(memory_space=pl.ANY)
SMEM = pl.BlockSpec(memory_space=pltpu.SMEM)
VMEM = pl.BlockSpec(memory_space=pltpu.VMEM)
PARAMS = pltpu.CompilerParams(vmem_limit_bytes=58 * 2**20)


LIGHT = pl.CostEstimate(flops=0, bytes_accessed=0, transcendentals=0)


def lanes_at(start, size=LANES):
    return pl.ds(pl.multiple_of(start, LANES), size)


def start_bands(shape, refs, scratch, sem, part):
    for k, ref in enumerate(refs):
        pltpu.make_async_copy(ref, scratch.at[pl.ds((part ^ k) * shape.band, shape.band), :], sem.at[k]).start()


def wait_bands(shape, refs, scratch, sem):
    for k, ref in enumerate(refs):
        pltpu.make_async_copy(ref, scratch.at[pl.ds(k * shape.band, shape.band), :], sem.at[k]).wait()


def split_features(shape, features, mask, c):
    tiles, n = shape.width // LANES, shape.nr // 2

    def kernel(info, x, mask_ref, *outs):
        valid = mask_ref[...].astype(jnp.bfloat16)
        for k, out in enumerate(outs):
            for q in range(n):
                for i in range(tiles):
                    at = (i * shape.nr + (info[0] ^ k) * n + q) * LANES
                    out[q, :, i * LANES : (i + 1) * LANES] = x[:, lanes_at(at)] * valid

    return pl.pallas_call(
        kernel,
        out_shape=[jax.ShapeDtypeStruct((n, shape.band, shape.width), jnp.bfloat16)] * 2,
        in_specs=[SMEM, VMEM, VMEM],
        out_specs=[VMEM] * 2,
        compiler_params=PARAMS,
        cost_estimate=LIGHT,
        name="split_features",
    )(c.reshape(1), features, mask)


def join_features(shape, own, other, c, zl):
    tiles, n = shape.width // LANES, shape.nr // 2

    def kernel(info, *refs):
        for k, part in enumerate(refs[: 2 * n]):
            core, q = info[0] ^ (k // n), info[1] ^ (k % n)
            for i in range(tiles):
                at = (i * shape.nr + core * n + q) * LANES
                refs[2 * n][:, lanes_at(at)] = part[:, i * LANES : (i + 1) * LANES]

    return pl.pallas_call(
        kernel,
        out_shape=jax.ShapeDtypeStruct((shape.band, shape.width * shape.nr), jnp.bfloat16),
        in_specs=[SMEM] + [VMEM] * shape.nr,
        out_specs=VMEM,
        compiler_params=PARAMS,
        cost_estimate=LIGHT,
        name="join_features",
    )(jnp.stack([c, zl]).astype(jnp.int32), *own, *other)


def packed_near(shape, zl, own, neighbour):
    size = shape.quarter

    def kernel(info, own, neighbour, out, rest):
        for kl, ref in enumerate((own, neighbour)):
            out[:, pl.ds(pl.multiple_of((info[0] ^ kl) * size, size), size), :] = ref[...]
        rest[: SLOTS - FIRST] = own[FIRST:]
        rest[SLOTS - FIRST :] = neighbour[...]

    return pl.pallas_call(
        kernel,
        out_shape=[
            jax.ShapeDtypeStruct((SLOTS, 2 * size, LANES), jnp.bfloat16),
            jax.ShapeDtypeStruct((2 * SLOTS - FIRST, size, LANES), jnp.bfloat16),
        ],
        in_specs=[SMEM, VMEM, VMEM],
        out_specs=[VMEM, VMEM],
        compiler_params=PARAMS,
        cost_estimate=LIGHT,
        name="packed_near",
    )(zl.reshape(1), own, neighbour)


def packed_far(shape, zl, first, rest):
    size = shape.quarter

    def kernel(info, first, rest, out):
        for kl in range(2):
            columns = pl.ds(pl.multiple_of((info[0] ^ kl) * size, size), size)
            if kl == 0:
                out[:FIRST, columns, :] = first[...]
                out[FIRST:, columns, :] = rest[: SLOTS - FIRST]
            else:
                out[:, columns, :] = rest[SLOTS - FIRST :]

    return pl.pallas_call(
        kernel,
        out_shape=jax.ShapeDtypeStruct((SLOTS, 2 * size, LANES), jnp.bfloat16),
        in_specs=[SMEM, VMEM, VMEM],
        out_specs=VMEM,
        compiler_params=PARAMS,
        cost_estimate=LIGHT,
        name="packed_far",
    )(zl.reshape(1), first, rest)


def chip_slot(t, c):
    return jnp.where(jnp.where(c == 0, t < FULL, t >= SHORT), t - SHORT * c, FULL + 2 + t - FULL * (1 - c))


def assembled_weights(shape, info, own, by_x, by_y, diagonal):
    def kernel(info, *refs):
        ins, out, sem = refs[:5], refs[5], refs[6]
        m, c = info[0], info[1]

        def copy(ref, slot, tap, lane):
            pltpu.make_async_copy(ref.at[slot], out.at[tap, :, lanes_at(lane)], sem).start()

        def place(rel, slot, tap, lane):
            if rel < 3:
                copy(ins[rel], slot, tap, lane)
            else:

                @pl.when(slot < CUT)
                def _():
                    copy(ins[3], slot, tap, lane)

                @pl.when(slot >= CUT)
                def _():
                    copy(ins[4], slot - CUT, tap, lane)

        for rel in range(4):
            chip = m ^ rel

            def body(t, carry):
                v = chip * PER_CHIP + t
                place(rel, chip_slot(t, c), v // 4, (v % 4) * LANES)
                return carry

            lax.fori_loop(0, PER_CHIP, body, 0)
            for extra in range(2):
                place(rel, FULL + extra, 27 + extra, chip * LANES)
        pltpu.make_async_copy(out, out, sem).wait()

    return pl.pallas_call(
        kernel,
        out_shape=jax.ShapeDtypeStruct((29, shape.out // 2, shape.width), jnp.bfloat16),
        in_specs=[SMEM] + [ANY] * 5,
        out_specs=VMEM,
        scratch_shapes=[pltpu.SemaphoreType.DMA],
        compiler_params=PARAMS,
        cost_estimate=LIGHT,
        name="assembled_weights",
    )(info, own, by_x, by_y, *diagonal)


def shifted(values, by, columns):
    if by == 0:
        return values
    pixels = values.shape[0]
    source = lax.broadcasted_iota(jnp.int32, (pixels, 1), 0) % columns - by
    return jnp.where((source >= 0) & (source < columns), pltpu.roll(values, by % pixels, 0), 0.0)


def send_halves(shape, c, kept, low, outs, sem):
    half = shape.pixels // 2
    copies = []
    for n, (source, core) in enumerate(((kept, c), (low, 1 - c))):
        rows = source.at[pl.ds(pl.multiple_of(core * half, half), half)]
        copies.append(pltpu.make_async_copy(rows, outs[n], sem.at[n]))
    for copy in copies:
        copy.start()
    for copy in copies:
        copy.wait()


def half_shapes(shape, n):
    half = shape.pixels // 2
    return [
        jax.ShapeDtypeStruct((half, n * shape.out), jnp.float32),
        jax.ShapeDtypeStruct((half, n * shape.out), jnp.bfloat16),
    ]


def start_taps(weights, scratch, sem, taps, zh):
    half = weights[0].shape[1]
    for n, tap in enumerate(taps):
        for kh, ref in enumerate(weights):
            columns = pl.ds(pl.multiple_of((zh ^ kh) * half, half), half)
            pltpu.make_async_copy(ref.at[tap], scratch.at[n, columns], sem.at[n]).start()


def wait_taps(scratch, sem, some):
    for n in some:
        pltpu.make_async_copy(scratch.at[n], scratch.at[n], sem.at[n]).wait()


def dilated_products(shape, branch, x, w, first, y):
    dilation, columns = dilations[branch], shape.columns
    for s in range(3):
        for lo, hi, rs in shape.regions(dilation):
            pixels = jnp.concatenate(
                [x[(lo + (r - 1) * dilation) * columns : (hi + (r - 1) * dilation) * columns, :] for r in rs], axis=1
            )
            taps = jnp.concatenate([w[first + 3 * s + r] for r in rs], axis=1)
            y[s, lo * columns : hi * columns, :] = dot(pixels, taps, NT)


def put_dilated(shape, branch, y, kept, low, lane):
    dilation, columns = dilations[branch], shape.columns
    for blk in range(shape.blocks):
        at = slice(blk * shape.block, (blk + 1) * shape.block)
        z = y[1, at, :] + shifted(y[0, at, :], dilation, columns) + shifted(y[2, at, :], -dilation, columns)
        kept[at, lane : lane + shape.out] = z
        low[at, lane : lane + shape.out] = z.astype(jnp.bfloat16)


def taps_of(branch):
    return [9 * branch + 3 * r + s for s in range(3) for r in range(3)]


def branch_sums(shape, info, area, bands, weights):
    nr = shape.nr

    def kernel(info, area, *refs):
        ins, weights = refs[:nr], refs[nr : nr + 2]
        keep, sent, pooled, lifted, x, w, y, kept, low_sums, band_sem, w_sem, out_sem = refs[nr + 2 :]
        start_bands(shape, ins, x, band_sem, info[5])
        start_taps(weights, w, w_sem, taps_of(2) + taps_of(1) + taps_of(0) + [27, 28], info[2])
        wait_bands(shape, ins, x, band_sem)
        wait_taps(w, w_sem, range(29))
        for n, branch in enumerate((2, 1, 0)):
            dilated_products(shape, branch, x, w, 9 * n, y.at[n % 2])
            put_dilated(shape, branch, y.at[n % 2], kept, low_sums, n * shape.out)
        z = dot(x[...], w[27], NT)
        kept[:, 3 * shape.out :] = z
        low_sums[:, 3 * shape.out :] = z.astype(jnp.bfloat16)
        sums = jnp.zeros((1, shape.width), jnp.float32)
        for blk in range(shape.blocks):
            values = x[blk * shape.block : (blk + 1) * shape.block, :]
            sums = sums + jnp.sum(values.astype(jnp.float32), axis=0, keepdims=True)
        low = jnp.broadcast_to(sums / area[0], pooled.shape).astype(jnp.bfloat16)
        first = lax.broadcasted_iota(jnp.int32, pooled.shape, 0) == 0
        pooled[...] = jnp.where(first, low.astype(jnp.float32), 0.0).astype(jnp.bfloat16)
        lifted[...] = dot(pooled[...], w[28], NT)
        send_halves(shape, info[1], kept, low_sums, (keep, sent), out_sem)

    return pl.pallas_call(
        kernel,
        out_shape=half_shapes(shape, 4)
        + [jax.ShapeDtypeStruct((16, shape.width), jnp.bfloat16), jax.ShapeDtypeStruct((16, shape.out), jnp.float32)],
        in_specs=[SMEM, SMEM] + [ANY] * (nr + 2),
        out_specs=[ANY] * 2 + [VMEM] * 2,
        scratch_shapes=[
            pltpu.VMEM((shape.pixels, shape.width), jnp.bfloat16),
            pltpu.VMEM((29, shape.out, shape.width), jnp.bfloat16),
            pltpu.VMEM((2, 3, shape.pixels, shape.out), jnp.float32),
            pltpu.VMEM((shape.pixels, 4 * shape.out), jnp.float32),
            pltpu.VMEM((shape.pixels, 4 * shape.out), jnp.bfloat16),
            pltpu.SemaphoreType.DMA((nr,)),
            pltpu.SemaphoreType.DMA((29,)),
            pltpu.SemaphoreType.DMA((2,)),
        ],
        compiler_params=PARAMS,
        cost_estimate=LIGHT,
        name="branch_sums",
    )(info, area, *bands, *weights)


def moved_columns(shape, delta, lane, lanes, branch, moved):
    for blk in range(shape.blocks):
        at = slice(blk * shape.block, (blk + 1) * shape.block)
        values = delta[at, lanes_at(lane, lanes)].astype(jnp.float32)
        for s in range(3):
            moved[at, s * lanes : (s + 1) * lanes] = shifted(
                values, (s - 1) * dilations[branch], shape.columns
            ).astype(jnp.bfloat16)


def input_gradient(shape, info, area, deltas, pool_delta, weights):
    nr, columns = shape.nr, shape.columns

    def kernel(info, area, *refs):
        ins, pool_delta, weights = refs[:nr], refs[nr], refs[nr + 1 : nr + 3]
        outs = refs[nr + 3 : 2 * nr + 3]
        delta, moved, w, acc, delta_sem, w_sem = refs[2 * nr + 3 :]
        start_bands(shape, ins, delta, delta_sem, info[4])
        start_taps(weights, w, w_sem, range(29), info[2])
        wait_bands(shape, ins, delta, delta_sem)
        wait_taps(w, w_sem, range(29))
        pool = dot(pool_delta[...], w[28], NN)[0:1] / area[0]
        acc[...] = dot(delta[:, : shape.out], w[27], NN) + pool
        for branch in range(3):
            dilation = dilations[branch]
            moved_columns(shape, delta, (branch + 1) * shape.out, shape.out, branch, moved)
            for lo, hi, rs in shape.regions(dilation):
                rows = [2 - r for r in rs]
                cut = lambda r: moved[(lo - (r - 1) * dilation) * columns : (hi - (r - 1) * dilation) * columns, :]
                pixels = jnp.concatenate([cut(r) for r in rows], axis=1)
                taps = jnp.concatenate([w[9 * branch + 3 * r + s] for r in rows for s in range(3)], axis=0)
                acc[lo * columns : hi * columns, :] += dot(pixels, taps, NN)
        pixel = lax.broadcasted_iota(jnp.int32, (shape.band, 1), 0)
        for k in range(nr):
            first = (info[5] ^ k) * shape.band
            inside = ((pixel + first) // columns < info[6]) & (pixel % columns < info[7])
            values = acc[pl.ds(pl.multiple_of(first, shape.band), shape.band), :]
            outs[k][...] = jnp.where(inside, values, 0.0).astype(jnp.bfloat16)

    return pl.pallas_call(
        kernel,
        out_shape=[jax.ShapeDtypeStruct((shape.band, shape.width), jnp.bfloat16)] * nr,
        in_specs=[SMEM, SMEM] + [ANY] * nr + [VMEM] + [ANY] * 2,
        out_specs=[VMEM] * nr,
        scratch_shapes=[
            pltpu.VMEM((shape.pixels, 4 * shape.out), jnp.bfloat16),
            pltpu.VMEM((shape.pixels, 3 * shape.out), jnp.bfloat16),
            pltpu.VMEM((29, shape.out, shape.width), jnp.bfloat16),
            pltpu.VMEM((shape.pixels, shape.width), jnp.float32),
            pltpu.SemaphoreType.DMA((nr,)),
            pltpu.SemaphoreType.DMA((29,)),
        ],
        compiler_params=PARAMS,
        cost_estimate=pl.CostEstimate(
            flops=44 * shape.pixels * shape.width * shape.out, bytes_accessed=2**24, transcendentals=0
        ),
        name="input_gradient",
    )(info, area, *deltas, pool_delta, *weights)


def weight_gradients(shape, info, bands, far_bands, deltas, far_deltas, pool_deltas, pooled):
    nr, columns, half = shape.nr, shape.columns, shape.out // 2
    n_outs = 8 if shape.pieces else 1
    by_rows = lambda v: v.reshape(v.shape[0] // columns, columns, v.shape[1])
    bands = [by_rows(band) for band in [*bands, *far_bands]]

    def kernel(info, *refs):
        ins, delta_ins, far_delta_ins = (refs[n * nr : (n + 1) * nr] for n in range(3))
        far_ins, refs = refs[3 * nr : 4 * nr], refs[4 * nr :]
        pool_deltas, pooled, outs = refs[0], refs[1], refs[2 : 2 + n_outs]
        x, delta, far_delta, moved, grads, sem, out_sem = refs[2 + n_outs :]
        m, c, zh, part, z = info[0], info[1], info[2], info[4], info[5]
        rows = shape.band_rows
        start_bands(shape, delta_ins, delta, sem.at[0], part)
        start_bands(shape, far_delta_ins, far_delta, sem.at[1], part)
        for image, sources in enumerate((ins, far_ins)):
            for k, ref in enumerate(sources):
                pltpu.make_async_copy(ref, x.at[pl.ds((z ^ k) * rows, rows), image], sem.at[2 + image, k]).start()

        def arrive(n):
            for k in range(nr):
                if n < 2:
                    some = (delta, far_delta)[n].at[pl.ds(k * shape.band, shape.band)]
                else:
                    some = x.at[pl.ds(k * rows, rows), n - 2]
                pltpu.make_async_copy(some, some, sem.at[n, k]).wait()

        def move(branch):
            for image, source in enumerate((delta, far_delta)):
                lane = (branch + 1) * half if image else (branch + 1) * shape.out + zh * half
                for blk in range(shape.blocks):
                    at = slice(blk * shape.block, (blk + 1) * shape.block)
                    values = source[at, lanes_at(lane, half)].astype(jnp.float32)
                    for s in range(3):
                        value = shifted(values, (s - 1) * dilations[branch], columns).astype(jnp.bfloat16)
                        moved[blk * BLOCK_ROWS : (blk + 1) * BLOCK_ROWS, image, :, s * half : (s + 1) * half] = (
                            value.reshape(BLOCK_ROWS, columns, half)
                        )

        flat = lambda v: v.reshape(-1, v.shape[-1])

        def put(tap, value):
            value = value.astype(jnp.bfloat16)
            if not shape.pieces:
                grads[tap] = value
                return
            for i in range(4):
                if tap < 27:
                    v = 4 * tap + i
                    chip, slot = v // PER_CHIP, chip_slot(v % PER_CHIP, c)
                else:
                    chip, slot = i, FULL + tap - 27
                for q in range(2):
                    rows = slice(q * shape.quarter, (q + 1) * shape.quarter)
                    grads[2 * (m ^ chip) + q, slot] = value[rows, i * LANES : (i + 1) * LANES]

        arrive(0)
        arrive(1)
        for branch in range(3):
            move(branch)
            if branch == 0:
                arrive(2)
                arrive(3)
            dilation = dilations[branch]
            for r in range(3):
                up, down = max(0, 1 - r) * dilation, max(0, r - 1) * dilation
                to = flat(moved[up : shape.rows - down])
                value = dot(to, flat(x[down : shape.rows - up]), TN)
                for s in range(3):
                    put(9 * branch + 3 * r + s, value[s * half : (s + 1) * half])
        one = jnp.concatenate(
            [
                delta[:, lanes_at(zh * half, half)].reshape(shape.rows, 1, columns, half),
                far_delta[:, :half].reshape(shape.rows, 1, columns, half),
            ],
            axis=1,
        )
        put(27, dot(flat(one), flat(x[...]), TN))
        put(28, dot(pool_deltas[...], pooled[...], TN))
        copies = [pltpu.make_async_copy(grads.at[n] if shape.pieces else grads, outs[n], out_sem.at[n]) for n in range(n_outs)]
        for copy in copies:
            copy.start()
        for copy in copies:
            copy.wait()

    if shape.pieces:
        out_shape = [jax.ShapeDtypeStruct((SLOTS, shape.quarter, LANES), jnp.bfloat16)] * 8
        grads_shape = (8, SLOTS, shape.quarter, LANES)
    else:
        out_shape = [jax.ShapeDtypeStruct((29, half, shape.width), jnp.bfloat16)]
        grads_shape = (29, half, shape.width)
    return pl.pallas_call(
        kernel,
        out_shape=out_shape,
        in_specs=[SMEM] + [ANY] * (4 * nr) + [VMEM] * 2,
        out_specs=[ANY] * n_outs,
        scratch_shapes=[
            pltpu.VMEM((shape.rows, 2, columns, shape.width), jnp.bfloat16),
            pltpu.VMEM((shape.pixels, 4 * shape.out), jnp.bfloat16),
            pltpu.VMEM((shape.pixels, 2 * shape.out), jnp.bfloat16),
            pltpu.VMEM((shape.rows, 2, columns, 3 * half), jnp.bfloat16),
            pltpu.VMEM(grads_shape, jnp.bfloat16),
            pltpu.SemaphoreType.DMA((4, nr)),
            pltpu.SemaphoreType.DMA((n_outs,)),
        ],
        compiler_params=PARAMS,
        cost_estimate=pl.CostEstimate(
            flops=44 * shape.pixels * shape.width * shape.out, bytes_accessed=2**24, transcendentals=0
        ),
        name="weight_gradients",
    )(info, *bands[:nr], *deltas, *far_deltas, *bands[nr:], pool_deltas, pooled)


def valid_pixels(extent, first_row, rows, columns):
    r = first_row + lax.broadcasted_iota(jnp.int32, (rows, columns), 0)
    w = lax.broadcasted_iota(jnp.int32, (rows, columns), 1)
    return ((r < extent[0]) & (w < extent[1])).astype(jnp.float32).reshape(rows * columns, 1)


def to_logical(place, x):
    return jnp.where(place.zh == place.c, x, place.swap(x, c=1, zh=1))


def on_device(
    features, extent, pointwise_weight, pooling_weight, dilated_weight, projection_weight, norm_gain, norm_bias, cotangent
):
    place = Place()
    nr, nzl = place.nr, place.nzl
    _, band_rows, columns, channels = features.shape
    width, out = channels // nr, norm_gain.shape[1]
    band = band_rows * columns
    pieces = nr == 4 and place.nd == 8 and dilated_weight.shape[0] == 2 * PER_CHIP * LANES
    shape = Shape(band_rows, columns, nr, width, out, pieces)
    images = place.nd

    partner = place.swap(extent, c=1)
    extent_here = jnp.where(place.zh == place.c, extent, partner)[0]
    area = (extent_here[0] * extent_here[1]).astype(jnp.float32)
    mask = valid_pixels(extent_here, place.part * band_rows, band_rows, columns)
    own_mask = valid_pixels(extent[0], place.z * band_rows, band_rows, columns)
    here_now = [place.m, place.c, place.zh, place.zl, place.part, place.z, extent_here[0], extent_here[1]]
    info = jnp.stack(here_now).astype(jnp.int32)
    areas = area.reshape(1)

    own_parts, other_parts = split_features(shape, features.reshape(band, channels), own_mask, place.c)
    held = by_xor([own_parts, place.swap(other_parts, c=1)], place.c)
    held = [by_xor([v[q] for q in range(nzl)], place.zl) for v in by_xor(held, place.zh)]

    def sent(image, k, first=()):
        kh, kl = divmod(k, nzl)
        v = held[kh ^ image][kl]
        return place.swap(after(v, first), zh=kh, zl=kl) if k else v

    steps = doubling(place)
    nd_bits = (place.nd // 2).bit_length() - 1
    projection = projection_weight.T
    if pieces:
        sources = line_pieces(place, dilated_weight, pointwise_weight, pooling_weight)
        crossed = place.swap(sources[0][:FIRST], zh=1)
        neighbour = after(place.swap(sources[1], zl=1), crossed, own_parts, other_parts, partner)
        near, rest = packed_near(shape, place.zl, sources[0], neighbour)
        rest = place.swap(rest, zh=1)
        near_x, near_y = plane_direct(place, near)
        near_d = plane_diagonal(place, near_x, near_y)
        far = packed_far(shape, place.zl, crossed, after(rest, near_d, held))
        crossing_band = sent(0, nzl, first=far)
        far_x, far_y = after(plane_direct(place, far), crossing_band)
        far_d = plane_diagonal(place, far_x, far_y)
        bands = [sent(0, k, first=far_x) for k in range(nzl)] + [crossing_band]
        bands += [sent(0, k, first=far_x) for k in range(nzl + 1, nr)]
        near = assembled_weights(shape, info, near, near_x, near_y, near_d)
        weights = [near, assembled_weights(shape, info, far, far_x, far_y, after(far_d, near))]
    else:
        bands = [sent(0, k) for k in range(nr)]
        weights = gathered_tiles(place, dilated_weight, pointwise_weight, pooling_weight)
        weights = by_xor([weights[:, : out // 2], weights[:, out // 2 :]], place.zh)

    def reduce(keep, got):
        bands_of = lambda v: v.reshape(nzl, band, v.shape[1])
        at = lambda k: [lax.dynamic_index_in_dim(bands_of(v), place.zl ^ k, 0, keepdims=False) for v in (keep, got)]
        summed = lambda k: at(k)[0] + at(k)[1].astype(jnp.float32)
        swapped = [place.swap(summed(k).astype(jnp.bfloat16), zl=k) for k in range(1, nzl)]
        return sum((v.astype(jnp.float32) for v in swapped), summed(0))

    ready = (bands, weights)
    keep, given, pooled, lifted = branch_sums(shape, info, areas, bands, weights)
    far_bands = [sent(1, k, first=ready) for k in range(nzl + 1)]
    projection = after(projection, ready)
    for step in steps[: -nd_bits - 2]:
        projection = joined(place, projection, step)
    given = after(given, far_bands, projection)
    projection = joined(place, after(projection, given), steps[-nd_bits - 2])
    got, projection = after((place.swap(given, c=1), projection), projection)
    projection = joined(place, projection, steps[-nd_bits - 1])
    upstream_low = to_logical(place, after(cotangent.reshape(band, out), got))
    plane = [projection] + [place.swap(projection, m=k) for k in range(1, images // 2)]
    sums = after(reduce(keep, got), plane, upstream_low)
    projection = jnp.stack(by_xor(plane, place.m))
    projection = projection.reshape((place.nd, nr) + projection_weight.shape[::-1])
    projection = jnp.transpose(projection, (1, 2, 0, 3)).reshape(out, -1)
    z = [sums[:, k * out : (k + 1) * out] for k in (3, 2, 1, 0)]

    local_count = jnp.sum(mask)
    stats = [local_moments(v, mask, local_count) for v in z]
    table = (lax.broadcasted_iota(jnp.int32, (images, 1), 0) == place.image).astype(jnp.float32) * lifted[0:1]
    average, spread, count, pool_pre = moments(
        place,
        jnp.concatenate([s for s, _ in stats], axis=0),
        jnp.concatenate([q for _, q in stats], axis=0),
        local_count,
        table,
    )
    inv_std = lax.rsqrt(spread + epsilon)
    normed = [(z[k] - average[k : k + 1]) * inv_std[k : k + 1] for k in range(4)]
    pre_act = [norm_gain[k : k + 1] * normed[k] + norm_bias[k : k + 1] for k in range(4)]

    pool_average = jnp.mean(pool_pre, axis=0, keepdims=True)
    pool_centred = pool_pre - pool_average
    pool_inv = lax.rsqrt(jnp.mean(pool_centred * pool_centred, axis=0, keepdims=True) + epsilon)
    pool_normed = pool_centred * pool_inv
    pool_lift = norm_gain[4:5] * pool_normed + norm_bias[4:5]
    here = lambda rows: lax.dynamic_slice_in_dim(rows, place.image, 1, axis=0)
    pool_act = here(jax.nn.silu(pool_lift))

    concat = jnp.concatenate([jax.nn.silu(u) * mask for u in pre_act] + [pool_act * mask], axis=1).astype(jnp.bfloat16)
    pooled_far = place.swap(pooled, zh=1)
    proj_pre = dot(concat, projection, NT)
    proj_sums, proj_squares = local_moments(proj_pre, mask, local_count)
    proj_average, proj_spread, _, _ = moments(place, proj_sums, proj_squares, local_count)
    proj_inv = lax.rsqrt(proj_spread + epsilon)
    proj_normed = (proj_pre - proj_average) * proj_inv
    proj_lift = norm_gain[5:6] * proj_normed + norm_bias[5:6]
    output_here = (jax.nn.silu(proj_lift) * mask).astype(jnp.bfloat16)

    upstream = upstream_low.astype(jnp.float32) * mask * silu_slope(proj_lift)
    sums = jnp.concatenate(
        [jnp.sum(upstream * proj_normed, axis=0, keepdims=True), jnp.sum(upstream, axis=0, keepdims=True)], axis=0
    )
    proj_totals = total(place, sums)
    proj_gain_grad, proj_bias_grad = proj_totals[0:1], proj_totals[1:2]
    gain = norm_gain[5:6]
    proj_delta = (
        mask
        * proj_inv
        * (gain * upstream - gain * proj_bias_grad / count - proj_normed * gain * proj_gain_grad / count)
    ).astype(jnp.bfloat16)
    concat_grad = dot(proj_delta, projection, NN)
    projection_partial = lambda first: dot(after(proj_delta, first), concat, TN)
    branch_up = [
        concat_grad[:, k * out : (k + 1) * out] * mask * silu_slope(pre_act[k]) for k in range(4)
    ]
    pool_part = jnp.sum(concat_grad[:, 4 * out :] * mask, axis=0, keepdims=True)
    table = (lax.broadcasted_iota(jnp.int32, (images, 1), 0) == place.image).astype(jnp.float32) * pool_part
    totals = total(
        place,
        after(jnp.concatenate(
            [jnp.sum(branch_up[k] * normed[k], axis=0, keepdims=True) for k in range(4)]
            + [jnp.sum(branch_up[k], axis=0, keepdims=True) for k in range(4)]
            + [table],
            axis=0,
        ), pooled_far),
    )
    branch_gain_grad, branch_bias_grad = totals[:4], totals[4:8]
    pool_up = totals[8:] * silu_slope(pool_lift)
    pool_gain_grad = jnp.sum(pool_up * pool_normed, axis=0, keepdims=True)
    pool_bias_grad = jnp.sum(pool_up, axis=0, keepdims=True)
    pool_deltas = pool_inv * (
        norm_gain[4:5] * pool_up
        - norm_gain[4:5] * pool_bias_grad / images
        - pool_normed * norm_gain[4:5] * pool_gain_grad / images
    )
    low_rows = lambda rows: jnp.pad(rows, ((0, 16 - rows.shape[0]), (0, 0))).astype(jnp.bfloat16)
    pool_pair = lax.dynamic_slice_in_dim(pool_deltas, 2 * place.m, 2, axis=0)
    halves = lambda v, n: by_xor([v[:, n * out : n * out + out // 2], v[:, n * out + out // 2 : (n + 1) * out]], place.zh)
    deltas = []
    for k in range(4):
        gain = norm_gain[k : k + 1]
        deltas.append(
            mask
            * inv_std[k : k + 1]
            * (
                gain * branch_up[k]
                - gain * branch_bias_grad[k : k + 1] / count
                - normed[k] * gain * branch_gain_grad[k : k + 1] / count
            )
        )
    delta = jnp.concatenate(deltas, axis=1).astype(jnp.bfloat16)
    crossing = jnp.concatenate([halves(delta, k)[1] for k in range(4)], axis=1)

    def over_group(v, first):
        near = [v] + [after(place.swap(v, zl=k), first) for k in range(1, nzl)]
        return near + [place.swap(n, c=1) for n in near]

    crossing = place.swap(crossing, zh=1)
    rows = projection_weight.shape[0]
    part = projection_partial(delta).astype(jnp.bfloat16).reshape(out, images // 2, 2, rows)
    part = jnp.transpose(part, (2, 1, 0, 3)).reshape(2, images // 2, 2, nzl, out // nr, rows)
    part = halved(place, [part[k] for k in range(2)], steps[-nd_bits - 1])
    spread_deltas = over_group(delta, (crossing, part))
    part = m_halved(place, after(part, spread_deltas), steps, 1)
    far_deltas = [crossing] + [place.swap(crossing, zl=k) for k in range(1, nzl)]
    inputs = input_gradient(shape, info, areas, spread_deltas, low_rows(here(pool_deltas)), weights)

    far_bands += [sent(1, k, first=spread_deltas) for k in range(nzl + 1, nr)]
    crossing = after(far_deltas, inputs, far_bands)
    pooled_pair = pooled + jnp.roll(pooled_far, 1, axis=0)
    pool_pair = jnp.concatenate([pool_pair[i : i + 1] for i in range(2)], axis=0)
    pool_pair = jnp.concatenate(by_xor([pool_pair[0:1], pool_pair[1:2]], place.zh), axis=0)
    pool_pair = halves(low_rows(pool_pair), 0)[0]
    far_deltas = crossing + [place.swap(n, c=1) for n in crossing]
    grads = weight_gradients(shape, info, bands, far_bands, spread_deltas, far_deltas, pool_pair, pooled_pair)

    done = (far_deltas, far_bands, part)
    handed = [place.swap(after(inputs[nzl + k], done), zh=1) for k in range(1, nzl)]
    near_handed = [place.swap(after(inputs[k], done), zl=k) for k in range(1, nzl)]
    output = to_logical(place, after(output_here, inputs))
    part = m_halved(place, after(part, inputs), steps, 2)
    crossed = (handed, near_handed, output, part)
    if pieces:
        pairs = [[grads[2 * rel], grads[2 * rel + 1]] for rel in range(4)]
        first_d, second_d = plane_scatter_diagonal(place, pairs)
        first_d, second_d = after((first_d, second_d), crossed, part)
        quarters = plane_scatter(place, pairs, first_d, second_d)
    else:
        quarters = grads
    part, last = after((part, inputs[nzl]), crossed)
    part = part.reshape((2, nzl) + part.shape[-2:])
    part = halved(place, [part[k] for k in range(2)], steps[-nd_bits - 2])
    last = place.swap(last, zh=1)
    handed = [place.swap(after(handed[k - 1], near_handed), zl=k) for k in range(1, nzl)]
    returned = by_xor([[inputs[0]] + near_handed, [last] + handed], place.zh)
    quarters = after(quarters, part, output, returned)
    returned = by_xor(returned, place.c)
    traded = place.swap(jnp.stack(returned[1]), c=1)
    feature_gradient = join_features(shape, returned[0], [traded[k] for k in range(nzl)], place.c, place.zl)
    if pieces:
        dilated_gradient, pointwise_gradient, pooling_gradient = line_back(place, quarters, feature_gradient)
    else:
        dilated_gradient, pointwise_gradient, pooling_gradient = scattered_tiles(place, quarters[0])
    part = after(part, quarters)
    for step in [step for step in steps if "zl" in step[0]]:
        part = part.reshape((-1, 2) + part.shape[-2:])
        part = halved(place, [part[:, k] for k in range(2)], step)
    projection_gradient = part.reshape(out // nr, rows).astype(jnp.float32).T

    return (
        output.reshape(cotangent.shape),
        feature_gradient.reshape(features.shape),
        pointwise_gradient,
        pooling_gradient,
        dilated_gradient,
        projection_gradient,
        jnp.concatenate([branch_gain_grad, pool_gain_grad, proj_gain_grad], axis=0),
        jnp.concatenate([branch_bias_grad, pool_bias_grad, proj_bias_grad], axis=0),
    )


def solution(mesh):
    banded = P("dp", "rows", None, None)
    blocks = P("dp", "rows")
    return jax.shard_map(
        on_device,
        mesh=mesh,
        in_specs=(banded, P("dp", None), blocks, blocks, blocks, blocks, P(), P(), banded),
        out_specs=(banded, banded, blocks, blocks, blocks, blocks, P(), P()),
        check_vma=False,
    )
```

profile of v0, /device:TPU:0, one launch (start us, length us, event | category | flops | bytes accessed | tf_op | source)
XLA Modules:
  0.0 387.8 jit_solution(17289251707328639188)
XLA Ops:
  4.2 3.0 collective-permute-start.4
  8.8 3.2 split_features.1
  12.1 2.7 collective-permute-start.3
  15.9 10.2 %collective-permute-done.3.first = bf16[14,64,128]{2,1,0:T(8,128)(2,1)S(1)} collective-permute-done((bf16[14,64,128]{2,1,0:T(8,128)(2,1)S(1)}, bf16[14,64,128]{2,1,0:T(8,128)(2,1)S(1)}, u32[]{:S(2)}, u32[]{:S(2)}) %collective-permute-start.3) | collective-permute-done | bytes 229408 | tf_op jit(solution)/shard_map/ppermute | solution.py:52
  26.8 2.4 packed_near.1
  29.2 1.5 collective-permute-start.6
  30.7 1.5 collective-permute-start.8
  33.6 15.9 %collective-permute-done.6.refs_1_ = bf16[29,128,128]{2,1,0:T(8,128)(2,1)S(1)} collective-permute-done((bf16[29,128,128]{2,1,0:T(8,128)(2,1)}, bf16[29,128,128]{2,1,0:T(8,128)(2,1)S(1)}, u32[]{:S(2)}, u32[]{:S(2)}) %collective-permute-start.6) | collective-permute-done | bytes 950304 | tf_op jit(solution)/shard_map/ppermute | solution.py:52
  49.6 1.7 collective-permute-start.7
  55.3 7.7 %collective-permute-done.5.rest = bf16[44,64,128]{2,1,0:T(8,128)(2,1)S(1)} collective-permute-done((bf16[44,64,128]{2,1,0:T(8,128)(2,1)}, bf16[44,64,128]{2,1,0:T(8,128)(2,1)S(1)}, u32[]{:S(2)}, u32[]{:S(2)}) %collective-permute-start.5) | collective-permute-done | bytes 720928 | tf_op jit(solution)/shard_map/ppermute | solution.py:52
  63.8 2.2 packed_far.1.refs_0_
  67.1 1.6 collective-permute-start.12
  68.7 17.3 %collective-permute-done.12.refs_2_ = bf16[432,512]{1,0:T(8,128)(2,1)S(1)} collective-permute-done((bf16[432,512]{1,0:T(8,128)(2,1)S(1)}, bf16[432,512]{1,0:T(8,128)(2,1)S(1)}, u32[]{:S(2)}, u32[]{:S(2)}) %collective-permute-start.12) | collective-permute-done | bytes 442400 | tf_op jit(solution)/shard_map/ppermute | solution.py:52
  89.3 1.5 collective-permute-start.16
  90.8 2.5 collective-permute-start.13
  93.3 2.7 collective-permute-start.14
  96.6 1.9 stack.122.info
  98.5 5.9 %assembled_weights.2.refs_4_.refs_5_ = bf16[29,128,512]{2,1,0:T(8,128)(2,1)} custom-call(s32[8]{0:T(128)} %stack.122.info, bf16[29,128,128]{2,1,0:T(8,128)(2,1)} %get-tuple-element.70.refs_0_, bf16[29,128,128]{2,1,0:T(8,128)(2,1)} %copy-done.3, bf16[29,128,128]{2,1,0:T(8,128)(2,1)} %copy-done.5, bf16[15,128,128]{2,1,0:T(8,128)(2,1)} %copy-done.19, ...), custom_call_target="tpu_custom_call" | custom-call | tf_op jit(solution)/shard_map/assembled_weights/pallas_call | solution.py:386
  104.5 5.4 %assembled_weights.3.refs_5_.refs_6_ = bf16[29,128,512]{2,1,0:T(8,128)(2,1)} custom-call(s32[8]{0:T(128)} %stack.122.info, bf16[29,128,128]{2,1,0:T(8,128)(2,1)} %packed_far.1.refs_0_, bf16[29,128,128]{2,1,0:T(8,128)(2,1)} %copy-done.4, bf16[29,128,128]{2,1,0:T(8,128)(2,1)} %copy-done.6, bf16[15,128,128]{2,1,0:T(8,128)(2,1)} %collective-permute-done.15.refs_3_, ...), custom_call_target="tpu_custom_call" | custom-call | tf_op jit(solution)/shard_map/assembled_weights/pallas_call | solution.py:386
  109.9 4.4 %collective-permute-done.14.refs_3_ = bf16[432,512]{1,0:T(8,128)(2,1)} collective-permute-done((bf16[432,512]{1,0:T(8,128)(2,1)}, bf16[432,512]{1,0:T(8,128)(2,1)}, u32[]{:S(2)}, u32[]{:S(2)}) %collective-permute-start.14) | collective-permute-done | bytes 442400 | tf_op jit(solution)/shard_map/ppermute | solution.py:52
  114.8 1.7 collective-permute-start.18
  116.5 2.0 collective-permute-start.19
  119.9 18.4 %branch_sums.1 = (f32[864,1024]{1,0:T(8,128)}, bf16[864,1024]{1,0:T(8,128)(2,1)}, bf16[16,512]{1,0:T(8,128)(2,1)}, f32[16,256]{1,0:T(8,128)}) custom-call(s32[8]{0:T(128)} %stack.122.info, f32[1]{0:T(128)} %bitcast.12.area, bf16[432,512]{1,0:T(8,128)(2,1)} %bitcast.306, bf16[432,512]{1,0:T(8,128)(2,1)} %copy-done.29, bf16[432,512]{1,0:T(8,128)(2,1)} %copy-done.28, ...), custom_call_target="tpu_custom_call" | custom-call | tf_op jit(solution)/shard_map/branch_sums/pallas_call | solution.py:489
  142.1 5.3 %collective-permute-done.21 = bf16[2,64,160]{2,1,0:T(8,128)(2,1)S(1)} collective-permute-done((bf16[2,64,160]{2,1,0:T(8,128)(2,1)S(1)}, bf16[2,64,160]{2,1,0:T(8,128)(2,1)S(1)}, u32[]{:S(2)}, u32[]{:S(2)}) %collective-permute-start.21) | collective-permute-done | bytes 40992 | tf_op jit(solution)/shard_map/ppermute | solution.py:52
  147.5 1.8 fusion.2
  151.7 1.8 collective-permute-start.27
  154.9 1.6 collective-permute-start.25
  157.8 15.8 %collective-permute-done.27 = bf16[432,256]{1,0:T(8,128)(2,1)S(1)} collective-permute-done((bf16[432,256]{1,0:T(8,128)(2,1)S(1)}, bf16[432,256]{1,0:T(8,128)(2,1)S(1)}, u32[]{:S(2)}, u32[]{:S(2)}) %collective-permute-start.27) | collective-permute-done | bytes 221216 | tf_op jit(solution)/shard_map/ppermute | solution.py:52
  174.3 1.6 collective-permute-done.22
  175.9 2.1 bitcast_add_fusion
  183.0 1.6 collective-permute-start.30
  185.1 1.5 collective-permute-start.29
  187.7 1.6 collective-permute-done.31
  192.6 1.5 collective-permute-start.32
  196.1 1.5 collective-permute-done.34
  208.9 1.4 collective-permute-start.38
  211.4 2.0 collective-permute-done.38
  214.7 1.6 collective-permute-start.41
  218.6 1.5 collective-permute-done.41
  222.4 1.6 collective-permute-start.44
  226.1 2.4 collective-permute-done.45
  229.7 2.3 collective-permute-start.48
  232.1 2.0 collective-permute-start.49
  238.3 2.0 multiply_reduce_fusion
  245.6 2.1 collective-permute-done.53
  248.9 1.8 collective-permute-start.56
  259.6 1.6 collective-permute-start.58
  263.4 20.5 %collective-permute-done.58.refs_8_ = bf16[432,512]{1,0:T(8,128)(2,1)} collective-permute-done((bf16[432,512]{1,0:T(8,128)(2,1)S(1)}, bf16[432,512]{1,0:T(8,128)(2,1)}, u32[]{:S(2)}, u32[]{:S(2)}) %collective-permute-start.58) | collective-permute-done | bytes 442400 | tf_op jit(solution)/shard_map/ppermute | solution.py:52
  283.9 1.8 collective-permute-done.57.refs_1_.refs_5_
  290.2 2.3 collective-permute-start.66
  292.5 17.9 %input_gradient.1 = (bf16[432,512]{1,0:T(8,128)(2,1)}, bf16[432,512]{1,0:T(8,128)(2,1)}, bf16[432,512]{1,0:T(8,128)(2,1)}, bf16[432,512]{1,0:T(8,128)(2,1)}) custom-call(s32[8]{0:T(128)} %stack.122.info, f32[1]{0:T(128)} %bitcast.12.area, bf16[432,1024]{1,0:T(8,128)(2,1)} %pad_maximum_fusion.4.refs_0_.refs_4_, ...), custom_call_target="tpu_custom_call" | custom-call | flops 9965666304 | bytes 16777216 | tf_op jit(solution)/shard_map/input_gradient/pallas_call | solution.py:550
  311.7 2.2 collective-permute-start.64
  313.9 1.9 collective-permute-start.69
  316.5 17.6 %weight_gradients.1 = (bf16[29,64,128]{2,1,0:T(8,128)(2,1)}, bf16[29,64,128]{2,1,0:T(8,128)(2,1)}, bf16[29,64,128]{2,1,0:T(8,128)(2,1)}, bf16[29,64,128]{2,1,0:T...) custom-call(s32[8]{0:T(128)} %stack.122.info, ...), custom_call_target="tpu_custom_call" | custom-call | flops 9965666304 | bytes 16777216 | tf_op jit(solution)/shard_map/weight_gradients/pallas_call | solution.py:662
  334.1 1.9 collective-permute-start.74
  336.9 5.1 %collective-permute-done.69 = bf16[432,512]{1,0:T(8,128)(2,1)S(1)} collective-permute-done((bf16[432,512]{1,0:T(8,128)(2,1)}, bf16[432,512]{1,0:T(8,128)(2,1)S(1)}, u32[]{:S(2)}, u32[]{:S(2)}) %collective-permute-start.69) | collective-permute-done | bytes 442400 | tf_op jit(solution)/shard_map/ppermute | solution.py:52
  342.1 2.1 collective-permute-start.72
  345.1 1.7 collective-permute-done.74
  346.8 1.5 collective-permute-done.75
  351.2 15.2 %collective-permute-done.78 = bf16[2,64,160]{2,1,0:T(8,128)(2,1)S(1)} collective-permute-done((bf16[2,64,160]{2,1,0:T(8,128)(2,1)S(1)}, bf16[2,64,160]{2,1,0:T(8,128)(2,1)S(1)}, u32[]{:S(2)}, u32[]{:S(2)}) %collective-permute-start.78) | collective-permute-done | bytes 40992 | tf_op jit(solution)/shard_map/ppermute | solution.py:52
  368.5 2.4 collective-permute-done.77
  374.7 2.2 collective-permute-done.81
  378.5 3.1 join_features.1
  381.6 2.0 collective-permute-done.79
  (473 shorter events, 103.9 us)
Async XLA Ops:
  4.2 21.8 %collective-permute-start.4 = (bf16[29,64,128]{2,1,0:T(8,128)(2,1)S(1)}, bf16[29,64,128]{2,1,0:T(8,128)(2,1)S(1)}, u32[]{:S(2)}, u32[]{:S(2)}) collective-permute-start(bf16[29,64,128]{2,1,0:T(8,128)(2,1)S(1)} %get-tuple-element.172), channel_id=1, source_target_pairs={{0,1},{1,0},{2,3},{3,2},{4,5},{5,4},{6,7},{7,6},{8,9},{9,8},{10,11... | collective-permute-start | bytes 1425416 | tf_op jit(solution)/shard_map/ppermute | solution.py:52
  12.0 20.3 %collective-permute-start.1 = (bf16[2,432,512]{2,1,0:T(8,128)(2,1)}, bf16[2,432,512]{2,1,0:T(8,128)(2,1)}, u32[]{:S(2)}, u32[]{:S(2)}) collective-permute-start(bf16[2,432,512]{2,1,0:T(8,128)(2,1)} %get-tuple-element.67), channel_id=1, source_target_pairs={{0,4},{1,5},{2,6},{3,7},{4,0},{5,1},{6,2},{7,3},{8,12},{9,13},{10,... | collective-permute-start | bytes 2654216 | tf_op jit(solution)/shard_map/ppermute | solution.py:52
  12.1 13.9 %collective-permute-start.3 = (bf16[14,64,128]{2,1,0:T(8,128)(2,1)S(1)}, bf16[14,64,128]{2,1,0:T(8,128)(2,1)S(1)}, u32[]{:S(2)}, u32[]{:S(2)}) collective-permute-start(bf16[14,64,128]{2,1,0:T(8,128)(2,1)S(1)} %slice.706), channel_id=1, source_target_pairs={{0,2},{1,3},{2,0},{3,1},{4,6},{5,7},{6,4},{7,5},{8,10},{9,11},{10,... | collective-permute-start | bytes 688136 | tf_op jit(solution)/shard_map/ppermute | solution.py:52
  29.2 20.3 %collective-permute-start.6 = (bf16[29,128,128]{2,1,0:T(8,128)(2,1)}, bf16[29,128,128]{2,1,0:T(8,128)(2,1)S(1)}, u32[]{:S(2)}, u32[]{:S(2)}) collective-permute-start(bf16[29,128,128]{2,1,0:T(8,128)(2,1)} %get-tuple-element.70.refs_0_), channel_id=1, source_target_pairs={{0,8},{1,9},{2,10},{3,11},{4,12},{5,13},{6,14},{7,15},{8,0},{9,1},... | collective-permute-start | bytes 2850824 | tf_op jit(solution)/shard_map/ppermute | solution.py:52
  30.7 21.9 %collective-permute-start.8 = (bf16[29,128,128]{2,1,0:T(8,128)(2,1)}, bf16[29,128,128]{2,1,0:T(8,128)(2,1)S(1)}, u32[]{:S(2)}, u32[]{:S(2)}) collective-permute-start(bf16[29,128,128]{2,1,0:T(8,128)(2,1)} %get-tuple-element.70.refs_0_), channel_id=1, source_target_pairs={{0,16},{1,17},{2,18},{3,19},{4,20},{5,21},{6,22},{7,23},{8,24},{9,... | collective-permute-start | bytes 2850824 | tf_op jit(solution)/shard_map/ppermute | solution.py:52
  32.3 30.7 %collective-permute-start.5 = (bf16[44,64,128]{2,1,0:T(8,128)(2,1)}, bf16[44,64,128]{2,1,0:T(8,128)(2,1)S(1)}, u32[]{:S(2)}, u32[]{:S(2)}) collective-permute-start(bf16[44,64,128]{2,1,0:T(8,128)(2,1)} %get-tuple-element.69), channel_id=1, source_target_pairs={{0,2},{1,3},{2,0},{3,1},{4,6},{5,7},{6,4},{7,5},{8,10},{9,11},{10,... | collective-permute-start | bytes 2162696 | tf_op jit(solution)/shard_map/ppermute | solution.py:52
  49.6 13.4 %collective-permute-start.7 = (bf16[15,128,128]{2,1,0:T(8,128)(2,1)S(1)}, bf16[15,128,128]{2,1,0:T(8,128)(2,1)S(1)}, u32[]{:S(2)}, u32[]{:S(2)}) collective-permute-start(bf16[15,128,128]{2,1,0:T(8,128)(2,1)S(1)} %slice.707), channel_id=1, source_target_pairs={{0,16},{1,17},{2,18},{3,19},{4,20},{5,21},{6,22},{7,23},{8,24},{9,... | collective-permute-start | bytes 1474568 | tf_op jit(solution)/shard_map/ppermute | solution.py:52
  52.7 10.2 %collective-permute-start.9 = (bf16[14,128,128]{2,1,0:T(8,128)(2,1)S(1)}, bf16[14,128,128]{2,1,0:T(8,128)(2,1)S(1)}, u32[]{:S(2)}, u32[]{:S(2)}) collective-permute-start(bf16[14,128,128]{2,1,0:T(8,128)(2,1)S(1)} %slice.708), channel_id=1, source_target_pairs={{0,8},{1,9},{2,10},{3,11},{4,12},{5,13},{6,14},{7,15},{8,0},{9,1},... | collective-permute-start | bytes 1376264 | tf_op jit(solution)/shard_map/ppermute | solution.py:52
  66.1 20.2 %collective-permute-start.10 = (bf16[29,128,128]{2,1,0:T(8,128)(2,1)}, bf16[29,128,128]{2,1,0:T(8,128)(2,1)S(1)}, u32[]{:S(2)}, u32[]{:S(2)}) collective-permute-start(bf16[29,128,128]{2,1,0:T(8,128)(2,1)} %packed_far.1.refs_0_), channel_id=1, source_target_pairs={{0,8},{1,9},{2,10},{3,11},{4,12},{5,13},{6,14},{7,15},{8,0},{9,1},... | collective-permute-start | bytes 2850824 | tf_op jit(solution)/shard_map/ppermute | solution.py:52
  66.6 20.8 %collective-permute-start.11 = (bf16[29,128,128]{2,1,0:T(8,128)(2,1)}, bf16[29,128,128]{2,1,0:T(8,128)(2,1)S(1)}, u32[]{:S(2)}, u32[]{:S(2)}) collective-permute-start(bf16[29,128,128]{2,1,0:T(8,128)(2,1)} %packed_far.1.refs_0_), channel_id=1, source_target_pairs={{0,16},{1,17},{2,18},{3,19},{4,20},{5,21},{6,22},{7,23},{8,24},{9,... | collective-permute-start | bytes 2850824 | tf_op jit(solution)/shard_map/ppermute | solution.py:52
  67.1 19.0 %collective-permute-start.12 = (bf16[432,512]{1,0:T(8,128)(2,1)S(1)}, bf16[432,512]{1,0:T(8,128)(2,1)S(1)}, u32[]{:S(2)}, u32[]{:S(2)}) collective-permute-start(bf16[432,512]{1,0:T(8,128)(2,1)S(1)} %bitcast.313), channel_id=1, source_target_pairs={{0,2},{1,3},{2,0},{3,1},{4,6},{5,7},{6,4},{7,5},{8,10},{9,11},{10,... | collective-permute-start | bytes 1327112 | tf_op jit(solution)/shard_map/ppermute | solution.py:52
  87.4 17.0 %collective-permute-start.15 = (bf16[15,128,128]{2,1,0:T(8,128)(2,1)S(1)}, bf16[15,128,128]{2,1,0:T(8,128)(2,1)}, u32[]{:S(2)}, u32[]{:S(2)}) collective-permute-start(bf16[15,128,128]{2,1,0:T(8,128)(2,1)S(1)} %slice.565), channel_id=1, source_target_pairs={{0,16},{1,17},{2,18},{3,19},{4,20},{5,21},{6,22},{7,23},{8,24},{9,... | collective-permute-start | bytes 1474568 | tf_op jit(solution)/shard_map/ppermute | solution.py:52
  89.3 15.1 %collective-permute-start.16 = (bf16[14,128,128]{2,1,0:T(8,128)(2,1)}, bf16[14,128,128]{2,1,0:T(8,128)(2,1)}, u32[]{:S(2)}, u32[]{:S(2)}) collective-permute-start(bf16[14,128,128]{2,1,0:T(8,128)(2,1)} %slice.566), channel_id=1, source_target_pairs={{0,8},{1,9},{2,10},{3,11},{4,12},{5,13},{6,14},{7,15},{8,0},{9,1},... | collective-permute-start | bytes 1376264 | tf_op jit(solution)/shard_map/ppermute | solution.py:52
  90.8 19.1 %collective-permute-start.13 = (bf16[432,512]{1,0:T(8,128)(2,1)}, bf16[432,512]{1,0:T(8,128)(2,1)S(1)}, u32[]{:S(2)}, u32[]{:S(2)}) collective-permute-start(bf16[432,512]{1,0:T(8,128)(2,1)} %get-tuple-element.102), channel_id=1, source_target_pairs={{0,1},{1,0},{2,3},{3,2},{4,5},{5,4},{6,7},{7,6},{8,9},{9,8},{10,11... | collective-permute-start | bytes 1327112 | tf_op jit(solution)/shard_map/ppermute | solution.py:52
  93.3 21.1 %collective-permute-start.14 = (bf16[432,512]{1,0:T(8,128)(2,1)}, bf16[432,512]{1,0:T(8,128)(2,1)}, u32[]{:S(2)}, u32[]{:S(2)}) collective-permute-start(bf16[432,512]{1,0:T(8,128)(2,1)} %get-tuple-element.81), channel_id=1, source_target_pairs={{0,3},{1,2},{2,1},{3,0},{4,7},{5,6},{6,5},{7,4},{8,11},{9,10},{10,... | collective-permute-start | bytes 1327112 | tf_op jit(solution)/shard_map/ppermute | solution.py:52
  114.3 24.1 %collective-permute-start.17 = (bf16[432,512]{1,0:T(8,128)(2,1)}, bf16[432,512]{1,0:T(8,128)(2,1)S(1)}, u32[]{:S(2)}, u32[]{:S(2)}) collective-permute-start(bf16[432,512]{1,0:T(8,128)(2,1)} %get-tuple-element.81), channel_id=1, source_target_pairs={{0,1},{1,0},{2,3},{3,2},{4,5},{5,4},{6,7},{7,6},{8,9},{9,8},{10,11... | collective-permute-start | bytes 1327112 | tf_op jit(solution)/shard_map/ppermute | solution.py:52
  114.8 23.6 %collective-permute-start.18 = (bf16[432,512]{1,0:T(8,128)(2,1)S(1)}, bf16[432,512]{1,0:T(8,128)(2,1)S(1)}, u32[]{:S(2)}, u32[]{:S(2)}) collective-permute-start(bf16[432,512]{1,0:T(8,128)(2,1)S(1)} %bitcast.305), channel_id=1, source_target_pairs={{0,2},{1,3},{2,0},{3,1},{4,6},{5,7},{6,4},{7,5},{8,10},{9,11},{10,... | collective-permute-start | bytes 1327112 | tf_op jit(solution)/shard_map/ppermute | solution.py:52
  116.5 21.8 %collective-permute-start.19 = (bf16[64,160]{1,0:T(8,128)(2,1)S(1)}, bf16[64,160]{1,0:T(8,128)(2,1)S(1)}, u32[]{:S(2)}, u32[]{:S(2)}) collective-permute-start(bf16[64,160]{1,0:T(8,128)(2,1)S(1)} %bitcast.320), channel_id=1, source_target_pairs={{0,1},{1,0},{2,3},{3,2},{4,5},{5,4},{6,7},{7,6},{8,9},{9,8},{10,11... | collective-permute-start | bytes 61448 | tf_op jit(solution)/shard_map/ppermute | solution.py:52
  139.1 8.3 %collective-permute-start.20 = (bf16[864,1024]{1,0:T(8,128)(2,1)}, bf16[864,1024]{1,0:T(8,128)(2,1)S(1)}, u32[]{:S(2)}, u32[]{:S(2)}) collective-permute-start(bf16[864,1024]{1,0:T(8,128)(2,1)} %get-tuple-element.84), channel_id=1, source_target_pairs={{0,4},{1,5},{2,6},{3,7},{4,0},{5,1},{6,2},{7,3},{8,12},{9,13},{10,... | collective-permute-start | bytes 5308424 | tf_op jit(solution)/shard_map/ppermute | solution.py:52
  141.2 6.2 %collective-permute-start.21 = (bf16[2,64,160]{2,1,0:T(8,128)(2,1)S(1)}, bf16[2,64,160]{2,1,0:T(8,128)(2,1)S(1)}, u32[]{:S(2)}, u32[]{:S(2)}) collective-permute-start(bf16[2,64,160]{2,1,0:T(8,128)(2,1)S(1)} %pad_maximum_fusion.13), channel_id=1, source_target_pairs={{0,2},{1,3},{2,0},{3,1},{4,6},{5,7},{6,4},{7,5},{8,10},{9,11},{10,... | collective-permute-start | bytes 122888 | tf_op jit(solution)/shard_map/ppermute | solution.py:52
  149.3 26.5 %collective-permute-start.22 = (bf16[432,1024]{1,0:T(8,128)(2,1)S(1)}, bf16[432,1024]{1,0:T(8,128)(2,1)}, u32[]{:S(2)}, u32[]{:S(2)}) collective-permute-start(bf16[432,1024]{1,0:T(8,128)(2,1)S(1)} %fusion.2), channel_id=1, source_target_pairs={{0,1},{1,0},{2,3},{3,2},{4,5},{5,4},{6,7},{7,6},{8,9},{9,8},{10,11... | collective-permute-start | bytes 2654216 | tf_op jit(solution)/shard_map/ppermute | solution.py:52
  151.7 21.9 %collective-permute-start.27 = (bf16[432,256]{1,0:T(8,128)(2,1)S(1)}, bf16[432,256]{1,0:T(8,128)(2,1)S(1)}, u32[]{:S(2)}, u32[]{:S(2)}) collective-permute-start(bf16[432,256]{1,0:T(8,128)(2,1)S(1)} %bitcast.317), channel_id=1, source_target_pairs={{0,6},{1,7},{2,4},{3,5},{4,2},{5,3},{6,0},{7,1},{8,14},{9,15},{10,... | collective-permute-start | bytes 663560 | tf_op jit(solution)/shard_map/ppermute | solution.py:52
  154.3 23.8 %collective-permute-start.24 = (bf16[2,2,2,64,160]{4,3,2,1,0:T(8,128)(2,1)S(1)}, bf16[2,2,2,64,160]{4,3,2,1,0:T(8,128)(2,1)S(1)}, u32[]{:S(2)}, u32[]{:S(2)}) collective-permute-start(bf16[2,2,2,64,160]{4,3,2,1,0:T(8,128)(2,1)S(1)} %pad_maximum_fusion.11), channel_id=1, source_target_pairs={{0,8},{1,9},{2,10},{3,11},{4,12},{5,13},{6,14},{7,15},{8,0},{9,1},... | collective-permute-start | bytes 491528 | tf_op jit(solution)/shard_map/ppermute | solution.py:52
  154.9 23.1 %collective-permute-start.25 = (bf16[2,2,2,64,160]{4,3,2,1,0:T(8,128)(2,1)S(1)}, bf16[2,2,2,64,160]{4,3,2,1,0:T(8,128)(2,1)S(1)}, u32[]{:S(2)}, u32[]{:S(2)}) collective-permute-start(bf16[2,2,2,64,160]{4,3,2,1,0:T(8,128)(2,1)S(1)} %pad_maximum_fusion.11), channel_id=1, source_target_pairs={{0,16},{1,17},{2,18},{3,19},{4,20},{5,21},{6,22},{7,23},{8,24},{9,... | collective-permute-start | bytes 491528 | tf_op jit(solution)/shard_map/ppermute | solution.py:52
  156.5 21.6 %collective-permute-start.26 = (bf16[2,2,2,64,160]{4,3,2,1,0:T(8,128)(2,1)S(1)}, bf16[2,2,2,64,160]{4,3,2,1,0:T(8,128)(2,1)S(1)}, u32[]{:S(2)}, u32[]{:S(2)}) collective-permute-start(bf16[2,2,2,64,160]{4,3,2,1,0:T(8,128)(2,1)S(1)} %pad_maximum_fusion.11), channel_id=1, source_target_pairs={{0,24},{1,25},{2,26},{3,27},{4,28},{5,29},{6,30},{7,31},{8,16},{9,... | collective-permute-start | bytes 491528 | tf_op jit(solution)/shard_map/ppermute | solution.py:52
  183.0 4.7 %collective-permute-start.30 = (f32[17,256]{1,0:T(8,128)S(1)}, f32[17,256]{1,0:T(8,128)S(1)}, u32[]{:S(2)}, u32[]{:S(2)}) collective-permute-start(f32[17,256]{1,0:T(8,128)S(1)} %pad_maximum_fusion.14), channel_id=1, source_target_pairs={{0,16},{1,17},{2,18},{3,19},{4,20},{5,21},{6,22},{7,23},{8,24},{9,... | collective-permute-start | bytes 52232 | tf_op jit(solution)/shard_map/ppermute | solution.py:52
  184.6 4.7 %collective-permute-start.31 = (f32[17,256]{1,0:T(8,128)S(1)}, f32[17,256]{1,0:T(8,128)S(1)}, u32[]{:S(2)}, u32[]{:S(2)}) collective-permute-start(f32[17,256]{1,0:T(8,128)S(1)} %pad_maximum_fusion.14), channel_id=1, source_target_pairs={{0,24},{1,25},{2,26},{3,27},{4,28},{5,29},{6,30},{7,31},{8,16},{9,... | collective-permute-start | bytes 52232 | tf_op jit(solution)/shard_map/ppermute | solution.py:52
  185.1 4.2 %collective-permute-start.29 = (f32[17,256]{1,0:T(8,128)S(1)}, f32[17,256]{1,0:T(8,128)S(1)}, u32[]{:S(2)}, u32[]{:S(2)}) collective-permute-start(f32[17,256]{1,0:T(8,128)S(1)} %pad_maximum_fusion.14), channel_id=1, source_target_pairs={{0,8},{1,9},{2,10},{3,11},{4,12},{5,13},{6,14},{7,15},{8,0},{9,1},... | collective-permute-start | bytes 52232 | tf_op jit(solution)/shard_map/ppermute | solution.py:52
  190.6 5.5 %collective-permute-start.33 = (f32[17,256]{1,0:T(8,128)}, f32[17,256]{1,0:T(8,128)S(1)}, u32[]{:S(2)}, u32[]{:S(2)}) collective-permute-start(f32[17,256]{1,0:T(8,128)} %pad_maximum_fusion.15), channel_id=1, source_target_pairs={{0,2},{1,3},{2,0},{3,1},{4,6},{5,7},{6,4},{7,5},{8,10},{9,11},{10,... | collective-permute-start | bytes 52232 | tf_op jit(solution)/shard_map/ppermute | solution.py:52
  191.9 5.8 %collective-permute-start.34 = (f32[17,256]{1,0:T(8,128)}, f32[17,256]{1,0:T(8,128)S(1)}, u32[]{:S(2)}, u32[]{:S(2)}) collective-permute-start(f32[17,256]{1,0:T(8,128)} %pad_maximum_fusion.15), channel_id=1, source_target_pairs={{0,3},{1,2},{2,1},{3,0},{4,7},{5,6},{6,5},{7,4},{8,11},{9,10},{10,... | collective-permute-start | bytes 52232 | tf_op jit(solution)/shard_map/ppermute | solution.py:52
  192.6 5.7 %collective-permute-start.32 = (f32[17,256]{1,0:T(8,128)}, f32[17,256]{1,0:T(8,128)}, u32[]{:S(2)}, u32[]{:S(2)}) collective-permute-start(f32[17,256]{1,0:T(8,128)} %pad_maximum_fusion.15), channel_id=1, source_target_pairs={{0,1},{1,0},{2,3},{3,2},{4,5},{5,4},{6,7},{7,6},{8,9},{9,8},{10,11... | collective-permute-start | bytes 52232 | tf_op jit(solution)/shard_map/ppermute | solution.py:52
  208.9 4.5 %collective-permute-start.38 = (f32[3,256]{1,0:T(4,128)S(1)}, f32[3,256]{1,0:T(4,128)S(1)}, u32[]{:S(2)}, u32[]{:S(2)}) collective-permute-start(f32[3,256]{1,0:T(4,128)S(1)} %pad_maximum_fusion.19), channel_id=1, source_target_pairs={{0,24},{1,25},{2,26},{3,27},{4,28},{5,29},{6,30},{7,31},{8,16},{9,... | collective-permute-start | bytes 9224 | tf_op jit(solution)/shard_map/ppermute | solution.py:52
  214.0 4.6 %collective-permute-start.40 = (f32[3,256]{1,0:T(4,128)S(1)}, f32[3,256]{1,0:T(4,128)S(1)}, u32[]{:S(2)}, u32[]{:S(2)}) collective-permute-start(f32[3,256]{1,0:T(4,128)S(1)} %pad_maximum_fusion.20), channel_id=1, source_target_pairs={{0,2},{1,3},{2,0},{3,1},{4,6},{5,7},{6,4},{7,5},{8,10},{9,11},{10,... | collective-permute-start | bytes 9224 | tf_op jit(solution)/shard_map/ppermute | solution.py:52
  214.7 5.4 %collective-permute-start.41 = (f32[3,256]{1,0:T(4,128)S(1)}, f32[3,256]{1,0:T(4,128)S(1)}, u32[]{:S(2)}, u32[]{:S(2)}) collective-permute-start(f32[3,256]{1,0:T(4,128)S(1)} %pad_maximum_fusion.20), channel_id=1, source_target_pairs={{0,3},{1,2},{2,1},{3,0},{4,7},{5,6},{6,5},{7,4},{8,11},{9,10},{10,... | collective-permute-start | bytes 9224 | tf_op jit(solution)/shard_map/ppermute | solution.py:52
  216.3 3.8 collective-permute-start.39
  224.0 4.5 %collective-permute-start.45 = (f32[2,256]{1,0:T(2,128)S(1)}, f32[2,256]{1,0:T(2,128)S(1)}, u32[]{:S(2)}, u32[]{:S(2)}) collective-permute-start(f32[2,256]{1,0:T(2,128)S(1)} %fusion.69), channel_id=1, source_target_pairs={{0,24},{1,25},{2,26},{3,27},{4,28},{5,29},{6,30},{7,31},{8,16},{9,... | collective-permute-start | bytes 6152 | tf_op jit(solution)/shard_map/ppermute | solution.py:52
  228.5 5.6 %collective-permute-start.47 = (f32[2,256]{1,0:T(2,128)S(1)}, f32[2,256]{1,0:T(2,128)S(1)}, u32[]{:S(2)}, u32[]{:S(2)}) collective-permute-start(f32[2,256]{1,0:T(2,128)S(1)} %add_add_fusion.7), channel_id=1, source_target_pairs={{0,2},{1,3},{2,0},{3,1},{4,6},{5,7},{6,4},{7,5},{8,10},{9,11},{10,... | collective-permute-start | bytes 6152 | tf_op jit(solution)/shard_map/ppermute | solution.py:52
  229.7 5.4 %collective-permute-start.48 = (f32[2,256]{1,0:T(2,128)S(1)}, f32[2,256]{1,0:T(2,128)S(1)}, u32[]{:S(2)}, u32[]{:S(2)}) collective-permute-start(f32[2,256]{1,0:T(2,128)S(1)} %add_add_fusion.7), channel_id=1, source_target_pairs={{0,3},{1,2},{2,1},{3,0},{4,7},{5,6},{6,5},{7,4},{8,11},{9,10},{10,... | collective-permute-start | bytes 6152 | tf_op jit(solution)/shard_map/ppermute | solution.py:52
  232.1 8.6 %collective-permute-start.49 = (bf16[16,512]{1,0:T(8,128)(2,1)}, bf16[16,512]{1,0:T(8,128)(2,1)}, u32[]{:S(2)}, u32[]{:S(2)}) collective-permute-start(bf16[16,512]{1,0:T(8,128)(2,1)} %get-tuple-element.91), channel_id=1, source_target_pairs={{0,2},{1,3},{2,0},{3,1},{4,6},{5,7},{6,4},{7,5},{8,10},{9,11},{10,... | collective-permute-start | bytes 49160 | tf_op jit(solution)/shard_map/ppermute | solution.py:52
  241.9 3.7 collective-permute-start.52
  243.0 4.7 %collective-permute-start.53 = (f32[16,256]{1,0:T(8,128)S(1)}, f32[16,256]{1,0:T(8,128)S(1)}, u32[]{:S(2)}, u32[]{:S(2)}) collective-permute-start(f32[16,256]{1,0:T(8,128)S(1)} %add.455), channel_id=1, source_target_pairs={{0,24},{1,25},{2,26},{3,27},{4,28},{5,29},{6,30},{7,31},{8,16},{9,... | collective-permute-start | bytes 49160 | tf_op jit(solution)/shard_map/ppermute | solution.py:52
  248.2 4.9 %collective-permute-start.55 = (f32[16,256]{1,0:T(8,128)S(1)}, f32[16,256]{1,0:T(8,128)S(1)}, u32[]{:S(2)}, u32[]{:S(2)}) collective-permute-start(f32[16,256]{1,0:T(8,128)S(1)} %add_add_fusion.3), channel_id=1, source_target_pairs={{0,2},{1,3},{2,0},{3,1},{4,6},{5,7},{6,4},{7,5},{8,10},{9,11},{10,... | collective-permute-start | bytes 49160 | tf_op jit(solution)/shard_map/ppermute | solution.py:52
  248.9 5.6 %collective-permute-start.56 = (f32[16,256]{1,0:T(8,128)S(1)}, f32[16,256]{1,0:T(8,128)S(1)}, u32[]{:S(2)}, u32[]{:S(2)}) collective-permute-start(f32[16,256]{1,0:T(8,128)S(1)} %add_add_fusion.3), channel_id=1, source_target_pairs={{0,3},{1,2},{2,1},{3,0},{4,7},{5,6},{6,5},{7,4},{8,11},{9,10},{10,... | collective-permute-start | bytes 49160 | tf_op jit(solution)/shard_map/ppermute | solution.py:52
  250.7 3.9 %collective-permute-start.54 = (f32[16,256]{1,0:T(8,128)S(1)}, f32[16,256]{1,0:T(8,128)S(1)}, u32[]{:S(2)}, u32[]{:S(2)}) collective-permute-start(f32[16,256]{1,0:T(8,128)S(1)} %add_add_fusion.3), channel_id=1, source_target_pairs={{0,1},{1,0},{2,3},{3,2},{4,5},{5,4},{6,7},{7,6},{8,9},{9,8},{10,11... | collective-permute-start | bytes 49160 | tf_op jit(solution)/shard_map/ppermute | solution.py:52
  257.5 28.2 %collective-permute-start.57 = (bf16[432,1024]{1,0:T(8,128)(2,1)}, bf16[432,1024]{1,0:T(8,128)(2,1)}, u32[]{:S(2)}, u32[]{:S(2)}) collective-permute-start(bf16[432,1024]{1,0:T(8,128)(2,1)} %pad_maximum_fusion.4.refs_0_.refs_4_), channel_id=1, source_target_pairs={{0,1},{1,0},{2,3},{3,2},{4,5},{5,4},{6,7},{7,6},{8,9},{9,8},{10,11... | collective-permute-start | bytes 2654216 | tf_op jit(solution)/shard_map/ppermute | solution.py:52
  259.6 24.2 %collective-permute-start.58 = (bf16[432,512]{1,0:T(8,128)(2,1)S(1)}, bf16[432,512]{1,0:T(8,128)(2,1)}, u32[]{:S(2)}, u32[]{:S(2)}) collective-permute-start(bf16[432,512]{1,0:T(8,128)(2,1)S(1)} %pad_maximum_fusion.8), channel_id=1, source_target_pairs={{0,2},{1,3},{2,0},{3,1},{4,6},{5,7},{6,4},{7,5},{8,10},{9,11},{10,... | collective-permute-start | bytes 1327112 | tf_op jit(solution)/shard_map/ppermute | solution.py:52
  262.6 26.1 %collective-permute-start.60 = (bf16[432,1024]{1,0:T(8,128)(2,1)}, bf16[432,1024]{1,0:T(8,128)(2,1)}, u32[]{:S(2)}, u32[]{:S(2)}) collective-permute-start(bf16[432,1024]{1,0:T(8,128)(2,1)} %pad_maximum_fusion.4.refs_0_.refs_4_), channel_id=1, source_target_pairs={{0,4},{1,5},{2,6},{3,7},{4,0},{5,1},{6,2},{7,3},{8,12},{9,13},{10,... | collective-permute-start | bytes 2654216 | tf_op jit(solution)/shard_map/ppermute | solution.py:52
  287.6 22.9 %collective-permute-start.65 = (bf16[432,512]{1,0:T(8,128)(2,1)}, bf16[432,512]{1,0:T(8,128)(2,1)S(1)}, u32[]{:S(2)}, u32[]{:S(2)}) collective-permute-start(bf16[432,512]{1,0:T(8,128)(2,1)} %collective-permute-done.58.refs_8_), channel_id=1, source_target_pairs={{0,1},{1,0},{2,3},{3,2},{4,5},{5,4},{6,7},{7,6},{8,9},{9,8},{10,11... | collective-permute-start | bytes 1327112 | tf_op jit(solution)/shard_map/ppermute | solution.py:52
  288.8 22.8 %collective-permute-start.63 = (bf16[2,2,2,64,160]{4,3,2,1,0:T(8,128)(2,1)S(1)}, bf16[2,2,2,64,160]{4,3,2,1,0:T(8,128)(2,1)S(1)}, u32[]{:S(2)}, u32[]{:S(2)}) collective-permute-start(bf16[2,2,2,64,160]{4,3,2,1,0:T(8,128)(2,1)S(1)} %fusion.16), channel_id=1, source_target_pairs={{0,8},{1,9},{2,10},{3,11},{4,12},{5,13},{6,14},{7,15},{8,0},{9,1},... | collective-permute-start | bytes 491528 | tf_op jit(solution)/shard_map/ppermute | solution.py:52
  290.2 20.9 %collective-permute-start.66 = (bf16[432,512]{1,0:T(8,128)(2,1)}, bf16[432,512]{1,0:T(8,128)(2,1)S(1)}, u32[]{:S(2)}, u32[]{:S(2)}) collective-permute-start(bf16[432,512]{1,0:T(8,128)(2,1)} %get-tuple-element.102), channel_id=1, source_target_pairs={{0,3},{1,2},{2,1},{3,0},{4,7},{5,6},{6,5},{7,4},{8,11},{9,10},{10,... | collective-permute-start | bytes 1327112 | tf_op jit(solution)/shard_map/ppermute | solution.py:52
  310.4 25.6 %collective-permute-start.62 = (bf16[432,256]{1,0:T(8,128)(2,1)S(1)}, bf16[432,256]{1,0:T(8,128)(2,1)S(1)}, u32[]{:S(2)}, u32[]{:S(2)}) collective-permute-start(bf16[432,256]{1,0:T(8,128)(2,1)S(1)} %copy-done.16), channel_id=1, source_target_pairs={{0,6},{1,7},{2,4},{3,5},{4,2},{5,3},{6,0},{7,1},{8,14},{9,15},{10,... | collective-permute-start | bytes 663560 | tf_op jit(solution)/shard_map/ppermute | solution.py:52
  311.7 25.1 %collective-permute-start.64 = (bf16[1,2,2,64,160]{4,3,2,1,0:T(8,128)(2,1)S(1)}, bf16[1,2,2,64,160]{4,3,2,1,0:T(8,128)(2,1)S(1)}, u32[]{:S(2)}, u32[]{:S(2)}) collective-permute-start(bf16[1,2,2,64,160]{4,3,2,1,0:T(8,128)(2,1)S(1)} %select_bitcast_fusion.8), channel_id=1, source_target_pairs={{0,16},{1,17},{2,18},{3,19},{4,20},{5,21},{6,22},{7,23},{8,24},{9,... | collective-permute-start | bytes 245768 | tf_op jit(solution)/shard_map/ppermute | solution.py:52
  313.9 28.1 %collective-permute-start.69 = (bf16[432,512]{1,0:T(8,128)(2,1)}, bf16[432,512]{1,0:T(8,128)(2,1)S(1)}, u32[]{:S(2)}, u32[]{:S(2)}) collective-permute-start(bf16[432,512]{1,0:T(8,128)(2,1)} %get-tuple-element.105), channel_id=1, source_target_pairs={{0,2},{1,3},{2,0},{3,1},{4,6},{5,7},{6,4},{7,5},{8,10},{9,11},{10,... | collective-permute-start | bytes 1327112 | tf_op jit(solution)/shard_map/ppermute | solution.py:52
  315.8 26.3 %collective-permute-start.70 = (bf16[432,512]{1,0:T(8,128)(2,1)}, bf16[432,512]{1,0:T(8,128)(2,1)S(1)}, u32[]{:S(2)}, u32[]{:S(2)}) collective-permute-start(bf16[432,512]{1,0:T(8,128)(2,1)} %get-tuple-element.106), channel_id=1, source_target_pairs={{0,1},{1,0},{2,3},{3,2},{4,5},{5,4},{6,7},{7,6},{8,9},{9,8},{10,11... | collective-permute-start | bytes 1327112 | tf_op jit(solution)/shard_map/ppermute | solution.py:52
  334.1 12.7 %collective-permute-start.74 = (bf16[29,64,128]{2,1,0:T(8,128)(2,1)}, bf16[29,64,128]{2,1,0:T(8,128)(2,1)S(1)}, u32[]{:S(2)}, u32[]{:S(2)}) collective-permute-start(bf16[29,64,128]{2,1,0:T(8,128)(2,1)} %get-tuple-element.111), channel_id=1, source_target_pairs={{0,16},{1,17},{2,18},{3,19},{4,20},{5,21},{6,22},{7,23},{8,24},{9,... | collective-permute-start | bytes 1425416 | tf_op jit(solution)/shard_map/ppermute | solution.py:52
  336.0 12.2 %collective-permute-start.75 = (bf16[29,64,128]{2,1,0:T(8,128)(2,1)}, bf16[29,64,128]{2,1,0:T(8,128)(2,1)S(1)}, u32[]{:S(2)}, u32[]{:S(2)}) collective-permute-start(bf16[29,64,128]{2,1,0:T(8,128)(2,1)} %get-tuple-element.112), channel_id=1, source_target_pairs={{0,8},{1,9},{2,10},{3,11},{4,12},{5,13},{6,14},{7,15},{8,0},{9,1},... | collective-permute-start | bytes 1425416 | tf_op jit(solution)/shard_map/ppermute | solution.py:52
  342.1 24.4 %collective-permute-start.71 = (bf16[432,512]{1,0:T(8,128)(2,1)S(1)}, bf16[432,512]{1,0:T(8,128)(2,1)S(1)}, u32[]{:S(2)}, u32[]{:S(2)}) collective-permute-start(bf16[432,512]{1,0:T(8,128)(2,1)S(1)} %copy-done.88), channel_id=1, source_target_pairs={{0,2},{1,3},{2,0},{3,1},{4,6},{5,7},{6,4},{7,5},{8,10},{9,11},{10,... | collective-permute-start | bytes 1327112 | tf_op jit(solution)/shard_map/ppermute | solution.py:52
  342.1 24.5 %collective-permute-start.72 = (bf16[432,512]{1,0:T(8,128)(2,1)S(1)}, bf16[432,512]{1,0:T(8,128)(2,1)S(1)}, u32[]{:S(2)}, u32[]{:S(2)}) collective-permute-start(bf16[432,512]{1,0:T(8,128)(2,1)S(1)} %collective-permute-done.69), channel_id=1, source_target_pairs={{0,1},{1,0},{2,3},{3,2},{4,5},{5,4},{6,7},{7,6},{8,9},{9,8},{10,11... | collective-permute-start | bytes 1327112 | tf_op jit(solution)/shard_map/ppermute | solution.py:52
  344.2 22.2 %collective-permute-start.78 = (bf16[2,64,160]{2,1,0:T(8,128)(2,1)S(1)}, bf16[2,64,160]{2,1,0:T(8,128)(2,1)S(1)}, u32[]{:S(2)}, u32[]{:S(2)}) collective-permute-start(bf16[2,64,160]{2,1,0:T(8,128)(2,1)S(1)} %select_bitcast_fusion.11), channel_id=1, source_target_pairs={{0,2},{1,3},{2,0},{3,1},{4,6},{5,7},{6,4},{7,5},{8,10},{9,11},{10,... | collective-permute-start | bytes 122888 | tf_op jit(solution)/shard_map/ppermute | solution.py:52
  349.6 21.3 %collective-permute-start.77 = (bf16[2,29,64,128]{3,2,1,0:T(8,128)(2,1)S(1)}, bf16[2,29,64,128]{3,2,1,0:T(8,128)(2,1)S(1)}, u32[]{:S(2)}, u32[]{:S(2)}) collective-permute-start(bf16[2,29,64,128]{3,2,1,0:T(8,128)(2,1)S(1)} %pad_maximum_fusion.2), channel_id=1, source_target_pairs={{0,16},{1,17},{2,18},{3,19},{4,20},{5,21},{6,22},{7,23},{8,24},{9,... | collective-permute-start | bytes 2850824 | tf_op jit(solution)/shard_map/ppermute | solution.py:52
  350.6 21.3 %collective-permute-start.76 = (bf16[2,29,64,128]{3,2,1,0:T(8,128)(2,1)S(1)}, bf16[2,29,64,128]{3,2,1,0:T(8,128)(2,1)S(1)}, u32[]{:S(2)}, u32[]{:S(2)}) collective-permute-start(bf16[2,29,64,128]{3,2,1,0:T(8,128)(2,1)S(1)} %pad_maximum_fusion.1), channel_id=1, source_target_pairs={{0,8},{1,9},{2,10},{3,11},{4,12},{5,13},{6,14},{7,15},{8,0},{9,1},... | collective-permute-start | bytes 2850824 | tf_op jit(solution)/shard_map/ppermute | solution.py:52
  366.8 10.7 %collective-permute-start.73 = (bf16[2,432,512]{2,1,0:T(8,128)(2,1)S(1)}, bf16[2,432,512]{2,1,0:T(8,128)(2,1)S(1)}, u32[]{:S(2)}, u32[]{:S(2)}) collective-permute-start(bf16[2,432,512]{2,1,0:T(8,128)(2,1)S(1)} %pad_maximum_fusion.5), channel_id=1, source_target_pairs={{0,4},{1,5},{2,6},{3,7},{4,0},{5,1},{6,2},{7,3},{8,12},{9,13},{10,... | collective-permute-start | bytes 2654216 | tf_op jit(solution)/shard_map/ppermute | solution.py:52
  372.5 4.4 %collective-permute-start.81 = (bf16[1,64,160]{2,1,0:T(8,128)(2,1)S(1)}, bf16[1,64,160]{2,1,0:T(8,128)(2,1)S(1)}, u32[]{:S(2)}, u32[]{:S(2)}) collective-permute-start(bf16[1,64,160]{2,1,0:T(8,128)(2,1)S(1)} %select_bitcast_fusion.14), channel_id=1, source_target_pairs={{0,1},{1,0},{2,3},{3,2},{4,5},{5,4},{6,7},{7,6},{8,9},{9,8},{10,11... | collective-permute-start | bytes 61448 | tf_op jit(solution)/shard_map/ppermute | solution.py:52
  373.5 10.2 %collective-permute-start.79 = (bf16[29,64,128]{2,1,0:T(8,128)(2,1)S(1)}, bf16[29,64,128]{2,1,0:T(8,128)(2,1)S(1)}, u32[]{:S(2)}, u32[]{:S(2)}) collective-permute-start(bf16[29,64,128]{2,1,0:T(8,128)(2,1)S(1)} %broadcast_select_fusion.7), channel_id=1, source_target_pairs={{0,1},{1,0},{2,3},{3,2},{4,5},{5,4},{6,7},{7,6},{8,9},{9,8},{10,11... | collective-permute-start | bytes 1425416 | tf_op jit(solution)/shard_map/ppermute | solution.py:52
  (111 other events, 1242.9 us)
where the time goes:
time: 392 us; the launch traced here: 388 us
  waiting for transfers between devices  156 us (40%)
  starting transfers between devices  84.7 us (22%)
  Pallas kernels  76.3 us (19%)
  other arithmetic  42.6 us (11%)
  local copies, waits for them, and re-layouts  21.4 us (5%)
  between operations  4.96 us (1%)
    ppermute x82, waiting for transfers between devices, swap(): return lax.ppermute(x, AXES, pairs)  156 us
    ppermute x82, starting transfers between devices, swap(): return lax.ppermute(x, AXES, pairs)  84.7 us
    pallas_call x1, Pallas kernels, branch_sums(): pl.pallas_call(kernel, out_shape=half_shapes(shape, 4) + [jax.ShapeDtypeS...  18.4 us
    pallas_call x1, Pallas kernels, input_gradient(): pl.pallas_call(kernel, out_shape=[jax.ShapeDtypeStruct((shape.band, shape...  17.9 us
    pallas_call x1, Pallas kernels, weight_gradients(): pl.pallas_call(kernel, out_shape=out_shape, in_specs=[SMEM] + [ANY] * (4...  17.6 us
    pallas_call x2, Pallas kernels, assembled_weights(): pl.pallas_call(kernel, out_shape=jax.ShapeDtypeStruct((29, shape.out // 2...  11.4 us
    unnamed x186, local copies, waits for them, and re-layouts  8.03 us
  transfers between devices with their start and end apart: 82, of which 44 were waited for; matrix products, arithmetic and copies ran while one was open for 10% of the time, Pallas kernels for 19%

commit v1 on v0

--- a/solution.py
+++ b/solution.py
@@ -84,32 +84,22 @@
     return x
 
 
-def moments(place, sums, squares, count, extra=None):
-    width = sums.shape[1]
-    k = sums.shape[0]
-    rows = [sums, squares, jnp.full((1, width), count, jnp.float32)]
-    if extra is not None:
-        rows.append(extra)
-    x = jnp.concatenate(rows, axis=0)
-    for stage in exchange_stages(place):
-        xs = [x] + [place.swap(x, **s) for s in stage]
-        whole = tree(xs)
-        n = whole[2 * k : 2 * k + 1]
-        mean = whole[:k] / jnp.maximum(n, 1.0)
-        between = []
-        for y in xs:
-            own = y[2 * k : 2 * k + 1]
-            gap = y[:k] / jnp.maximum(own, 1.0) - mean
-            between.append(own * gap * gap)
-        x = jnp.concatenate([whole[:k], whole[k : 2 * k] + tree(between), whole[2 * k :]], axis=0)
-    n = x[2 * k : 2 * k + 1]
-    return x[:k] / n, x[k : 2 * k] / n, n, x[2 * k + 1 :]
-
-
-def local_moments(values, mask, count):
-    sums = jnp.sum(values * mask, axis=0, keepdims=True)
-    centred = (values - sums / jnp.maximum(count, 1.0)) * mask
-    return sums, jnp.sum(centred * centred, axis=0, keepdims=True)
+def merged(xs, k):
+    whole = tree(xs)
+    mean = whole[:k] / jnp.maximum(whole[2 * k : 2 * k + 1], 1.0)
+    between = []
+    for y in xs:
+        own = y[2 * k : 2 * k + 1]
+        gap = y[:k] / jnp.maximum(own, 1.0) - mean
+        between.append(own * gap * gap)
+    return jnp.concatenate([whole[:k], whole[k : 2 * k] + tree(between), whole[2 * k :]], axis=0)
+
+
+def exchanged(place, x, combine):
+    *stages, last = exchange_stages(place)
+    for stage in stages:
+        x = combine([x] + [place.swap(x, **s) for s in stage])
+    return [x] + [place.swap(x, **s) for s in last]
 
 
 def line_pieces(place, dilated, pointwise, pooling):
@@ -237,6 +227,7 @@
 SMEM = pl.BlockSpec(memory_space=pltpu.SMEM)
 VMEM = pl.BlockSpec(memory_space=pltpu.VMEM)
 PARAMS = pltpu.CompilerParams(vmem_limit_bytes=58 * 2**20)
+SMALL = pltpu.CompilerParams(vmem_limit_bytes=12 * 2**20)
 
 
 LIGHT = pl.CostEstimate(flops=0, bytes_accessed=0, transcendentals=0)
@@ -272,7 +263,7 @@
         out_shape=[jax.ShapeDtypeStruct((n, shape.band, shape.width), jnp.bfloat16)] * 2,
         in_specs=[SMEM, VMEM, VMEM],
         out_specs=[VMEM] * 2,
-        compiler_params=PARAMS,
+        compiler_params=SMALL,
         cost_estimate=LIGHT,
         name="split_features",
     )(c.reshape(1), features, mask)
@@ -293,7 +284,7 @@
         out_shape=jax.ShapeDtypeStruct((shape.band, shape.width * shape.nr), jnp.bfloat16),
         in_specs=[SMEM] + [VMEM] * shape.nr,
         out_specs=VMEM,
-        compiler_params=PARAMS,
+        compiler_params=SMALL,
         cost_estimate=LIGHT,
         name="join_features",
     )(jnp.stack([c, zl]).astype(jnp.int32), *own, *other)
@@ -316,7 +307,7 @@
         ],
         in_specs=[SMEM, VMEM, VMEM],
         out_specs=[VMEM, VMEM],
-        compiler_params=PARAMS,
+        compiler_params=SMALL,
         cost_estimate=LIGHT,
         name="packed_near",
     )(zl.reshape(1), own, neighbour)
@@ -339,7 +330,7 @@
         out_shape=jax.ShapeDtypeStruct((SLOTS, 2 * size, LANES), jnp.bfloat16),
         in_specs=[SMEM, VMEM, VMEM],
         out_specs=VMEM,
-        compiler_params=PARAMS,
+        compiler_params=SMALL,
         cost_estimate=LIGHT,
         name="packed_far",
     )(zl.reshape(1), first, rest)
@@ -506,6 +497,200 @@
         cost_estimate=LIGHT,
         name="branch_sums",
     )(info, area, *bands, *weights)
+
+
+def band_mask(shape, info):
+    pixel = lax.broadcasted_iota(jnp.int32, (shape.band, 1), 0)
+    row, column = info[4] * shape.band_rows + pixel // shape.columns, pixel % shape.columns
+    return ((row < info[6]) & (column < info[7])).astype(jnp.float32)
+
+
+def put_moments(values, mask, ref, at_sum, at_square, count):
+    total = jnp.sum(values * mask, axis=0, keepdims=True)
+    centred = (values - total / jnp.maximum(count, 1.0)) * mask
+    ref[at_sum : at_sum + 1, :] = total
+    ref[at_square : at_square + 1, :] = jnp.sum(centred * centred, axis=0, keepdims=True)
+
+
+def merged_rows(refs, k, n):
+    count = tree([ref[2 * n : 2 * n + 1, :] for ref in refs])
+    mean = tree([ref[k : k + 1, :] for ref in refs]) / jnp.maximum(count, 1.0)
+    between = []
+    for ref in refs:
+        own = ref[2 * n : 2 * n + 1, :]
+        gap = ref[k : k + 1, :] / jnp.maximum(own, 1.0) - mean
+        between.append(own * gap * gap)
+    squares = tree([ref[n + k : n + k + 1, :] for ref in refs]) + tree(between)
+    return mean, squares / count, count
+
+
+def silu(v):
+    return v * jax.nn.sigmoid(v)
+
+
+def call(shape, kernel, name, outs, out_specs, in_specs, scratch=()):
+    return pl.pallas_call(
+        kernel,
+        out_shape=[jax.ShapeDtypeStruct(*o) for o in outs],
+        in_specs=in_specs,
+        out_specs=out_specs,
+        scratch_shapes=list(scratch),
+        compiler_params=SMALL,
+        cost_estimate=LIGHT,
+        name=name,
+    )
+
+
+TABLE = 16
+
+
+def branch_moments(shape, info, images, mine, others, lifted):
+    n = len(others)
+
+    def kernel(info, mine, lifted, *refs):
+        others, (z, rows) = refs[:n], refs[n:]
+        mask = band_mask(shape, info)
+        count = jnp.sum(mask)
+        rows[...] = jnp.zeros(rows.shape, jnp.float32)
+        for k in range(4):
+            lanes = slice((3 - k) * shape.out, (4 - k) * shape.out)
+            value = mine[:, lanes]
+            for other in others:
+                value = value + other[:, lanes].astype(jnp.float32)
+            z[:, k * shape.out : (k + 1) * shape.out] = value
+            put_moments(value, mask, rows, k, 4 + k, count)
+        rows[8:9, :] = jnp.full((1, shape.out), count, jnp.float32)
+        rows[pl.ds(TABLE + 2 * info[0] + info[2], 1), :] = lifted[0:1, :]
+
+    return call(
+        shape,
+        kernel,
+        "branch_moments",
+        [((shape.band, 4 * shape.out), jnp.float32), ((TABLE + images, shape.out), jnp.float32)],
+        [VMEM] * 2,
+        [SMEM] + [VMEM] * (2 + n),
+    )(info, mine, lifted, *others)
+
+
+def projected(shape, info, images, rows, z, projection, gain, bias):
+    out = shape.out
+
+    def kernel(info, z, projection, gain, bias, *refs):
+        n = len(rows)
+        rows_in, (concat, pre, moments, stats) = refs[:n], refs[n:]
+        mask = band_mask(shape, info)
+        pool = tree([ref[TABLE : TABLE + images, :] for ref in rows_in])
+        pool = pool - jnp.sum(pool, axis=0, keepdims=True) / images
+        pool_inv = lax.rsqrt(jnp.sum(pool * pool, axis=0, keepdims=True) / images + epsilon)
+        pool = pool * pool_inv
+        stats[9:10, :] = pool_inv
+        stats[TABLE : TABLE + images, :] = pool
+        stats[TABLE + images :, :] = gain[4:5, :] * pool + bias[4:5, :]
+        for k in range(4):
+            average, spread, count = merged_rows(rows_in, k, 4)
+            inv = lax.rsqrt(spread + epsilon)
+            stats[k : k + 1, :] = average
+            stats[4 + k : 5 + k, :] = inv
+            lanes = slice(k * out, (k + 1) * out)
+            lifted = gain[k : k + 1, :] * ((z[:, lanes] - average) * inv) + bias[k : k + 1, :]
+            concat[:, lanes] = (silu(lifted) * mask).astype(jnp.bfloat16)
+        stats[8:9, :] = count
+        line = stats[pl.ds(TABLE + images + 2 * info[0] + info[2], 1), :]
+        concat[:, 4 * out :] = (silu(line) * mask).astype(jnp.bfloat16)
+        value = dot(concat[...], projection[...], NT)
+        pre[...] = value
+        local = jnp.sum(mask)
+        put_moments(value, mask, moments, 0, 1, local)
+        moments[2:, :] = jnp.full((6, out), local, jnp.float32)
+
+    return call(
+        shape,
+        kernel,
+        "projected",
+        [
+            ((shape.band, 5 * out), jnp.bfloat16),
+            ((shape.band, out), jnp.float32),
+            ((8, out), jnp.float32),
+            ((TABLE + 2 * images, out), jnp.float32),
+        ],
+        [VMEM] * 4,
+        [SMEM] + [VMEM] * (4 + len(rows)),
+    )(info, z, projection, gain, bias, *rows)
+
+
+def branch_gradients(shape, info, images, rows, upstream, normed, inv, z, stats, projection, gain, bias):
+    out = shape.out
+
+    def kernel(info, upstream, normed, inv, z, stats, projection, gain, bias, *refs):
+        n = len(rows)
+        rows_in, (delta, up, sums, totals) = refs[:n], refs[n:]
+        mask = band_mask(shape, info)
+        whole = tree([ref[...] for ref in rows_in])
+        totals[...] = whole
+        count, scale = stats[8:9, :], gain[5:6, :]
+        low = (
+            mask
+            * inv[...]
+            * (scale * upstream[...] - scale * whole[1:2] / count - normed[...] * scale * whole[0:1] / count)
+        ).astype(jnp.bfloat16)
+        delta[...] = low
+        sums[...] = jnp.zeros(sums.shape, jnp.float32)
+        for k in range(4):
+            lanes = slice(k * out, (k + 1) * out)
+            at = (z[:, lanes] - stats[k : k + 1, :]) * stats[4 + k : 5 + k, :]
+            slope = silu_slope(gain[k : k + 1, :] * at + bias[k : k + 1, :])
+            value = dot(low, projection[:, lanes], NN) * mask * slope
+            up[:, lanes] = value
+            sums[k : k + 1, :] = jnp.sum(value * at, axis=0, keepdims=True)
+            sums[4 + k : 5 + k, :] = jnp.sum(value, axis=0, keepdims=True)
+        line = jnp.sum(dot(low, projection[:, 4 * out :], NN) * mask, axis=0, keepdims=True)
+        sums[pl.ds(8 + 2 * info[0] + info[2], 1), :] = line
+
+    return call(
+        shape,
+        kernel,
+        "branch_gradients",
+        [
+            ((shape.band, out), jnp.bfloat16),
+            ((shape.band, 4 * out), jnp.float32),
+            ((8 + images, out), jnp.float32),
+            ((8, out), jnp.float32),
+        ],
+        [VMEM] * 4,
+        [SMEM] + [VMEM] * (8 + len(rows)),
+    )(info, upstream, normed, inv, z, stats, projection, gain, bias, *rows)
+
+
+def branch_deltas(shape, info, rows, up, z, stats, gain):
+    out, half = shape.out, shape.out // 2
+
+    def kernel(info, up, z, stats, gain, *refs):
+        n = len(rows)
+        rows_in, (delta, crossing, totals) = refs[:n], refs[n:]
+        mask = band_mask(shape, info)
+        totals[...] = tree([ref[...] for ref in rows_in])
+        count = stats[8:9, :]
+        for k in range(4):
+            lanes = slice(k * out, (k + 1) * out)
+            inv, scale = stats[4 + k : 5 + k, :], gain[k : k + 1, :]
+            at = (z[:, lanes] - stats[k : k + 1, :]) * inv
+            by_gain, by_bias = totals[k : k + 1, :], totals[4 + k : 5 + k, :]
+            value = mask * inv * (scale * up[:, lanes] - scale * by_bias / count - at * scale * by_gain / count)
+            delta[:, lanes] = value.astype(jnp.bfloat16)
+            crossing[:, k * half : (k + 1) * half] = delta[:, lanes_at(k * out + (1 - info[2]) * half, half)]
+
+    return call(
+        shape,
+        kernel,
+        "branch_deltas",
+        [
+            ((shape.band, 4 * out), jnp.bfloat16),
+            ((shape.band, 4 * half), jnp.bfloat16),
+            (rows[0].shape, jnp.float32),
+        ],
+        [VMEM] * 3,
+        [SMEM] + [VMEM] * (4 + len(rows)),
+    )(info, up, z, stats, gain, *rows)
 
 
 def moved_columns(shape, delta, lane, lanes, branch, moved):
@@ -737,7 +922,7 @@
         far_x, far_y = after(plane_direct(place, far), crossing_band)
         far_d = plane_diagonal(place, far_x, far_y)
         bands = [sent(0, k, first=far_x) for k in range(nzl)] + [crossing_band]
-        bands += [sent(0, k, first=far_x) for k in range(nzl + 1, nr)]
+        bands += [sent(0, k, first=crossing_band) for k in range(nzl + 1, nr)]
         near = assembled_weights(shape, info, near, near_x, near_y, near_d)
         weights = [near, assembled_weights(shape, info, far, far_x, far_y, after(far_d, near))]
     else:
@@ -745,12 +930,11 @@
         weights = gathered_tiles(place, dilated_weight, pointwise_weight, pooling_weight)
         weights = by_xor([weights[:, : out // 2], weights[:, out // 2 :]], place.zh)
 
-    def reduce(keep, got):
+    def given_on(keep, got):
         bands_of = lambda v: v.reshape(nzl, band, v.shape[1])
         at = lambda k: [lax.dynamic_index_in_dim(bands_of(v), place.zl ^ k, 0, keepdims=False) for v in (keep, got)]
         summed = lambda k: at(k)[0] + at(k)[1].astype(jnp.float32)
-        swapped = [place.swap(summed(k).astype(jnp.bfloat16), zl=k) for k in range(1, nzl)]
-        return sum((v.astype(jnp.float32) for v in swapped), summed(0))
+        return summed(0), [place.swap(summed(k).astype(jnp.bfloat16), zl=k) for k in range(1, nzl)]
 
     ready = (bands, weights)
     keep, given, pooled, lifted = branch_sums(shape, info, areas, bands, weights)
@@ -764,73 +948,35 @@
     projection = joined(place, projection, steps[-nd_bits - 1])
     upstream_low = to_logical(place, after(cotangent.reshape(band, out), got))
     plane = [projection] + [place.swap(projection, m=k) for k in range(1, images // 2)]
-    sums = after(reduce(keep, got), plane, upstream_low)
+    mine, others = given_on(keep, got)
+    mine, others = after((mine, others), plane, upstream_low)
+    z, rows = branch_moments(shape, info, images, mine, others, lifted)
     projection = jnp.stack(by_xor(plane, place.m))
     projection = projection.reshape((place.nd, nr) + projection_weight.shape[::-1])
     projection = jnp.transpose(projection, (1, 2, 0, 3)).reshape(out, -1)
-    z = [sums[:, k * out : (k + 1) * out] for k in (3, 2, 1, 0)]
-
-    local_count = jnp.sum(mask)
-    stats = [local_moments(v, mask, local_count) for v in z]
-    table = (lax.broadcasted_iota(jnp.int32, (images, 1), 0) == place.image).astype(jnp.float32) * lifted[0:1]
-    average, spread, count, pool_pre = moments(
-        place,
-        jnp.concatenate([s for s, _ in stats], axis=0),
-        jnp.concatenate([q for _, q in stats], axis=0),
-        local_count,
-        table,
-    )
-    inv_std = lax.rsqrt(spread + epsilon)
-    normed = [(z[k] - average[k : k + 1]) * inv_std[k : k + 1] for k in range(4)]
-    pre_act = [norm_gain[k : k + 1] * normed[k] + norm_bias[k : k + 1] for k in range(4)]
-
-    pool_average = jnp.mean(pool_pre, axis=0, keepdims=True)
-    pool_centred = pool_pre - pool_average
-    pool_inv = lax.rsqrt(jnp.mean(pool_centred * pool_centred, axis=0, keepdims=True) + epsilon)
-    pool_normed = pool_centred * pool_inv
-    pool_lift = norm_gain[4:5] * pool_normed + norm_bias[4:5]
-    here = lambda rows: lax.dynamic_slice_in_dim(rows, place.image, 1, axis=0)
-    pool_act = here(jax.nn.silu(pool_lift))
-
-    concat = jnp.concatenate([jax.nn.silu(u) * mask for u in pre_act] + [pool_act * mask], axis=1).astype(jnp.bfloat16)
+    rows = exchanged(place, rows, lambda xs: merged(xs, 4))
+    concat, proj_pre, rows, stats = projected(shape, info, images, rows, z, projection, norm_gain, norm_bias)
     pooled_far = place.swap(pooled, zh=1)
-    proj_pre = dot(concat, projection, NT)
-    proj_sums, proj_squares = local_moments(proj_pre, mask, local_count)
-    proj_average, proj_spread, _, _ = moments(place, proj_sums, proj_squares, local_count)
+    rows = merged(exchanged(place, rows, lambda xs: merged(xs, 1)), 1)
+    proj_average, proj_spread = rows[0:1] / rows[2:3], rows[1:2] / rows[2:3]
     proj_inv = lax.rsqrt(proj_spread + epsilon)
     proj_normed = (proj_pre - proj_average) * proj_inv
     proj_lift = norm_gain[5:6] * proj_normed + norm_bias[5:6]
     output_here = (jax.nn.silu(proj_lift) * mask).astype(jnp.bfloat16)
 
     upstream = upstream_low.astype(jnp.float32) * mask * silu_slope(proj_lift)
-    sums = jnp.concatenate(
-        [jnp.sum(upstream * proj_normed, axis=0, keepdims=True), jnp.sum(upstream, axis=0, keepdims=True)], axis=0
+    sums = [jnp.sum(upstream * proj_normed, axis=0, keepdims=True), jnp.sum(upstream, axis=0, keepdims=True)]
+    rows = exchanged(place, jnp.concatenate(sums + [jnp.zeros((6, out), jnp.float32)], axis=0), tree)
+    proj_delta, branch_up, rows, proj_totals = branch_gradients(
+        shape, info, images, rows, upstream, proj_normed, proj_inv, z, stats, projection, norm_gain, norm_bias
     )
-    proj_totals = total(place, sums)
+    projection_partial = lambda first: dot(after(proj_delta, first), concat, TN)
+    rows = exchanged(place, rows, tree)
+    delta, crossing, totals = branch_deltas(shape, info, after(rows, pooled_far), branch_up, z, stats, norm_gain)
     proj_gain_grad, proj_bias_grad = proj_totals[0:1], proj_totals[1:2]
-    gain = norm_gain[5:6]
-    proj_delta = (
-        mask
-        * proj_inv
-        * (gain * upstream - gain * proj_bias_grad / count - proj_normed * gain * proj_gain_grad / count)
-    ).astype(jnp.bfloat16)
-    concat_grad = dot(proj_delta, projection, NN)
-    projection_partial = lambda first: dot(after(proj_delta, first), concat, TN)
-    branch_up = [
-        concat_grad[:, k * out : (k + 1) * out] * mask * silu_slope(pre_act[k]) for k in range(4)
-    ]
-    pool_part = jnp.sum(concat_grad[:, 4 * out :] * mask, axis=0, keepdims=True)
-    table = (lax.broadcasted_iota(jnp.int32, (images, 1), 0) == place.image).astype(jnp.float32) * pool_part
-    totals = total(
-        place,
-        after(jnp.concatenate(
-            [jnp.sum(branch_up[k] * normed[k], axis=0, keepdims=True) for k in range(4)]
-            + [jnp.sum(branch_up[k], axis=0, keepdims=True) for k in range(4)]
-            + [table],
-            axis=0,
-        ), pooled_far),
-    )
     branch_gain_grad, branch_bias_grad = totals[:4], totals[4:8]
+    pool_inv, pool_normed, pool_lift = stats[9:10], stats[TABLE : TABLE + images], stats[TABLE + images :]
+    here = lambda rows: lax.dynamic_slice_in_dim(rows, place.image, 1, axis=0)
     pool_up = totals[8:] * silu_slope(pool_lift)
     pool_gain_grad = jnp.sum(pool_up * pool_normed, axis=0, keepdims=True)
     pool_bias_grad = jnp.sum(pool_up, axis=0, keepdims=True)
@@ -842,21 +988,6 @@
     low_rows = lambda rows: jnp.pad(rows, ((0, 16 - rows.shape[0]), (0, 0))).astype(jnp.bfloat16)
     pool_pair = lax.dynamic_slice_in_dim(pool_deltas, 2 * place.m, 2, axis=0)
     halves = lambda v, n: by_xor([v[:, n * out : n * out + out // 2], v[:, n * out + out // 2 : (n + 1) * out]], place.zh)
-    deltas = []
-    for k in range(4):
-        gain = norm_gain[k : k + 1]
-        deltas.append(
-            mask
-            * inv_std[k : k + 1]
-            * (
-                gain * branch_up[k]
-                - gain * branch_bias_grad[k : k + 1] / count
-                - normed[k] * gain * branch_gain_grad[k : k + 1] / count
-            )
-        )
-    delta = jnp.concatenate(deltas, axis=1).astype(jnp.bfloat16)
-    crossing = jnp.concatenate([halves(delta, k)[1] for k in range(4)], axis=1)
-
     def over_group(v, first):
         near = [v] + [after(place.swap(v, zl=k), first) for k in range(1, nzl)]
         return near + [place.swap(n, c=1) for n in near]
@@ -907,7 +1038,7 @@
         dilated_gradient, pointwise_gradient, pooling_gradient = line_back(place, quarters, feature_gradient)
     else:
         dilated_gradient, pointwise_gradient, pooling_gradient = scattered_tiles(place, quarters[0])
-    part = after(part, quarters)
+    part = after(part, feature_gradient)
     for step in [step for step in steps if "zl" in step[0]]:
         part = part.reshape((-1, 2) + part.shape[-2:])
         part = halved(place, [part[:, k] for k in range(2)], step)

time: 392 us -> 387 us (0.987)
  other arithmetic: 42.6 us -> 28.2 us
  starting transfers between devices: 84.7 us -> 91.4 us
    pallas_call x0 -> x4, Pallas kernels: none -> 6.85 us  [the longest x1 1.99 us: branch_deltas(): call(shape, kernel, 'branch_deltas', [((shape.band, 4 * out), jnp.bfloat1...]
    ppermute x82, starting transfers between devices: 84.7 us -> 91.4 us  [swap(): return lax.ppermute(x, AXES, pairs)]
    slice x15 -> x11, other arithmetic: 4.7 us -> 0.12 us  [the longest x4 0.09 us: merged(): whole[:k]]
    unnamed x186 -> x100, local copies, waits for them, and re-layouts: 8.03 us -> 8.98 us
  transfers between devices with their start and end apart: 82 -> 82, of which waited for: 44 -> 43; matrix products, arithmetic and copies ran while one was open for 10% -> 9% of each run, Pallas kernels for 19% -> 18%
where the time goes in v1:
time: 387 us; the launch traced here: 383 us
  waiting for transfers between devices  158 us (41%)
  starting transfers between devices  91.4 us (24%)
  Pallas kernels  76.5 us (20%)
  other arithmetic  28.2 us (7%)
  local copies, waits for them, and re-layouts  24.2 us (6%)
    ppermute x82, waiting for transfers between devices, swap(): return lax.ppermute(x, AXES, pairs)  158 us
    ppermute x82, starting transfers between devices, swap(): return lax.ppermute(x, AXES, pairs)  91.4 us
    pallas_call x1, Pallas kernels, branch_sums(): pl.pallas_call(kernel, out_shape=half_shapes(shape, 4) + [jax.ShapeDtypeS...  18.4 us
    pallas_call x1, Pallas kernels, input_gradient(): pl.pallas_call(kernel, out_shape=[jax.ShapeDtypeStruct((shape.band, shape...  17.9 us
    pallas_call x1, Pallas kernels, weight_gradients(): pl.pallas_call(kernel, out_shape=out_shape, in_specs=[SMEM] + [ANY] * (4...  17.6 us
    pallas_call x2, Pallas kernels, assembled_weights(): pl.pallas_call(kernel, out_shape=jax.ShapeDtypeStruct((29, shape.out // 2...  10.9 us
    unnamed x100, local copies, waits for them, and re-layouts  8.98 us
  transfers between devices with their start and end apart: 82, of which 43 were waited for; matrix products, arithmetic and copies ran while one was open for 9% of the time, Pallas kernels for 18%

profile of v1, /device:TPU:0, one launch (start us, length us, event | category | flops | bytes accessed | tf_op | source)
XLA Modules:
  0.0 382.9 jit_solution(1436556728708004352)
XLA Ops:
  5.5 2.6 collective-permute-start.4
  10.7 2.7 collective-permute-start.3
  14.4 9.5 %collective-permute-done.3.first = bf16[14,64,128]{2,1,0:T(8,128)(2,1)S(1)} collective-permute-done((bf16[14,64,128]{2,1,0:T(8,128)(2,1)S(1)}, bf16[14,64,128]{2,1,0:T(8,128)(2,1)S(1)}, u32[]{:S(2)}, u32[]{:S(2)}) %collective-permute-start.3) | collective-permute-done | bytes 229408 | tf_op jit(solution)/shard_map/ppermute | solution.py:52
  26.8 1.7 collective-permute-start.8
  28.5 1.5 collective-permute-start.6
  30.0 2.4 collective-permute-start.5
  33.7 16.1 %collective-permute-done.8.refs_2_ = bf16[29,128,128]{2,1,0:T(8,128)(2,1)} collective-permute-done((bf16[29,128,128]{2,1,0:T(8,128)(2,1)S(1)}, bf16[29,128,128]{2,1,0:T(8,128)(2,1)}, u32[]{:S(2)}, u32[]{:S(2)}) %collective-permute-start.8) | collective-permute-done | bytes 950304 | tf_op jit(solution)/shard_map/ppermute | solution.py:52
  50.8 1.5 collective-permute-start.9
  52.4 1.6 collective-permute-start.7
  55.7 8.0 %collective-permute-done.5.rest = bf16[44,64,128]{2,1,0:T(8,128)(2,1)S(1)} collective-permute-done((bf16[44,64,128]{2,1,0:T(8,128)(2,1)}, bf16[44,64,128]{2,1,0:T(8,128)(2,1)S(1)}, u32[]{:S(2)}, u32[]{:S(2)}) %collective-permute-start.5) | collective-permute-done | bytes 720928 | tf_op jit(solution)/shard_map/ppermute | solution.py:52
  64.9 1.5 collective-permute-start.11
  66.9 2.4 collective-permute-start.12
  69.3 17.1 %collective-permute-done.12.refs_2_ = bf16[432,512]{1,0:T(8,128)(2,1)S(1)} collective-permute-done((bf16[432,512]{1,0:T(8,128)(2,1)S(1)}, bf16[432,512]{1,0:T(8,128)(2,1)S(1)}, u32[]{:S(2)}, u32[]{:S(2)}) %collective-permute-start.12) | collective-permute-done | bytes 442400 | tf_op jit(solution)/shard_map/ppermute | solution.py:52
  91.3 3.5 collective-permute-start.14
  95.5 2.0 stack.122.info
  97.5 5.5 %assembled_weights.2.refs_4_.refs_5_ = bf16[29,128,512]{2,1,0:T(8,128)(2,1)} custom-call(s32[8]{0:T(128)} %stack.122.info, bf16[29,128,128]{2,1,0:T(8,128)(2,1)} %copy-done.6, bf16[29,128,128]{2,1,0:T(8,128)(2,1)} %copy-done.17, bf16[29,128,128]{2,1,0:T(8,128)(2,1)} %collective-permute-done.8.refs_2_, bf16[15,128,128]{2,1,0:T(8,128)(2,1)} %copy-done.22, ...), custom_call_target="tpu_custom_call" | custom-call | tf_op jit(solution)/shard_map/assembled_weights/pallas_call | solution.py:377
  103.0 5.4 %assembled_weights.3.refs_5_.refs_6_ = bf16[29,128,512]{2,1,0:T(8,128)(2,1)} custom-call(s32[8]{0:T(128)} %stack.122.info, bf16[29,128,128]{2,1,0:T(8,128)(2,1)} %copy-done.2, bf16[29,128,128]{2,1,0:T(8,128)(2,1)} %copy-done.18, bf16[29,128,128]{2,1,0:T(8,128)(2,1)} %copy-done.19, bf16[15,128,128]{2,1,0:T(8,128)(2,1)} %collective-permute-done.15.refs_3_, ...), custom_call_target="tpu_custom_call" | custom-call | tf_op jit(solution)/shard_map/assembled_weights/pallas_call | solution.py:377
  108.5 5.5 %collective-permute-done.13.refs_1_ = bf16[432,512]{1,0:T(8,128)(2,1)} collective-permute-done((bf16[432,512]{1,0:T(8,128)(2,1)}, bf16[432,512]{1,0:T(8,128)(2,1)}, u32[]{:S(2)}, u32[]{:S(2)}) %collective-permute-start.13) | collective-permute-done | bytes 442400 | tf_op jit(solution)/shard_map/ppermute | solution.py:52
  114.0 1.7 collective-permute-start.17
  117.9 18.4 %branch_sums.1 = (f32[864,1024]{1,0:T(8,128)}, bf16[864,1024]{1,0:T(8,128)(2,1)}, bf16[16,512]{1,0:T(8,128)(2,1)}, f32[16,256]{1,0:T(8,128)}) custom-call(s32[8]{0:T(128)} %stack.122.info, f32[1]{0:T(128)} %bitcast.11.area, bf16[432,512]{1,0:T(8,128)(2,1)} %bitcast.248, bf16[432,512]{1,0:T(8,128)(2,1)} %collective-permute-done.13.refs_1_, ...), custom_call_target="tpu_custom_call" | custom-call | tf_op jit(solution)/shard_map/branch_sums/pallas_call | solution.py:480
  136.6 2.4 collective-permute-start.21
  139.0 4.4 %collective-permute-done.21 = bf16[2,64,160]{2,1,0:T(8,128)(2,1)S(1)} collective-permute-done((bf16[2,64,160]{2,1,0:T(8,128)(2,1)S(1)}, bf16[2,64,160]{2,1,0:T(8,128)(2,1)S(1)}, u32[]{:S(2)}, u32[]{:S(2)}) %collective-permute-start.21) | collective-permute-done | bytes 40992 | tf_op jit(solution)/shard_map/ppermute | solution.py:52
  144.1 3.5 fusion.2
  149.9 3.5 collective-permute-start.27
  154.4 1.6 collective-permute-start.26
  156.4 1.5 collective-permute-start.24
  157.9 14.4 %collective-permute-done.27 = bf16[432,256]{1,0:T(8,128)(2,1)S(1)} collective-permute-done((bf16[432,256]{1,0:T(8,128)(2,1)}, bf16[432,256]{1,0:T(8,128)(2,1)S(1)}, u32[]{:S(2)}, u32[]{:S(2)}) %collective-permute-start.27) | collective-permute-done | bytes 221216 | tf_op jit(solution)/shard_map/ppermute | solution.py:52
  172.3 1.6 broadcast_select_fusion.24
  177.4 1.5 branch_moments.1
  180.2 1.6 collective-permute-start.30
  182.3 1.5 collective-permute-start.29
  184.1 2.4 collective-permute-done.31
  186.6 3.6 collective-permute-start.34
  191.9 2.0 copy.48
  193.9 2.2 reshape.330.projection
  196.2 1.6 projected.1
  207.1 1.6 collective-permute-start.40
  208.7 2.8 collective-permute-start.41
  211.7 2.4 collective-permute-done.41
  218.0 1.5 collective-permute-start.44
  222.2 1.9 collective-permute-done.45
  224.2 1.8 collective-permute-start.48
  226.0 2.6 collective-permute-start.46
  230.6 1.8 branch_gradients.1
  233.6 2.0 collective-permute-start.52
  239.9 2.1 collective-permute-start.55
  246.9 2.0 branch_deltas.1
  255.5 23.7 %collective-permute-done.58.refs_8_ = bf16[432,512]{1,0:T(8,128)(2,1)} collective-permute-done((bf16[432,512]{1,0:T(8,128)(2,1)S(1)}, bf16[432,512]{1,0:T(8,128)(2,1)}, u32[]{:S(2)}, u32[]{:S(2)}) %collective-permute-start.58) | collective-permute-done | bytes 442400 | tf_op jit(solution)/shard_map/ppermute | solution.py:52
  279.2 1.5 collective-permute-done.57.refs_1_.refs_5_
  282.6 1.7 collective-permute-start.65
  285.3 1.8 collective-permute-start.66
  287.1 17.9 %input_gradient.1 = (bf16[432,512]{1,0:T(8,128)(2,1)}, bf16[432,512]{1,0:T(8,128)(2,1)}, bf16[432,512]{1,0:T(8,128)(2,1)}, bf16[432,512]{1,0:T(8,128)(2,1)}) custom-call(s32[8]{0:T(128)} %stack.122.info, f32[1]{0:T(128)} %bitcast.11.area, bf16[432,1024]{1,0:T(8,128)(2,1)} %copy-done.15, bf16[432,1024]{1,0:T(8,128)(2,1)} %collective-permute-done.57.refs_1_.refs_5_, ...), custom_call_target="tpu_custom_call" | custom-call | flops 9965666304 | bytes 16777216 | tf_op jit(solution)/shard_map/input_gradient/pallas_call | solution.py:735
  307.0 1.6 collective-permute-start.64
  309.0 1.5 collective-permute-start.69
  311.7 17.6 %weight_gradients.1 = (bf16[29,64,128]{2,1,0:T(8,128)(2,1)}, bf16[29,64,128]{2,1,0:T(8,128)(2,1)}, bf16[29,64,128]{2,1,0:T(8,128)(2,1)}, bf16[29,64,128]{2,1,0:T...) custom-call(s32[8]{0:T(128)} %stack.122.info, ...), custom_call_target="tpu_custom_call" | custom-call | flops 9965666304 | bytes 16777216 | tf_op jit(solution)/shard_map/weight_gradients/pallas_call | solution.py:847
  329.2 1.6 collective-permute-start.74
  332.1 4.7 %collective-permute-done.69 = bf16[432,512]{1,0:T(8,128)(2,1)} collective-permute-done((bf16[432,512]{1,0:T(8,128)(2,1)}, bf16[432,512]{1,0:T(8,128)(2,1)}, u32[]{:S(2)}, u32[]{:S(2)}) %collective-permute-start.69) | collective-permute-done | bytes 442400 | tf_op jit(solution)/shard_map/ppermute | solution.py:52
  336.9 2.9 collective-permute-start.71
  339.8 1.9 collective-permute-done.74
  346.2 5.2 %collective-permute-done.78 = bf16[2,64,160]{2,1,0:T(8,128)(2,1)S(1)} collective-permute-done((bf16[2,64,160]{2,1,0:T(8,128)(2,1)S(1)}, bf16[2,64,160]{2,1,0:T(8,128)(2,1)S(1)}, u32[]{:S(2)}, u32[]{:S(2)}) %collective-permute-start.78) | collective-permute-done | bytes 40992 | tf_op jit(solution)/shard_map/ppermute | solution.py:52
  351.5 10.2 %collective-permute-done.71 = bf16[432,512]{1,0:T(8,128)(2,1)S(1)} collective-permute-done((bf16[432,512]{1,0:T(8,128)(2,1)}, bf16[432,512]{1,0:T(8,128)(2,1)S(1)}, u32[]{:S(2)}, u32[]{:S(2)}) %collective-permute-start.71) | collective-permute-done | bytes 442400 | tf_op jit(solution)/shard_map/ppermute | solution.py:52
  362.2 3.5 collective-permute-done.77
  368.1 2.3 join_features.1
  372.4 5.8 %collective-permute-done.81 = bf16[1,64,160]{2,1,0:T(8,128)(2,1)S(1)} collective-permute-done((bf16[1,64,160]{2,1,0:T(8,128)(2,1)S(1)}, bf16[1,64,160]{2,1,0:T(8,128)(2,1)S(1)}, u32[]{:S(2)}, u32[]{:S(2)}) %collective-permute-start.81) | collective-permute-done | bytes 20512 | tf_op jit(solution)/shard_map/ppermute | solution.py:52
  (348 shorter events, 91.6 us)
Async XLA Ops:
  5.5 19.3 %collective-permute-start.4 = (bf16[29,64,128]{2,1,0:T(8,128)(2,1)}, bf16[29,64,128]{2,1,0:T(8,128)(2,1)}, u32[]{:S(2)}, u32[]{:S(2)}) collective-permute-start(bf16[29,64,128]{2,1,0:T(8,128)(2,1)} %get-tuple-element.183), channel_id=1, source_target_pairs={{0,1},{1,0},{2,3},{3,2},{4,5},{5,4},{6,7},{7,6},{8,9},{9,8},{10,11... | collective-permute-start | bytes 1425416 | tf_op jit(solution)/shard_map/ppermute | solution.py:52
  10.4 21.9 %collective-permute-start.1 = (bf16[2,432,512]{2,1,0:T(8,128)(2,1)}, bf16[2,432,512]{2,1,0:T(8,128)(2,1)}, u32[]{:S(2)}, u32[]{:S(2)}) collective-permute-start(bf16[2,432,512]{2,1,0:T(8,128)(2,1)} %get-tuple-element.84), channel_id=1, source_target_pairs={{0,4},{1,5},{2,6},{3,7},{4,0},{5,1},{6,2},{7,3},{8,12},{9,13},{10,... | collective-permute-start | bytes 2654216 | tf_op jit(solution)/shard_map/ppermute | solution.py:52
  10.7 13.3 %collective-permute-start.3 = (bf16[14,64,128]{2,1,0:T(8,128)(2,1)S(1)}, bf16[14,64,128]{2,1,0:T(8,128)(2,1)S(1)}, u32[]{:S(2)}, u32[]{:S(2)}) collective-permute-start(bf16[14,64,128]{2,1,0:T(8,128)(2,1)S(1)} %slice.502), channel_id=1, source_target_pairs={{0,2},{1,3},{2,0},{3,1},{4,6},{5,7},{6,4},{7,5},{8,10},{9,11},{10,... | collective-permute-start | bytes 688136 | tf_op jit(solution)/shard_map/ppermute | solution.py:52
  26.8 23.0 %collective-permute-start.8 = (bf16[29,128,128]{2,1,0:T(8,128)(2,1)S(1)}, bf16[29,128,128]{2,1,0:T(8,128)(2,1)}, u32[]{:S(2)}, u32[]{:S(2)}) collective-permute-start(bf16[29,128,128]{2,1,0:T(8,128)(2,1)S(1)} %get-tuple-element.87.refs_0_), channel_id=1, source_target_pairs={{0,16},{1,17},{2,18},{3,19},{4,20},{5,21},{6,22},{7,23},{8,24},{9,... | collective-permute-start | bytes 2850824 | tf_op jit(solution)/shard_map/ppermute | solution.py:52
  28.5 23.8 %collective-permute-start.6 = (bf16[29,128,128]{2,1,0:T(8,128)(2,1)S(1)}, bf16[29,128,128]{2,1,0:T(8,128)(2,1)S(1)}, u32[]{:S(2)}, u32[]{:S(2)}) collective-permute-start(bf16[29,128,128]{2,1,0:T(8,128)(2,1)S(1)} %get-tuple-element.87.refs_0_), channel_id=1, source_target_pairs={{0,8},{1,9},{2,10},{3,11},{4,12},{5,13},{6,14},{7,15},{8,0},{9,1},... | collective-permute-start | bytes 2850824 | tf_op jit(solution)/shard_map/ppermute | solution.py:52
  30.0 33.7 %collective-permute-start.5 = (bf16[44,64,128]{2,1,0:T(8,128)(2,1)}, bf16[44,64,128]{2,1,0:T(8,128)(2,1)S(1)}, u32[]{:S(2)}, u32[]{:S(2)}) collective-permute-start(bf16[44,64,128]{2,1,0:T(8,128)(2,1)} %copy-done.16), channel_id=1, source_target_pairs={{0,2},{1,3},{2,0},{3,1},{4,6},{5,7},{6,4},{7,5},{8,10},{9,11},{10,... | collective-permute-start | bytes 2162696 | tf_op jit(solution)/shard_map/ppermute | solution.py:52
  50.8 12.9 %collective-permute-start.9 = (bf16[14,128,128]{2,1,0:T(8,128)(2,1)S(1)}, bf16[14,128,128]{2,1,0:T(8,128)(2,1)S(1)}, u32[]{:S(2)}, u32[]{:S(2)}) collective-permute-start(bf16[14,128,128]{2,1,0:T(8,128)(2,1)S(1)} %slice.504), channel_id=1, source_target_pairs={{0,8},{1,9},{2,10},{3,11},{4,12},{5,13},{6,14},{7,15},{8,0},{9,1},... | collective-permute-start | bytes 1376264 | tf_op jit(solution)/shard_map/ppermute | solution.py:52
  52.4 11.7 %collective-permute-start.7 = (bf16[15,128,128]{2,1,0:T(8,128)(2,1)S(1)}, bf16[15,128,128]{2,1,0:T(8,128)(2,1)S(1)}, u32[]{:S(2)}, u32[]{:S(2)}) collective-permute-start(bf16[15,128,128]{2,1,0:T(8,128)(2,1)S(1)} %slice.503), channel_id=1, source_target_pairs={{0,16},{1,17},{2,18},{3,19},{4,20},{5,21},{6,22},{7,23},{8,24},{9,... | collective-permute-start | bytes 1474568 | tf_op jit(solution)/shard_map/ppermute | solution.py:52
  64.9 21.5 %collective-permute-start.11 = (bf16[29,128,128]{2,1,0:T(8,128)(2,1)S(1)}, bf16[29,128,128]{2,1,0:T(8,128)(2,1)S(1)}, u32[]{:S(2)}, u32[]{:S(2)}) collective-permute-start(bf16[29,128,128]{2,1,0:T(8,128)(2,1)S(1)} %packed_far.1.refs_0_), channel_id=1, source_target_pairs={{0,16},{1,17},{2,18},{3,19},{4,20},{5,21},{6,22},{7,23},{8,24},{9,... | collective-permute-start | bytes 2850824 | tf_op jit(solution)/shard_map/ppermute | solution.py:52
  66.4 20.8 %collective-permute-start.10 = (bf16[29,128,128]{2,1,0:T(8,128)(2,1)S(1)}, bf16[29,128,128]{2,1,0:T(8,128)(2,1)S(1)}, u32[]{:S(2)}, u32[]{:S(2)}) collective-permute-start(bf16[29,128,128]{2,1,0:T(8,128)(2,1)S(1)} %packed_far.1.refs_0_), channel_id=1, source_target_pairs={{0,8},{1,9},{2,10},{3,11},{4,12},{5,13},{6,14},{7,15},{8,0},{9,1},... | collective-permute-start | bytes 2850824 | tf_op jit(solution)/shard_map/ppermute | solution.py:52
  66.9 19.5 %collective-permute-start.12 = (bf16[432,512]{1,0:T(8,128)(2,1)S(1)}, bf16[432,512]{1,0:T(8,128)(2,1)S(1)}, u32[]{:S(2)}, u32[]{:S(2)}) collective-permute-start(bf16[432,512]{1,0:T(8,128)(2,1)S(1)} %bitcast.254), channel_id=1, source_target_pairs={{0,2},{1,3},{2,0},{3,1},{4,6},{5,7},{6,4},{7,5},{8,10},{9,11},{10,... | collective-permute-start | bytes 1327112 | tf_op jit(solution)/shard_map/ppermute | solution.py:52
  88.2 14.9 %collective-permute-start.15 = (bf16[15,128,128]{2,1,0:T(8,128)(2,1)}, bf16[15,128,128]{2,1,0:T(8,128)(2,1)}, u32[]{:S(2)}, u32[]{:S(2)}) collective-permute-start(bf16[15,128,128]{2,1,0:T(8,128)(2,1)} %slice.404), channel_id=1, source_target_pairs={{0,16},{1,17},{2,18},{3,19},{4,20},{5,21},{6,22},{7,23},{8,24},{9,... | collective-permute-start | bytes 1474568 | tf_op jit(solution)/shard_map/ppermute | solution.py:52
  90.1 13.0 %collective-permute-start.16 = (bf16[14,128,128]{2,1,0:T(8,128)(2,1)}, bf16[14,128,128]{2,1,0:T(8,128)(2,1)}, u32[]{:S(2)}, u32[]{:S(2)}) collective-permute-start(bf16[14,128,128]{2,1,0:T(8,128)(2,1)} %slice.405), channel_id=1, source_target_pairs={{0,8},{1,9},{2,10},{3,11},{4,12},{5,13},{6,14},{7,15},{8,0},{9,1},... | collective-permute-start | bytes 1376264 | tf_op jit(solution)/shard_map/ppermute | solution.py:52
  91.3 17.2 %collective-permute-start.14 = (bf16[432,512]{1,0:T(8,128)(2,1)}, bf16[432,512]{1,0:T(8,128)(2,1)}, u32[]{:S(2)}, u32[]{:S(2)}) collective-permute-start(bf16[432,512]{1,0:T(8,128)(2,1)} %get-tuple-element.98), channel_id=1, source_target_pairs={{0,3},{1,2},{2,1},{3,0},{4,7},{5,6},{6,5},{7,4},{8,11},{9,10},{10,... | collective-permute-start | bytes 1327112 | tf_op jit(solution)/shard_map/ppermute | solution.py:52
  94.8 19.1 %collective-permute-start.13 = (bf16[432,512]{1,0:T(8,128)(2,1)}, bf16[432,512]{1,0:T(8,128)(2,1)}, u32[]{:S(2)}, u32[]{:S(2)}) collective-permute-start(bf16[432,512]{1,0:T(8,128)(2,1)} %get-tuple-element.135), channel_id=1, source_target_pairs={{0,1},{1,0},{2,3},{3,2},{4,5},{5,4},{6,7},{7,6},{8,9},{9,8},{10,11... | collective-permute-start | bytes 1327112 | tf_op jit(solution)/shard_map/ppermute | solution.py:52
  114.0 22.5 %collective-permute-start.17 = (bf16[432,512]{1,0:T(8,128)(2,1)}, bf16[432,512]{1,0:T(8,128)(2,1)S(1)}, u32[]{:S(2)}, u32[]{:S(2)}) collective-permute-start(bf16[432,512]{1,0:T(8,128)(2,1)} %get-tuple-element.98), channel_id=1, source_target_pairs={{0,1},{1,0},{2,3},{3,2},{4,5},{5,4},{6,7},{7,6},{8,9},{9,8},{10,11... | collective-permute-start | bytes 1327112 | tf_op jit(solution)/shard_map/ppermute | solution.py:52
  115.7 20.8 %collective-permute-start.18 = (bf16[432,512]{1,0:T(8,128)(2,1)S(1)}, bf16[432,512]{1,0:T(8,128)(2,1)S(1)}, u32[]{:S(2)}, u32[]{:S(2)}) collective-permute-start(bf16[432,512]{1,0:T(8,128)(2,1)S(1)} %bitcast.247), channel_id=1, source_target_pairs={{0,2},{1,3},{2,0},{3,1},{4,6},{5,7},{6,4},{7,5},{8,10},{9,11},{10,... | collective-permute-start | bytes 1327112 | tf_op jit(solution)/shard_map/ppermute | solution.py:52
  116.2 20.2 %collective-permute-start.19 = (bf16[64,160]{1,0:T(8,128)(2,1)S(1)}, bf16[64,160]{1,0:T(8,128)(2,1)S(1)}, u32[]{:S(2)}, u32[]{:S(2)}) collective-permute-start(bf16[64,160]{1,0:T(8,128)(2,1)S(1)} %bitcast.260), channel_id=1, source_target_pairs={{0,1},{1,0},{2,3},{3,2},{4,5},{5,4},{6,7},{7,6},{8,9},{9,8},{10,11... | collective-permute-start | bytes 61448 | tf_op jit(solution)/shard_map/ppermute | solution.py:52
  136.5 7.6 %collective-permute-start.20 = (bf16[864,1024]{1,0:T(8,128)(2,1)}, bf16[864,1024]{1,0:T(8,128)(2,1)S(1)}, u32[]{:S(2)}, u32[]{:S(2)}) collective-permute-start(bf16[864,1024]{1,0:T(8,128)(2,1)} %get-tuple-element.101), channel_id=1, source_target_pairs={{0,4},{1,5},{2,6},{3,7},{4,0},{5,1},{6,2},{7,3},{8,12},{9,13},{10,... | collective-permute-start | bytes 5308424 | tf_op jit(solution)/shard_map/ppermute | solution.py:52
  136.6 6.8 %collective-permute-start.21 = (bf16[2,64,160]{2,1,0:T(8,128)(2,1)S(1)}, bf16[2,64,160]{2,1,0:T(8,128)(2,1)S(1)}, u32[]{:S(2)}, u32[]{:S(2)}) collective-permute-start(bf16[2,64,160]{2,1,0:T(8,128)(2,1)S(1)} %pad_maximum_fusion.11), channel_id=1, source_target_pairs={{0,2},{1,3},{2,0},{3,1},{4,6},{5,7},{6,4},{7,5},{8,10},{9,11},{10,... | collective-permute-start | bytes 122888 | tf_op jit(solution)/shard_map/ppermute | solution.py:52
  147.6 26.3 %collective-permute-start.22 = (bf16[432,1024]{1,0:T(8,128)(2,1)}, bf16[432,1024]{1,0:T(8,128)(2,1)S(1)}, u32[]{:S(2)}, u32[]{:S(2)}) collective-permute-start(bf16[432,1024]{1,0:T(8,128)(2,1)} %get-tuple-element.171), channel_id=1, source_target_pairs={{0,1},{1,0},{2,3},{3,2},{4,5},{5,4},{6,7},{7,6},{8,9},{9,8},{10,11... | collective-permute-start | bytes 2654216 | tf_op jit(solution)/shard_map/ppermute | solution.py:52
  148.1 5.3 %collective-permute-start.23 = (bf16[2,2,64,160]{3,2,1,0:T(8,128)(2,1)}, bf16[2,2,64,160]{3,2,1,0:T(8,128)(2,1)S(1)}, u32[]{:S(2)}, u32[]{:S(2)}) collective-permute-start(bf16[2,2,64,160]{3,2,1,0:T(8,128)(2,1)} %pad_maximum_fusion.10), channel_id=1, source_target_pairs={{0,4},{1,5},{2,6},{3,7},{4,0},{5,1},{6,2},{7,3},{8,12},{9,13},{10,... | collective-permute-start | bytes 245768 | tf_op jit(solution)/shard_map/ppermute | solution.py:52
  149.9 22.4 %collective-permute-start.27 = (bf16[432,256]{1,0:T(8,128)(2,1)}, bf16[432,256]{1,0:T(8,128)(2,1)S(1)}, u32[]{:S(2)}, u32[]{:S(2)}) collective-permute-start(bf16[432,256]{1,0:T(8,128)(2,1)} %bitcast.257), channel_id=1, source_target_pairs={{0,6},{1,7},{2,4},{3,5},{4,2},{5,3},{6,0},{7,1},{8,14},{9,15},{10,... | collective-permute-start | bytes 663560 | tf_op jit(solution)/shard_map/ppermute | solution.py:52
  154.4 19.6 %collective-permute-start.26 = (bf16[2,2,2,64,160]{4,3,2,1,0:T(8,128)(2,1)S(1)}, bf16[2,2,2,64,160]{4,3,2,1,0:T(8,128)(2,1)S(1)}, u32[]{:S(2)}, u32[]{:S(2)}) collective-permute-start(bf16[2,2,2,64,160]{4,3,2,1,0:T(8,128)(2,1)S(1)} %pad_maximum_fusion.9), channel_id=1, source_target_pairs={{0,24},{1,25},{2,26},{3,27},{4,28},{5,29},{6,30},{7,31},{8,16},{9,... | collective-permute-start | bytes 491528 | tf_op jit(solution)/shard_map/ppermute | solution.py:52
  155.9 18.0 %collective-permute-start.25 = (bf16[2,2,2,64,160]{4,3,2,1,0:T(8,128)(2,1)S(1)}, bf16[2,2,2,64,160]{4,3,2,1,0:T(8,128)(2,1)S(1)}, u32[]{:S(2)}, u32[]{:S(2)}) collective-permute-start(bf16[2,2,2,64,160]{4,3,2,1,0:T(8,128)(2,1)S(1)} %pad_maximum_fusion.9), channel_id=1, source_target_pairs={{0,16},{1,17},{2,18},{3,19},{4,20},{5,21},{6,22},{7,23},{8,24},{9,... | collective-permute-start | bytes 491528 | tf_op jit(solution)/shard_map/ppermute | solution.py:52
  156.4 17.5 %collective-permute-start.24 = (bf16[2,2,2,64,160]{4,3,2,1,0:T(8,128)(2,1)S(1)}, bf16[2,2,2,64,160]{4,3,2,1,0:T(8,128)(2,1)S(1)}, u32[]{:S(2)}, u32[]{:S(2)}) collective-permute-start(bf16[2,2,2,64,160]{4,3,2,1,0:T(8,128)(2,1)S(1)} %pad_maximum_fusion.9), channel_id=1, source_target_pairs={{0,8},{1,9},{2,10},{3,11},{4,12},{5,13},{6,14},{7,15},{8,0},{9,1},... | collective-permute-start | bytes 491528 | tf_op jit(solution)/shard_map/ppermute | solution.py:52
  181.8 4.7 %collective-permute-start.31 = (f32[24,256]{1,0:T(8,128)S(1)}, f32[24,256]{1,0:T(8,128)S(1)}, u32[]{:S(2)}, u32[]{:S(2)}) collective-permute-start(f32[24,256]{1,0:T(8,128)S(1)} %pad_maximum_fusion.12), channel_id=1, source_target_pairs={{0,24},{1,25},{2,26},{3,27},{4,28},{5,29},{6,30},{7,31},{8,16},{9,... | collective-permute-start | bytes 73736 | tf_op jit(solution)/shard_map/ppermute | solution.py:52
  182.3 4.2 %collective-permute-start.29 = (f32[24,256]{1,0:T(8,128)S(1)}, f32[24,256]{1,0:T(8,128)S(1)}, u32[]{:S(2)}, u32[]{:S(2)}) collective-permute-start(f32[24,256]{1,0:T(8,128)S(1)} %pad_maximum_fusion.12), channel_id=1, source_target_pairs={{0,8},{1,9},{2,10},{3,11},{4,12},{5,13},{6,14},{7,15},{8,0},{9,1},... | collective-permute-start | bytes 73736 | tf_op jit(solution)/shard_map/ppermute | solution.py:52
  186.6 9.5 %collective-permute-start.34 = (f32[24,256]{1,0:T(8,128)S(1)}, f32[24,256]{1,0:T(8,128)S(1)}, u32[]{:S(2)}, u32[]{:S(2)}) collective-permute-start(f32[24,256]{1,0:T(8,128)S(1)} %pad_maximum_fusion.13.refs_0_), channel_id=1, source_target_pairs={{0,3},{1,2},{2,1},{3,0},{4,7},{5,6},{6,5},{7,4},{8,11},{9,10},{10,... | collective-permute-start | bytes 73736 | tf_op jit(solution)/shard_map/ppermute | solution.py:52
  190.2 6.0 %collective-permute-start.33 = (f32[24,256]{1,0:T(8,128)S(1)}, f32[24,256]{1,0:T(8,128)S(1)}, u32[]{:S(2)}, u32[]{:S(2)}) collective-permute-start(f32[24,256]{1,0:T(8,128)S(1)} %pad_maximum_fusion.13.refs_0_), channel_id=1, source_target_pairs={{0,2},{1,3},{2,0},{3,1},{4,6},{5,7},{6,4},{7,5},{8,10},{9,11},{10,... | collective-permute-start | bytes 73736 | tf_op jit(solution)/shard_map/ppermute | solution.py:52
  191.6 4.6 %collective-permute-start.32 = (f32[24,256]{1,0:T(8,128)S(1)}, f32[24,256]{1,0:T(8,128)S(1)}, u32[]{:S(2)}, u32[]{:S(2)}) collective-permute-start(f32[24,256]{1,0:T(8,128)S(1)} %pad_maximum_fusion.13.refs_0_), channel_id=1, source_target_pairs={{0,1},{1,0},{2,3},{3,2},{4,5},{5,4},{6,7},{7,6},{8,9},{9,8},{10,11... | collective-permute-start | bytes 73736 | tf_op jit(solution)/shard_map/ppermute | solution.py:52
  200.8 4.3 %collective-permute-start.37 = (f32[8,256]{1,0:T(8,128)S(1)}, f32[8,256]{1,0:T(8,128)S(1)}, u32[]{:S(2)}, u32[]{:S(2)}) collective-permute-start(f32[8,256]{1,0:T(8,128)S(1)} %pad_maximum_fusion.14), channel_id=1, source_target_pairs={{0,16},{1,17},{2,18},{3,19},{4,20},{5,21},{6,22},{7,23},{8,24},{9,... | collective-permute-start | bytes 24584 | tf_op jit(solution)/shard_map/ppermute | solution.py:52
  202.0 4.5 %collective-permute-start.38 = (f32[8,256]{1,0:T(8,128)S(1)}, f32[8,256]{1,0:T(8,128)S(1)}, u32[]{:S(2)}, u32[]{:S(2)}) collective-permute-start(f32[8,256]{1,0:T(8,128)S(1)} %pad_maximum_fusion.14), channel_id=1, source_target_pairs={{0,24},{1,25},{2,26},{3,27},{4,28},{5,29},{6,30},{7,31},{8,16},{9,... | collective-permute-start | bytes 24584 | tf_op jit(solution)/shard_map/ppermute | solution.py:52
  207.1 4.6 %collective-permute-start.40 = (f32[8,256]{1,0:T(8,128)S(1)}, f32[8,256]{1,0:T(8,128)S(1)}, u32[]{:S(2)}, u32[]{:S(2)}) collective-permute-start(f32[8,256]{1,0:T(8,128)S(1)} %pad_maximum_fusion.15), channel_id=1, source_target_pairs={{0,2},{1,3},{2,0},{3,1},{4,6},{5,7},{6,4},{7,5},{8,10},{9,11},{10,... | collective-permute-start | bytes 24584 | tf_op jit(solution)/shard_map/ppermute | solution.py:52
  208.7 5.4 %collective-permute-start.41 = (f32[8,256]{1,0:T(8,128)S(1)}, f32[8,256]{1,0:T(8,128)S(1)}, u32[]{:S(2)}, u32[]{:S(2)}) collective-permute-start(f32[8,256]{1,0:T(8,128)S(1)} %pad_maximum_fusion.15), channel_id=1, source_target_pairs={{0,3},{1,2},{2,1},{3,0},{4,7},{5,6},{6,5},{7,4},{8,11},{9,10},{10,... | collective-permute-start | bytes 24584 | tf_op jit(solution)/shard_map/ppermute | solution.py:52
  218.0 4.1 %collective-permute-start.44 = (f32[8,256]{1,0:T(8,128)S(1)}, f32[8,256]{1,0:T(8,128)S(1)}, u32[]{:S(2)}, u32[]{:S(2)}) collective-permute-start(f32[8,256]{1,0:T(8,128)S(1)} %fusion.41), channel_id=1, source_target_pairs={{0,16},{1,17},{2,18},{3,19},{4,20},{5,21},{6,22},{7,23},{8,24},{9,... | collective-permute-start | bytes 24584 | tf_op jit(solution)/shard_map/ppermute | solution.py:52
  219.6 4.5 %collective-permute-start.45 = (f32[8,256]{1,0:T(8,128)S(1)}, f32[8,256]{1,0:T(8,128)S(1)}, u32[]{:S(2)}, u32[]{:S(2)}) collective-permute-start(f32[8,256]{1,0:T(8,128)S(1)} %fusion.41), channel_id=1, source_target_pairs={{0,24},{1,25},{2,26},{3,27},{4,28},{5,29},{6,30},{7,31},{8,16},{9,... | collective-permute-start | bytes 24584 | tf_op jit(solution)/shard_map/ppermute | solution.py:52
  221.5 7.1 %collective-permute-start.56 = (bf16[16,512]{1,0:T(8,128)(2,1)S(1)}, bf16[16,512]{1,0:T(8,128)(2,1)S(1)}, u32[]{:S(2)}, u32[]{:S(2)}) collective-permute-start(bf16[16,512]{1,0:T(8,128)(2,1)S(1)} %copy-done.35), channel_id=1, source_target_pairs={{0,2},{1,3},{2,0},{3,1},{4,6},{5,7},{6,4},{7,5},{8,10},{9,11},{10,... | collective-permute-start | bytes 49160 | tf_op jit(solution)/shard_map/ppermute | solution.py:52
  224.2 5.5 %collective-permute-start.48 = (f32[8,256]{1,0:T(8,128)S(1)}, f32[8,256]{1,0:T(8,128)S(1)}, u32[]{:S(2)}, u32[]{:S(2)}) collective-permute-start(f32[8,256]{1,0:T(8,128)S(1)} %add_add_fusion.2.refs_0_), channel_id=1, source_target_pairs={{0,3},{1,2},{2,1},{3,0},{4,7},{5,6},{6,5},{7,4},{8,11},{9,10},{10,... | collective-permute-start | bytes 24584 | tf_op jit(solution)/shard_map/ppermute | solution.py:52
  226.0 4.5 %collective-permute-start.47 = (f32[8,256]{1,0:T(8,128)S(1)}, f32[8,256]{1,0:T(8,128)S(1)}, u32[]{:S(2)}, u32[]{:S(2)}) collective-permute-start(f32[8,256]{1,0:T(8,128)S(1)} %add_add_fusion.2.refs_0_), channel_id=1, source_target_pairs={{0,2},{1,3},{2,0},{3,1},{4,6},{5,7},{6,4},{7,5},{8,10},{9,11},{10,... | collective-permute-start | bytes 24584 | tf_op jit(solution)/shard_map/ppermute | solution.py:52
  226.0 4.5 %collective-permute-start.46 = (f32[8,256]{1,0:T(8,128)S(1)}, f32[8,256]{1,0:T(8,128)S(1)}, u32[]{:S(2)}, u32[]{:S(2)}) collective-permute-start(f32[8,256]{1,0:T(8,128)S(1)} %add_add_fusion.2.refs_0_), channel_id=1, source_target_pairs={{0,1},{1,0},{2,3},{3,2},{4,5},{5,4},{6,7},{7,6},{8,9},{9,8},{10,11... | collective-permute-start | bytes 24584 | tf_op jit(solution)/shard_map/ppermute | solution.py:52
  233.6 4.6 %collective-permute-start.52 = (f32[16,256]{1,0:T(8,128)S(1)}, f32[16,256]{1,0:T(8,128)S(1)}, u32[]{:S(2)}, u32[]{:S(2)}) collective-permute-start(f32[16,256]{1,0:T(8,128)S(1)} %add.282), channel_id=1, source_target_pairs={{0,24},{1,25},{2,26},{3,27},{4,28},{5,29},{6,30},{7,31},{8,16},{9,... | collective-permute-start | bytes 49160 | tf_op jit(solution)/shard_map/ppermute | solution.py:52
  239.9 5.6 %collective-permute-start.55 = (f32[16,256]{1,0:T(8,128)S(1)}, f32[16,256]{1,0:T(8,128)S(1)}, u32[]{:S(2)}, u32[]{:S(2)}) collective-permute-start(f32[16,256]{1,0:T(8,128)S(1)} %add_add_fusion.1.refs_0_), channel_id=1, source_target_pairs={{0,3},{1,2},{2,1},{3,0},{4,7},{5,6},{6,5},{7,4},{8,11},{9,10},{10,... | collective-permute-start | bytes 49160 | tf_op jit(solution)/shard_map/ppermute | solution.py:52
  242.0 4.8 %collective-permute-start.54 = (f32[16,256]{1,0:T(8,128)S(1)}, f32[16,256]{1,0:T(8,128)S(1)}, u32[]{:S(2)}, u32[]{:S(2)}) collective-permute-start(f32[16,256]{1,0:T(8,128)S(1)} %add_add_fusion.1.refs_0_), channel_id=1, source_target_pairs={{0,2},{1,3},{2,0},{3,1},{4,6},{5,7},{6,4},{7,5},{8,10},{9,11},{10,... | collective-permute-start | bytes 49160 | tf_op jit(solution)/shard_map/ppermute | solution.py:52
  249.0 35.3 %collective-permute-start.60 = (bf16[432,1024]{1,0:T(8,128)(2,1)S(1)}, bf16[432,1024]{1,0:T(8,128)(2,1)}, u32[]{:S(2)}, u32[]{:S(2)}) collective-permute-start(bf16[432,1024]{1,0:T(8,128)(2,1)S(1)} %get-tuple-element.121.refs_0_.refs_4_), channel_id=1, source_target_pairs={{0,4},{1,5},{2,6},{3,7},{4,0},{5,1},{6,2},{7,3},{8,12},{9,13},{10,... | collective-permute-start | bytes 2654216 | tf_op jit(solution)/shard_map/ppermute | solution.py:52
  249.0 31.6 %collective-permute-start.57 = (bf16[432,1024]{1,0:T(8,128)(2,1)S(1)}, bf16[432,1024]{1,0:T(8,128)(2,1)}, u32[]{:S(2)}, u32[]{:S(2)}) collective-permute-start(bf16[432,1024]{1,0:T(8,128)(2,1)S(1)} %get-tuple-element.121.refs_0_.refs_4_), channel_id=1, source_target_pairs={{0,1},{1,0},{2,3},{3,2},{4,5},{5,4},{6,7},{7,6},{8,9},{9,8},{10,11... | collective-permute-start | bytes 2654216 | tf_op jit(solution)/shard_map/ppermute | solution.py:52
  252.3 26.9 %collective-permute-start.58 = (bf16[432,512]{1,0:T(8,128)(2,1)S(1)}, bf16[432,512]{1,0:T(8,128)(2,1)}, u32[]{:S(2)}, u32[]{:S(2)}) collective-permute-start(bf16[432,512]{1,0:T(8,128)(2,1)S(1)} %get-tuple-element.122), channel_id=1, source_target_pairs={{0,2},{1,3},{2,0},{3,1},{4,6},{5,7},{6,4},{7,5},{8,10},{9,11},{10,... | collective-permute-start | bytes 1327112 | tf_op jit(solution)/shard_map/ppermute | solution.py:52
  282.6 22.6 %collective-permute-start.65 = (bf16[432,512]{1,0:T(8,128)(2,1)}, bf16[432,512]{1,0:T(8,128)(2,1)S(1)}, u32[]{:S(2)}, u32[]{:S(2)}) collective-permute-start(bf16[432,512]{1,0:T(8,128)(2,1)} %collective-permute-done.58.refs_8_), channel_id=1, source_target_pairs={{0,1},{1,0},{2,3},{3,2},{4,5},{5,4},{6,7},{7,6},{8,9},{9,8},{10,11... | collective-permute-start | bytes 1327112 | tf_op jit(solution)/shard_map/ppermute | solution.py:52
  284.3 22.6 %collective-permute-start.63 = (bf16[2,2,2,64,160]{4,3,2,1,0:T(8,128)(2,1)S(1)}, bf16[2,2,2,64,160]{4,3,2,1,0:T(8,128)(2,1)S(1)}, u32[]{:S(2)}, u32[]{:S(2)}) collective-permute-start(bf16[2,2,2,64,160]{4,3,2,1,0:T(8,128)(2,1)S(1)} %fusion.6), channel_id=1, source_target_pairs={{0,8},{1,9},{2,10},{3,11},{4,12},{5,13},{6,14},{7,15},{8,0},{9,1},... | collective-permute-start | bytes 491528 | tf_op jit(solution)/shard_map/ppermute | solution.py:52
  285.3 21.1 %collective-permute-start.66 = (bf16[432,512]{1,0:T(8,128)(2,1)}, bf16[432,512]{1,0:T(8,128)(2,1)S(1)}, u32[]{:S(2)}, u32[]{:S(2)}) collective-permute-start(bf16[432,512]{1,0:T(8,128)(2,1)} %get-tuple-element.135), channel_id=1, source_target_pairs={{0,3},{1,2},{2,1},{3,0},{4,7},{5,6},{6,5},{7,4},{8,11},{9,10},{10,... | collective-permute-start | bytes 1327112 | tf_op jit(solution)/shard_map/ppermute | solution.py:52
  305.1 25.8 %collective-permute-start.62 = (bf16[432,256]{1,0:T(8,128)(2,1)S(1)}, bf16[432,256]{1,0:T(8,128)(2,1)S(1)}, u32[]{:S(2)}, u32[]{:S(2)}) collective-permute-start(bf16[432,256]{1,0:T(8,128)(2,1)S(1)} %copy-done.21), channel_id=1, source_target_pairs={{0,6},{1,7},{2,4},{3,5},{4,2},{5,3},{6,0},{7,1},{8,14},{9,15},{10,... | collective-permute-start | bytes 663560 | tf_op jit(solution)/shard_map/ppermute | solution.py:52
  307.0 25.0 %collective-permute-start.64 = (bf16[1,2,2,64,160]{4,3,2,1,0:T(8,128)(2,1)S(1)}, bf16[1,2,2,64,160]{4,3,2,1,0:T(8,128)(2,1)S(1)}, u32[]{:S(2)}, u32[]{:S(2)}) collective-permute-start(bf16[1,2,2,64,160]{4,3,2,1,0:T(8,128)(2,1)S(1)} %select_bitcast_fusion.8), channel_id=1, source_target_pairs={{0,16},{1,17},{2,18},{3,19},{4,20},{5,21},{6,22},{7,23},{8,24},{9,... | collective-permute-start | bytes 245768 | tf_op jit(solution)/shard_map/ppermute | solution.py:52
  309.0 27.8 %collective-permute-start.69 = (bf16[432,512]{1,0:T(8,128)(2,1)}, bf16[432,512]{1,0:T(8,128)(2,1)}, u32[]{:S(2)}, u32[]{:S(2)}) collective-permute-start(bf16[432,512]{1,0:T(8,128)(2,1)} %get-tuple-element.138), channel_id=1, source_target_pairs={{0,2},{1,3},{2,0},{3,1},{4,6},{5,7},{6,4},{7,5},{8,10},{9,11},{10,... | collective-permute-start | bytes 1327112 | tf_op jit(solution)/shard_map/ppermute | solution.py:52
  310.5 26.4 %collective-permute-start.70 = (bf16[432,512]{1,0:T(8,128)(2,1)}, bf16[432,512]{1,0:T(8,128)(2,1)S(1)}, u32[]{:S(2)}, u32[]{:S(2)}) collective-permute-start(bf16[432,512]{1,0:T(8,128)(2,1)} %get-tuple-element.139), channel_id=1, source_target_pairs={{0,1},{1,0},{2,3},{3,2},{4,5},{5,4},{6,7},{7,6},{8,9},{9,8},{10,11... | collective-permute-start | bytes 1327112 | tf_op jit(solution)/shard_map/ppermute | solution.py:52
  329.2 12.6 %collective-permute-start.74 = (bf16[29,64,128]{2,1,0:T(8,128)(2,1)}, bf16[29,64,128]{2,1,0:T(8,128)(2,1)S(1)}, u32[]{:S(2)}, u32[]{:S(2)}) collective-permute-start(bf16[29,64,128]{2,1,0:T(8,128)(2,1)} %get-tuple-element.144), channel_id=1, source_target_pairs={{0,16},{1,17},{2,18},{3,19},{4,20},{5,21},{6,22},{7,23},{8,24},{9,... | collective-permute-start | bytes 1425416 | tf_op jit(solution)/shard_map/ppermute | solution.py:52
  330.8 12.2 %collective-permute-start.75 = (bf16[29,64,128]{2,1,0:T(8,128)(2,1)}, bf16[29,64,128]{2,1,0:T(8,128)(2,1)S(1)}, u32[]{:S(2)}, u32[]{:S(2)}) collective-permute-start(bf16[29,64,128]{2,1,0:T(8,128)(2,1)} %get-tuple-element.145), channel_id=1, source_target_pairs={{0,8},{1,9},{2,10},{3,11},{4,12},{5,13},{6,14},{7,15},{8,0},{9,1},... | collective-permute-start | bytes 1425416 | tf_op jit(solution)/shard_map/ppermute | solution.py:52
  336.9 14.6 %collective-permute-start.78 = (bf16[2,64,160]{2,1,0:T(8,128)(2,1)S(1)}, bf16[2,64,160]{2,1,0:T(8,128)(2,1)S(1)}, u32[]{:S(2)}, u32[]{:S(2)}) collective-permute-start(bf16[2,64,160]{2,1,0:T(8,128)(2,1)S(1)} %select_bitcast_fusion.11), channel_id=1, source_target_pairs={{0,2},{1,3},{2,0},{3,1},{4,6},{5,7},{6,4},{7,5},{8,10},{9,11},{10,... | collective-permute-start | bytes 122888 | tf_op jit(solution)/shard_map/ppermute | solution.py:52
  336.9 24.8 %collective-permute-start.71 = (bf16[432,512]{1,0:T(8,128)(2,1)}, bf16[432,512]{1,0:T(8,128)(2,1)S(1)}, u32[]{:S(2)}, u32[]{:S(2)}) collective-permute-start(bf16[432,512]{1,0:T(8,128)(2,1)} %get-tuple-element.140), channel_id=1, source_target_pairs={{0,2},{1,3},{2,0},{3,1},{4,6},{5,7},{6,4},{7,5},{8,10},{9,11},{10,... | collective-permute-start | bytes 1327112 | tf_op jit(solution)/shard_map/ppermute | solution.py:52
  339.8 21.9 %collective-permute-start.72 = (bf16[432,512]{1,0:T(8,128)(2,1)}, bf16[432,512]{1,0:T(8,128)(2,1)S(1)}, u32[]{:S(2)}, u32[]{:S(2)}) collective-permute-start(bf16[432,512]{1,0:T(8,128)(2,1)} %collective-permute-done.69), channel_id=1, source_target_pairs={{0,1},{1,0},{2,3},{3,2},{4,5},{5,4},{6,7},{7,6},{8,9},{9,8},{10,11... | collective-permute-start | bytes 1327112 | tf_op jit(solution)/shard_map/ppermute | solution.py:52
  344.4 21.3 %collective-permute-start.77 = (bf16[2,29,64,128]{3,2,1,0:T(8,128)(2,1)S(1)}, bf16[2,29,64,128]{3,2,1,0:T(8,128)(2,1)S(1)}, u32[]{:S(2)}, u32[]{:S(2)}) collective-permute-start(bf16[2,29,64,128]{3,2,1,0:T(8,128)(2,1)S(1)} %pad_maximum_fusion.2), channel_id=1, source_target_pairs={{0,16},{1,17},{2,18},{3,19},{4,20},{5,21},{6,22},{7,23},{8,24},{9,... | collective-permute-start | bytes 2850824 | tf_op jit(solution)/shard_map/ppermute | solution.py:52
  345.4 21.3 %collective-permute-start.76 = (bf16[2,29,64,128]{3,2,1,0:T(8,128)(2,1)S(1)}, bf16[2,29,64,128]{3,2,1,0:T(8,128)(2,1)S(1)}, u32[]{:S(2)}, u32[]{:S(2)}) collective-permute-start(bf16[2,29,64,128]{3,2,1,0:T(8,128)(2,1)S(1)} %pad_maximum_fusion.1), channel_id=1, source_target_pairs={{0,8},{1,9},{2,10},{3,11},{4,12},{5,13},{6,14},{7,15},{8,0},{9,1},... | collective-permute-start | bytes 2850824 | tf_op jit(solution)/shard_map/ppermute | solution.py:52
  362.0 6.1 %collective-permute-start.73 = (bf16[2,432,512]{2,1,0:T(8,128)(2,1)S(1)}, bf16[2,432,512]{2,1,0:T(8,128)(2,1)S(1)}, u32[]{:S(2)}, u32[]{:S(2)}) collective-permute-start(bf16[2,432,512]{2,1,0:T(8,128)(2,1)S(1)} %pad_maximum_fusion.4), channel_id=1, source_target_pairs={{0,4},{1,5},{2,6},{3,7},{4,0},{5,1},{6,2},{7,3},{8,12},{9,13},{10,... | collective-permute-start | bytes 2654216 | tf_op jit(solution)/shard_map/ppermute | solution.py:52
  367.3 11.6 %collective-permute-start.79 = (bf16[29,64,128]{2,1,0:T(8,128)(2,1)S(1)}, bf16[29,64,128]{2,1,0:T(8,128)(2,1)S(1)}, u32[]{:S(2)}, u32[]{:S(2)}) collective-permute-start(bf16[29,64,128]{2,1,0:T(8,128)(2,1)S(1)} %broadcast_select_fusion.7), channel_id=1, source_target_pairs={{0,1},{1,0},{2,3},{3,2},{4,5},{5,4},{6,7},{7,6},{8,9},{9,8},{10,11... | collective-permute-start | bytes 1425416 | tf_op jit(solution)/shard_map/ppermute | solution.py:52
  370.4 7.8 %collective-permute-start.81 = (bf16[1,64,160]{2,1,0:T(8,128)(2,1)S(1)}, bf16[1,64,160]{2,1,0:T(8,128)(2,1)S(1)}, u32[]{:S(2)}, u32[]{:S(2)}) collective-permute-start(bf16[1,64,160]{2,1,0:T(8,128)(2,1)S(1)} %select_bitcast_fusion.14), channel_id=1, source_target_pairs={{0,1},{1,0},{2,3},{3,2},{4,5},{5,4},{6,7},{7,6},{8,9},{9,8},{10,11... | collective-permute-start | bytes 61448 | tf_op jit(solution)/shard_map/ppermute | solution.py:52
  (68 other events, 490.7 us)

commit v2 on v1

--- a/solution.py
+++ b/solution.py
@@ -227,6 +227,7 @@
 SMEM = pl.BlockSpec(memory_space=pltpu.SMEM)
 VMEM = pl.BlockSpec(memory_space=pltpu.VMEM)
 PARAMS = pltpu.CompilerParams(vmem_limit_bytes=58 * 2**20)
+TINY = pltpu.CompilerParams(vmem_limit_bytes=8 * 2**20)
 SMALL = pltpu.CompilerParams(vmem_limit_bytes=12 * 2**20)
 
 
@@ -380,7 +381,7 @@
         in_specs=[SMEM] + [ANY] * 5,
         out_specs=VMEM,
         scratch_shapes=[pltpu.SemaphoreType.DMA],
-        compiler_params=PARAMS,
+        compiler_params=TINY,
         cost_estimate=LIGHT,
         name="assembled_weights",
     )(info, own, by_x, by_y, *diagonal)

time: 387 us -> 384 us (level)
  Pallas kernels: 76.5 us -> 71.9 us
  local copies, waits for them, and re-layouts: 24.2 us -> 28.2 us
  waiting for transfers between devices: 158 us -> 154 us
    unnamed x100 -> x114, local copies, waits for them, and re-layouts: 8.98 us -> 14.6 us
    ppermute x82, waiting for transfers between devices: 158 us -> 154 us  [swap(): return lax.ppermute(x, AXES, pairs)]
  transfers between devices with their start and end apart: 82 -> 82, of which waited for: 43 -> 46; matrix products, arithmetic and copies ran while one was open for 9% -> 9% of each run, Pallas kernels for 18% -> 17%
where the time goes in v2:
time: 384 us; the launch traced here: 380 us
  waiting for transfers between devices  154 us (40%)
  starting transfers between devices  92.9 us (24%)
  Pallas kernels  71.9 us (19%)
  other arithmetic  28.4 us (7%)
  local copies, waits for them, and re-layouts  28.2 us (7%)
    ppermute x82, waiting for transfers between devices, swap(): return lax.ppermute(x, AXES, pairs)  154 us
    ppermute x82, starting transfers between devices, swap(): return lax.ppermute(x, AXES, pairs)  92.9 us
    pallas_call x1, Pallas kernels, branch_sums(): pl.pallas_call(kernel, out_shape=half_shapes(shape, 4) + [jax.ShapeDtypeS...  18.4 us
    pallas_call x1, Pallas kernels, input_gradient(): pl.pallas_call(kernel, out_shape=[jax.ShapeDtypeStruct((shape.band, shape...  18 us
    pallas_call x1, Pallas kernels, weight_gradients(): pl.pallas_call(kernel, out_shape=out_shape, in_specs=[SMEM] + [ANY] * (4...  17.5 us
    unnamed x114, local copies, waits for them, and re-layouts  14.6 us
  transfers between devices with their start and end apart: 82, of which 46 were waited for; matrix products, arithmetic and copies ran while one was open for 9% of the time, Pallas kernels for 17%

profile of v2, /device:TPU:0, one launch (start us, length us, event | category | flops | bytes accessed | tf_op | source)
XLA Modules:
  0.0 379.8 jit_solution(1303701339616915937)
XLA Ops:
  5.5 2.6 collective-permute-start.4
  10.7 2.7 collective-permute-start.3
  14.4 9.5 %collective-permute-done.3.first = bf16[14,64,128]{2,1,0:T(8,128)(2,1)S(1)} collective-permute-done((bf16[14,64,128]{2,1,0:T(8,128)(2,1)S(1)}, bf16[14,64,128]{2,1,0:T(8,128)(2,1)S(1)}, u32[]{:S(2)}, u32[]{:S(2)}) %collective-permute-start.3) | collective-permute-done | bytes 229408 | tf_op jit(solution)/shard_map/ppermute | solution.py:52
  25.7 1.7 collective-permute-start.8
  27.4 1.5 collective-permute-start.6
  28.9 3.0 collective-permute-start.5
  31.9 1.6 broadcast_select_fusion.2
  33.5 15.0 %collective-permute-done.8.refs_2_ = bf16[29,128,128]{2,1,0:T(8,128)(2,1)S(1)} collective-permute-done((bf16[29,128,128]{2,1,0:T(8,128)(2,1)S(1)}, bf16[29,128,128]{2,1,0:T(8,128)(2,1)S(1)}, u32[]{:S(2)}, u32[]{:S(2)}) %collective-permute-start.8) | collective-permute-done | bytes 950304 | tf_op jit(solution)/shard_map/ppermute | solution.py:52
  48.6 1.5 collective-permute-start.9
  50.1 1.6 collective-permute-start.7
  53.6 9.4 %collective-permute-done.5.rest = bf16[44,64,128]{2,1,0:T(8,128)(2,1)S(1)} collective-permute-done((bf16[44,64,128]{2,1,0:T(8,128)(2,1)}, bf16[44,64,128]{2,1,0:T(8,128)(2,1)S(1)}, u32[]{:S(2)}, u32[]{:S(2)}) %collective-permute-start.5) | collective-permute-done | bytes 720928 | tf_op jit(solution)/shard_map/ppermute | solution.py:52
  64.2 2.9 collective-permute-start.12
  67.1 17.5 %collective-permute-done.12.refs_2_ = bf16[432,512]{1,0:T(8,128)(2,1)S(1)} collective-permute-done((bf16[432,512]{1,0:T(8,128)(2,1)S(1)}, bf16[432,512]{1,0:T(8,128)(2,1)S(1)}, u32[]{:S(2)}, u32[]{:S(2)}) %collective-permute-start.12) | collective-permute-done | bytes 442400 | tf_op jit(solution)/shard_map/ppermute | solution.py:52
  85.8 1.5 collective-permute-start.15
  89.4 3.5 collective-permute-start.14
  98.3 3.2 assembled_weights.2.refs_4_.refs_5_
  101.5 1.9 copy-done.2
  103.4 4.1 %assembled_weights.3.refs_5_.refs_6_ = bf16[29,128,512]{2,1,0:T(8,128)(2,1)S(1)} custom-call(s32[8]{0:T(128)S(1)} %stack.122.info, bf16[29,128,128]{2,1,0:T(8,128)(2,1)S(1)} %packed_far.1.refs_0_, bf16[29,128,128]{2,1,0:T(8,128)(2,1)S(1)} %collective-permute-done.10.refs_1_, bf16[29,128,128]{2,1,0:T(8,128)(2,1)S(1)} %copy-done.7, ...), custom_call_target="tpu_custom_call" | custom-call | tf_op jit(solution)/shard_map/assembled_weights/pallas_call | solution.py:378
  107.5 1.9 copy-done.3
  109.4 1.7 collective-permute-done.13.refs_1_
  111.1 1.7 collective-permute-start.17
  114.9 18.4 %branch_sums.1 = (f32[864,1024]{1,0:T(8,128)}, bf16[864,1024]{1,0:T(8,128)(2,1)}, bf16[16,512]{1,0:T(8,128)(2,1)}, f32[16,256]{1,0:T(8,128)}) custom-call(s32[8]{0:T(128)} %copy-done.23, f32[1]{0:T(128)} %bitcast.11.area, bf16[432,512]{1,0:T(8,128)(2,1)} %bitcast.247, bf16[432,512]{1,0:T(8,128)(2,1)} %collective-permute-done.13.refs_1_, ...), custom_call_target="tpu_custom_call" | custom-call | tf_op jit(solution)/shard_map/branch_sums/pallas_call | solution.py:481
  133.6 2.4 collective-permute-start.21
  136.0 4.4 %collective-permute-done.21 = bf16[2,64,160]{2,1,0:T(8,128)(2,1)S(1)} collective-permute-done((bf16[2,64,160]{2,1,0:T(8,128)(2,1)S(1)}, bf16[2,64,160]{2,1,0:T(8,128)(2,1)S(1)}, u32[]{:S(2)}, u32[]{:S(2)}) %collective-permute-start.21) | collective-permute-done | bytes 40992 | tf_op jit(solution)/shard_map/ppermute | solution.py:52
  141.2 3.5 fusion.2
  146.9 3.5 collective-permute-start.27
  151.4 1.6 collective-permute-start.26
  154.9 14.4 %collective-permute-done.27 = bf16[432,256]{1,0:T(8,128)(2,1)S(1)} collective-permute-done((bf16[432,256]{1,0:T(8,128)(2,1)}, bf16[432,256]{1,0:T(8,128)(2,1)S(1)}, u32[]{:S(2)}, u32[]{:S(2)}) %collective-permute-start.27) | collective-permute-done | bytes 221216 | tf_op jit(solution)/shard_map/ppermute | solution.py:52
  169.3 1.6 broadcast_select_fusion.24
  174.4 1.5 branch_moments.1
  177.2 1.5 collective-permute-start.30
  178.7 1.5 collective-permute-start.31
  181.1 2.3 collective-permute-done.31
  184.1 3.6 collective-permute-start.34
  189.3 2.0 copy.48
  191.3 2.2 reshape.330.projection
  193.7 1.6 projected.1
  204.1 1.6 collective-permute-start.40
  205.8 2.8 collective-permute-start.41
  208.8 2.4 collective-permute-done.41
  216.5 1.5 collective-permute-start.45
  219.2 1.8 collective-permute-done.45
  221.6 1.8 collective-permute-start.48
  223.5 2.6 collective-permute-start.46
  228.0 1.8 branch_gradients.1
  231.0 1.5 collective-permute-start.52
  236.9 2.1 collective-permute-start.55
  244.0 2.0 branch_deltas.1
  252.6 23.7 %collective-permute-done.58.refs_8_ = bf16[432,512]{1,0:T(8,128)(2,1)} collective-permute-done((bf16[432,512]{1,0:T(8,128)(2,1)S(1)}, bf16[432,512]{1,0:T(8,128)(2,1)}, u32[]{:S(2)}, u32[]{:S(2)}) %collective-permute-start.58) | collective-permute-done | bytes 442400 | tf_op jit(solution)/shard_map/ppermute | solution.py:52
  276.3 1.5 collective-permute-done.57.refs_1_.refs_5_
  279.6 1.7 collective-permute-start.65
  282.8 1.8 collective-permute-start.66
  284.6 18.0 %input_gradient.1 = (bf16[432,512]{1,0:T(8,128)(2,1)}, bf16[432,512]{1,0:T(8,128)(2,1)}, bf16[432,512]{1,0:T(8,128)(2,1)}, bf16[432,512]{1,0:T(8,128)(2,1)}) custom-call(s32[8]{0:T(128)} %copy-done.23, f32[1]{0:T(128)} %bitcast.11.area, bf16[432,1024]{1,0:T(8,128)(2,1)} %copy-done.27, bf16[432,1024]{1,0:T(8,128)(2,1)} %collective-permute-done.57.refs_1_.refs_5_, ...), custom_call_target="tpu_custom_call" | custom-call | flops 9965666304 | bytes 16777216 | tf_op jit(solution)/shard_map/input_gradient/pallas_call | solution.py:736
  304.1 1.5 collective-permute-start.64
  306.0 1.9 collective-permute-start.69
  308.7 17.5 %weight_gradients.1 = (bf16[29,64,128]{2,1,0:T(8,128)(2,1)}, bf16[29,64,128]{2,1,0:T(8,128)(2,1)}, bf16[29,64,128]{2,1,0:T(8,128)(2,1)}, bf16[29,64,128]{2,1,0:T...) custom-call(s32[8]{0:T(128)} %copy-done.23, ...), custom_call_target="tpu_custom_call" | custom-call | flops 9965666304 | bytes 16777216 | tf_op jit(solution)/shard_map/weight_gradients/pallas_call | solution.py:848
  329.2 5.2 %collective-permute-done.69 = bf16[432,512]{1,0:T(8,128)(2,1)} collective-permute-done((bf16[432,512]{1,0:T(8,128)(2,1)}, bf16[432,512]{1,0:T(8,128)(2,1)}, u32[]{:S(2)}, u32[]{:S(2)}) %collective-permute-start.69) | collective-permute-done | bytes 442400 | tf_op jit(solution)/shard_map/ppermute | solution.py:52
  334.4 2.9 collective-permute-start.71
  337.3 1.5 collective-permute-done.74
  343.7 5.2 %collective-permute-done.78 = bf16[2,64,160]{2,1,0:T(8,128)(2,1)S(1)} collective-permute-done((bf16[2,64,160]{2,1,0:T(8,128)(2,1)S(1)}, bf16[2,64,160]{2,1,0:T(8,128)(2,1)S(1)}, u32[]{:S(2)}, u32[]{:S(2)}) %collective-permute-start.78) | collective-permute-done | bytes 40992 | tf_op jit(solution)/shard_map/ppermute | solution.py:52
  349.0 10.2 %collective-permute-done.71 = bf16[432,512]{1,0:T(8,128)(2,1)S(1)} collective-permute-done((bf16[432,512]{1,0:T(8,128)(2,1)}, bf16[432,512]{1,0:T(8,128)(2,1)S(1)}, u32[]{:S(2)}, u32[]{:S(2)}) %collective-permute-start.71) | collective-permute-done | bytes 442400 | tf_op jit(solution)/shard_map/ppermute | solution.py:52
  359.7 2.9 collective-permute-done.77
  365.6 2.3 join_features.1
  369.3 5.8 %collective-permute-done.81 = bf16[1,64,160]{2,1,0:T(8,128)(2,1)S(1)} collective-permute-done((bf16[1,64,160]{2,1,0:T(8,128)(2,1)S(1)}, bf16[1,64,160]{2,1,0:T(8,128)(2,1)S(1)}, u32[]{:S(2)}, u32[]{:S(2)}) %collective-permute-start.81) | collective-permute-done | bytes 20512 | tf_op jit(solution)/shard_map/ppermute | solution.py:52
  (362 shorter events, 95.2 us)
Async XLA Ops:
  5.5 19.2 %collective-permute-start.4 = (bf16[29,64,128]{2,1,0:T(8,128)(2,1)}, bf16[29,64,128]{2,1,0:T(8,128)(2,1)S(1)}, u32[]{:S(2)}, u32[]{:S(2)}) collective-permute-start(bf16[29,64,128]{2,1,0:T(8,128)(2,1)} %get-tuple-element.183), channel_id=1, source_target_pairs={{0,1},{1,0},{2,3},{3,2},{4,5},{5,4},{6,7},{7,6},{8,9},{9,8},{10,11... | collective-permute-start | bytes 1425416 | tf_op jit(solution)/shard_map/ppermute | solution.py:52
  10.4 21.5 %collective-permute-start.1 = (bf16[2,432,512]{2,1,0:T(8,128)(2,1)}, bf16[2,432,512]{2,1,0:T(8,128)(2,1)}, u32[]{:S(2)}, u32[]{:S(2)}) collective-permute-start(bf16[2,432,512]{2,1,0:T(8,128)(2,1)} %get-tuple-element.84), channel_id=1, source_target_pairs={{0,4},{1,5},{2,6},{3,7},{4,0},{5,1},{6,2},{7,3},{8,12},{9,13},{10,... | collective-permute-start | bytes 2654216 | tf_op jit(solution)/shard_map/ppermute | solution.py:52
  10.7 13.3 %collective-permute-start.3 = (bf16[14,64,128]{2,1,0:T(8,128)(2,1)S(1)}, bf16[14,64,128]{2,1,0:T(8,128)(2,1)S(1)}, u32[]{:S(2)}, u32[]{:S(2)}) collective-permute-start(bf16[14,64,128]{2,1,0:T(8,128)(2,1)S(1)} %slice.502), channel_id=1, source_target_pairs={{0,2},{1,3},{2,0},{3,1},{4,6},{5,7},{6,4},{7,5},{8,10},{9,11},{10,... | collective-permute-start | bytes 688136 | tf_op jit(solution)/shard_map/ppermute | solution.py:52
  25.7 22.9 %collective-permute-start.8 = (bf16[29,128,128]{2,1,0:T(8,128)(2,1)S(1)}, bf16[29,128,128]{2,1,0:T(8,128)(2,1)S(1)}, u32[]{:S(2)}, u32[]{:S(2)}) collective-permute-start(bf16[29,128,128]{2,1,0:T(8,128)(2,1)S(1)} %get-tuple-element.87.refs_0_), channel_id=1, source_target_pairs={{0,16},{1,17},{2,18},{3,19},{4,20},{5,21},{6,22},{7,23},{8,24},{9,... | collective-permute-start | bytes 2850824 | tf_op jit(solution)/shard_map/ppermute | solution.py:52
  27.4 22.7 %collective-permute-start.6 = (bf16[29,128,128]{2,1,0:T(8,128)(2,1)S(1)}, bf16[29,128,128]{2,1,0:T(8,128)(2,1)S(1)}, u32[]{:S(2)}, u32[]{:S(2)}) collective-permute-start(bf16[29,128,128]{2,1,0:T(8,128)(2,1)S(1)} %get-tuple-element.87.refs_0_), channel_id=1, source_target_pairs={{0,8},{1,9},{2,10},{3,11},{4,12},{5,13},{6,14},{7,15},{8,0},{9,1},... | collective-permute-start | bytes 2850824 | tf_op jit(solution)/shard_map/ppermute | solution.py:52
  28.9 34.1 %collective-permute-start.5 = (bf16[44,64,128]{2,1,0:T(8,128)(2,1)}, bf16[44,64,128]{2,1,0:T(8,128)(2,1)S(1)}, u32[]{:S(2)}, u32[]{:S(2)}) collective-permute-start(bf16[44,64,128]{2,1,0:T(8,128)(2,1)} %copy-done.28), channel_id=1, source_target_pairs={{0,2},{1,3},{2,0},{3,1},{4,6},{5,7},{6,4},{7,5},{8,10},{9,11},{10,... | collective-permute-start | bytes 2162696 | tf_op jit(solution)/shard_map/ppermute | solution.py:52
  48.6 14.4 %collective-permute-start.9 = (bf16[14,128,128]{2,1,0:T(8,128)(2,1)S(1)}, bf16[14,128,128]{2,1,0:T(8,128)(2,1)S(1)}, u32[]{:S(2)}, u32[]{:S(2)}) collective-permute-start(bf16[14,128,128]{2,1,0:T(8,128)(2,1)S(1)} %slice.504), channel_id=1, source_target_pairs={{0,8},{1,9},{2,10},{3,11},{4,12},{5,13},{6,14},{7,15},{8,0},{9,1},... | collective-permute-start | bytes 1376264 | tf_op jit(solution)/shard_map/ppermute | solution.py:52
  50.1 12.9 %collective-permute-start.7 = (bf16[15,128,128]{2,1,0:T(8,128)(2,1)S(1)}, bf16[15,128,128]{2,1,0:T(8,128)(2,1)S(1)}, u32[]{:S(2)}, u32[]{:S(2)}) collective-permute-start(bf16[15,128,128]{2,1,0:T(8,128)(2,1)S(1)} %slice.503), channel_id=1, source_target_pairs={{0,16},{1,17},{2,18},{3,19},{4,20},{5,21},{6,22},{7,23},{8,24},{9,... | collective-permute-start | bytes 1474568 | tf_op jit(solution)/shard_map/ppermute | solution.py:52
  63.1 21.5 %collective-permute-start.11 = (bf16[29,128,128]{2,1,0:T(8,128)(2,1)S(1)}, bf16[29,128,128]{2,1,0:T(8,128)(2,1)S(1)}, u32[]{:S(2)}, u32[]{:S(2)}) collective-permute-start(bf16[29,128,128]{2,1,0:T(8,128)(2,1)S(1)} %packed_far.1.refs_0_), channel_id=1, source_target_pairs={{0,16},{1,17},{2,18},{3,19},{4,20},{5,21},{6,22},{7,23},{8,24},{9,... | collective-permute-start | bytes 2850824 | tf_op jit(solution)/shard_map/ppermute | solution.py:52
  63.7 21.2 %collective-permute-start.10 = (bf16[29,128,128]{2,1,0:T(8,128)(2,1)S(1)}, bf16[29,128,128]{2,1,0:T(8,128)(2,1)S(1)}, u32[]{:S(2)}, u32[]{:S(2)}) collective-permute-start(bf16[29,128,128]{2,1,0:T(8,128)(2,1)S(1)} %packed_far.1.refs_0_), channel_id=1, source_target_pairs={{0,8},{1,9},{2,10},{3,11},{4,12},{5,13},{6,14},{7,15},{8,0},{9,1},... | collective-permute-start | bytes 2850824 | tf_op jit(solution)/shard_map/ppermute | solution.py:52
  64.2 20.4 %collective-permute-start.12 = (bf16[432,512]{1,0:T(8,128)(2,1)S(1)}, bf16[432,512]{1,0:T(8,128)(2,1)S(1)}, u32[]{:S(2)}, u32[]{:S(2)}) collective-permute-start(bf16[432,512]{1,0:T(8,128)(2,1)S(1)} %bitcast.254), channel_id=1, source_target_pairs={{0,2},{1,3},{2,0},{3,1},{4,6},{5,7},{6,4},{7,5},{8,10},{9,11},{10,... | collective-permute-start | bytes 1327112 | tf_op jit(solution)/shard_map/ppermute | solution.py:52
  85.8 17.6 %collective-permute-start.15 = (bf16[15,128,128]{2,1,0:T(8,128)(2,1)}, bf16[15,128,128]{2,1,0:T(8,128)(2,1)}, u32[]{:S(2)}, u32[]{:S(2)}) collective-permute-start(bf16[15,128,128]{2,1,0:T(8,128)(2,1)} %slice.404), channel_id=1, source_target_pairs={{0,16},{1,17},{2,18},{3,19},{4,20},{5,21},{6,22},{7,23},{8,24},{9,... | collective-permute-start | bytes 1474568 | tf_op jit(solution)/shard_map/ppermute | solution.py:52
  88.2 15.2 %collective-permute-start.16 = (bf16[14,128,128]{2,1,0:T(8,128)(2,1)}, bf16[14,128,128]{2,1,0:T(8,128)(2,1)}, u32[]{:S(2)}, u32[]{:S(2)}) collective-permute-start(bf16[14,128,128]{2,1,0:T(8,128)(2,1)} %slice.405), channel_id=1, source_target_pairs={{0,8},{1,9},{2,10},{3,11},{4,12},{5,13},{6,14},{7,15},{8,0},{9,1},... | collective-permute-start | bytes 1376264 | tf_op jit(solution)/shard_map/ppermute | solution.py:52
  89.4 20.0 %collective-permute-start.14 = (bf16[432,512]{1,0:T(8,128)(2,1)}, bf16[432,512]{1,0:T(8,128)(2,1)}, u32[]{:S(2)}, u32[]{:S(2)}) collective-permute-start(bf16[432,512]{1,0:T(8,128)(2,1)} %get-tuple-element.98), channel_id=1, source_target_pairs={{0,3},{1,2},{2,1},{3,0},{4,7},{5,6},{6,5},{7,4},{8,11},{9,10},{10,... | collective-permute-start | bytes 1327112 | tf_op jit(solution)/shard_map/ppermute | solution.py:52
  92.9 18.2 %collective-permute-start.13 = (bf16[432,512]{1,0:T(8,128)(2,1)}, bf16[432,512]{1,0:T(8,128)(2,1)}, u32[]{:S(2)}, u32[]{:S(2)}) collective-permute-start(bf16[432,512]{1,0:T(8,128)(2,1)} %get-tuple-element.135), channel_id=1, source_target_pairs={{0,1},{1,0},{2,3},{3,2},{4,5},{5,4},{6,7},{7,6},{8,9},{9,8},{10,11... | collective-permute-start | bytes 1327112 | tf_op jit(solution)/shard_map/ppermute | solution.py:52
  111.1 22.4 %collective-permute-start.17 = (bf16[432,512]{1,0:T(8,128)(2,1)}, bf16[432,512]{1,0:T(8,128)(2,1)S(1)}, u32[]{:S(2)}, u32[]{:S(2)}) collective-permute-start(bf16[432,512]{1,0:T(8,128)(2,1)} %get-tuple-element.98), channel_id=1, source_target_pairs={{0,1},{1,0},{2,3},{3,2},{4,5},{5,4},{6,7},{7,6},{8,9},{9,8},{10,11... | collective-permute-start | bytes 1327112 | tf_op jit(solution)/shard_map/ppermute | solution.py:52
  112.8 20.8 %collective-permute-start.18 = (bf16[432,512]{1,0:T(8,128)(2,1)S(1)}, bf16[432,512]{1,0:T(8,128)(2,1)S(1)}, u32[]{:S(2)}, u32[]{:S(2)}) collective-permute-start(bf16[432,512]{1,0:T(8,128)(2,1)S(1)} %bitcast.249), channel_id=1, source_target_pairs={{0,2},{1,3},{2,0},{3,1},{4,6},{5,7},{6,4},{7,5},{8,10},{9,11},{10,... | collective-permute-start | bytes 1327112 | tf_op jit(solution)/shard_map/ppermute | solution.py:52
  113.3 20.1 %collective-permute-start.19 = (bf16[64,160]{1,0:T(8,128)(2,1)S(1)}, bf16[64,160]{1,0:T(8,128)(2,1)S(1)}, u32[]{:S(2)}, u32[]{:S(2)}) collective-permute-start(bf16[64,160]{1,0:T(8,128)(2,1)S(1)} %bitcast.260), channel_id=1, source_target_pairs={{0,1},{1,0},{2,3},{3,2},{4,5},{5,4},{6,7},{7,6},{8,9},{9,8},{10,11... | collective-permute-start | bytes 61448 | tf_op jit(solution)/shard_map/ppermute | solution.py:52
  133.6 7.5 %collective-permute-start.20 = (bf16[864,1024]{1,0:T(8,128)(2,1)}, bf16[864,1024]{1,0:T(8,128)(2,1)S(1)}, u32[]{:S(2)}, u32[]{:S(2)}) collective-permute-start(bf16[864,1024]{1,0:T(8,128)(2,1)} %get-tuple-element.101), channel_id=1, source_target_pairs={{0,4},{1,5},{2,6},{3,7},{4,0},{5,1},{6,2},{7,3},{8,12},{9,13},{10,... | collective-permute-start | bytes 5308424 | tf_op jit(solution)/shard_map/ppermute | solution.py:52
  133.6 6.8 %collective-permute-start.21 = (bf16[2,64,160]{2,1,0:T(8,128)(2,1)S(1)}, bf16[2,64,160]{2,1,0:T(8,128)(2,1)S(1)}, u32[]{:S(2)}, u32[]{:S(2)}) collective-permute-start(bf16[2,64,160]{2,1,0:T(8,128)(2,1)S(1)} %pad_maximum_fusion.11), channel_id=1, source_target_pairs={{0,2},{1,3},{2,0},{3,1},{4,6},{5,7},{6,4},{7,5},{8,10},{9,11},{10,... | collective-permute-start | bytes 122888 | tf_op jit(solution)/shard_map/ppermute | solution.py:52
  144.7 26.3 %collective-permute-start.22 = (bf16[432,1024]{1,0:T(8,128)(2,1)}, bf16[432,1024]{1,0:T(8,128)(2,1)S(1)}, u32[]{:S(2)}, u32[]{:S(2)}) collective-permute-start(bf16[432,1024]{1,0:T(8,128)(2,1)} %get-tuple-element.171), channel_id=1, source_target_pairs={{0,1},{1,0},{2,3},{3,2},{4,5},{5,4},{6,7},{7,6},{8,9},{9,8},{10,11... | collective-permute-start | bytes 2654216 | tf_op jit(solution)/shard_map/ppermute | solution.py:52
  145.1 5.3 %collective-permute-start.23 = (bf16[2,2,64,160]{3,2,1,0:T(8,128)(2,1)}, bf16[2,2,64,160]{3,2,1,0:T(8,128)(2,1)S(1)}, u32[]{:S(2)}, u32[]{:S(2)}) collective-permute-start(bf16[2,2,64,160]{3,2,1,0:T(8,128)(2,1)} %pad_maximum_fusion.10), channel_id=1, source_target_pairs={{0,4},{1,5},{2,6},{3,7},{4,0},{5,1},{6,2},{7,3},{8,12},{9,13},{10,... | collective-permute-start | bytes 245768 | tf_op jit(solution)/shard_map/ppermute | solution.py:52
  146.9 22.4 %collective-permute-start.27 = (bf16[432,256]{1,0:T(8,128)(2,1)}, bf16[432,256]{1,0:T(8,128)(2,1)S(1)}, u32[]{:S(2)}, u32[]{:S(2)}) collective-permute-start(bf16[432,256]{1,0:T(8,128)(2,1)} %bitcast.257), channel_id=1, source_target_pairs={{0,6},{1,7},{2,4},{3,5},{4,2},{5,3},{6,0},{7,1},{8,14},{9,15},{10,... | collective-permute-start | bytes 663560 | tf_op jit(solution)/shard_map/ppermute | solution.py:52
  151.4 19.6 %collective-permute-start.26 = (bf16[2,2,2,64,160]{4,3,2,1,0:T(8,128)(2,1)S(1)}, bf16[2,2,2,64,160]{4,3,2,1,0:T(8,128)(2,1)S(1)}, u32[]{:S(2)}, u32[]{:S(2)}) collective-permute-start(bf16[2,2,2,64,160]{4,3,2,1,0:T(8,128)(2,1)S(1)} %pad_maximum_fusion.9), channel_id=1, source_target_pairs={{0,24},{1,25},{2,26},{3,27},{4,28},{5,29},{6,30},{7,31},{8,16},{9,... | collective-permute-start | bytes 491528 | tf_op jit(solution)/shard_map/ppermute | solution.py:52
  152.9 18.0 %collective-permute-start.25 = (bf16[2,2,2,64,160]{4,3,2,1,0:T(8,128)(2,1)S(1)}, bf16[2,2,2,64,160]{4,3,2,1,0:T(8,128)(2,1)S(1)}, u32[]{:S(2)}, u32[]{:S(2)}) collective-permute-start(bf16[2,2,2,64,160]{4,3,2,1,0:T(8,128)(2,1)S(1)} %pad_maximum_fusion.9), channel_id=1, source_target_pairs={{0,16},{1,17},{2,18},{3,19},{4,20},{5,21},{6,22},{7,23},{8,24},{9,... | collective-permute-start | bytes 491528 | tf_op jit(solution)/shard_map/ppermute | solution.py:52
  154.3 16.7 %collective-permute-start.24 = (bf16[2,2,2,64,160]{4,3,2,1,0:T(8,128)(2,1)S(1)}, bf16[2,2,2,64,160]{4,3,2,1,0:T(8,128)(2,1)S(1)}, u32[]{:S(2)}, u32[]{:S(2)}) collective-permute-start(bf16[2,2,2,64,160]{4,3,2,1,0:T(8,128)(2,1)S(1)} %pad_maximum_fusion.9), channel_id=1, source_target_pairs={{0,8},{1,9},{2,10},{3,11},{4,12},{5,13},{6,14},{7,15},{8,0},{9,1},... | collective-permute-start | bytes 491528 | tf_op jit(solution)/shard_map/ppermute | solution.py:52
  177.2 3.9 %collective-permute-start.30 = (f32[24,256]{1,0:T(8,128)S(1)}, f32[24,256]{1,0:T(8,128)S(1)}, u32[]{:S(2)}, u32[]{:S(2)}) collective-permute-start(f32[24,256]{1,0:T(8,128)S(1)} %pad_maximum_fusion.12), channel_id=1, source_target_pairs={{0,16},{1,17},{2,18},{3,19},{4,20},{5,21},{6,22},{7,23},{8,24},{9,... | collective-permute-start | bytes 73736 | tf_op jit(solution)/shard_map/ppermute | solution.py:52
  178.7 4.7 %collective-permute-start.31 = (f32[24,256]{1,0:T(8,128)S(1)}, f32[24,256]{1,0:T(8,128)S(1)}, u32[]{:S(2)}, u32[]{:S(2)}) collective-permute-start(f32[24,256]{1,0:T(8,128)S(1)} %pad_maximum_fusion.12), channel_id=1, source_target_pairs={{0,24},{1,25},{2,26},{3,27},{4,28},{5,29},{6,30},{7,31},{8,16},{9,... | collective-permute-start | bytes 73736 | tf_op jit(solution)/shard_map/ppermute | solution.py:52
  184.1 9.5 %collective-permute-start.34 = (f32[24,256]{1,0:T(8,128)S(1)}, f32[24,256]{1,0:T(8,128)S(1)}, u32[]{:S(2)}, u32[]{:S(2)}) collective-permute-start(f32[24,256]{1,0:T(8,128)S(1)} %pad_maximum_fusion.13.refs_0_), channel_id=1, source_target_pairs={{0,3},{1,2},{2,1},{3,0},{4,7},{5,6},{6,5},{7,4},{8,11},{9,10},{10,... | collective-permute-start | bytes 73736 | tf_op jit(solution)/shard_map/ppermute | solution.py:52
  187.7 6.0 %collective-permute-start.33 = (f32[24,256]{1,0:T(8,128)S(1)}, f32[24,256]{1,0:T(8,128)S(1)}, u32[]{:S(2)}, u32[]{:S(2)}) collective-permute-start(f32[24,256]{1,0:T(8,128)S(1)} %pad_maximum_fusion.13.refs_0_), channel_id=1, source_target_pairs={{0,2},{1,3},{2,0},{3,1},{4,6},{5,7},{6,4},{7,5},{8,10},{9,11},{10,... | collective-permute-start | bytes 73736 | tf_op jit(solution)/shard_map/ppermute | solution.py:52
  189.0 4.6 %collective-permute-start.32 = (f32[24,256]{1,0:T(8,128)S(1)}, f32[24,256]{1,0:T(8,128)S(1)}, u32[]{:S(2)}, u32[]{:S(2)}) collective-permute-start(f32[24,256]{1,0:T(8,128)S(1)} %pad_maximum_fusion.13.refs_0_), channel_id=1, source_target_pairs={{0,1},{1,0},{2,3},{3,2},{4,5},{5,4},{6,7},{7,6},{8,9},{9,8},{10,11... | collective-permute-start | bytes 73736 | tf_op jit(solution)/shard_map/ppermute | solution.py:52
  198.2 4.2 %collective-permute-start.37 = (f32[8,256]{1,0:T(8,128)S(1)}, f32[8,256]{1,0:T(8,128)S(1)}, u32[]{:S(2)}, u32[]{:S(2)}) collective-permute-start(f32[8,256]{1,0:T(8,128)S(1)} %pad_maximum_fusion.14), channel_id=1, source_target_pairs={{0,16},{1,17},{2,18},{3,19},{4,20},{5,21},{6,22},{7,23},{8,24},{9,... | collective-permute-start | bytes 24584 | tf_op jit(solution)/shard_map/ppermute | solution.py:52
  199.0 4.6 %collective-permute-start.38 = (f32[8,256]{1,0:T(8,128)S(1)}, f32[8,256]{1,0:T(8,128)S(1)}, u32[]{:S(2)}, u32[]{:S(2)}) collective-permute-start(f32[8,256]{1,0:T(8,128)S(1)} %pad_maximum_fusion.14), channel_id=1, source_target_pairs={{0,24},{1,25},{2,26},{3,27},{4,28},{5,29},{6,30},{7,31},{8,16},{9,... | collective-permute-start | bytes 24584 | tf_op jit(solution)/shard_map/ppermute | solution.py:52
  204.1 4.6 %collective-permute-start.40 = (f32[8,256]{1,0:T(8,128)S(1)}, f32[8,256]{1,0:T(8,128)S(1)}, u32[]{:S(2)}, u32[]{:S(2)}) collective-permute-start(f32[8,256]{1,0:T(8,128)S(1)} %pad_maximum_fusion.15), channel_id=1, source_target_pairs={{0,2},{1,3},{2,0},{3,1},{4,6},{5,7},{6,4},{7,5},{8,10},{9,11},{10,... | collective-permute-start | bytes 24584 | tf_op jit(solution)/shard_map/ppermute | solution.py:52
  205.8 5.4 %collective-permute-start.41 = (f32[8,256]{1,0:T(8,128)S(1)}, f32[8,256]{1,0:T(8,128)S(1)}, u32[]{:S(2)}, u32[]{:S(2)}) collective-permute-start(f32[8,256]{1,0:T(8,128)S(1)} %pad_maximum_fusion.15), channel_id=1, source_target_pairs={{0,3},{1,2},{2,1},{3,0},{4,7},{5,6},{6,5},{7,4},{8,11},{9,10},{10,... | collective-permute-start | bytes 24584 | tf_op jit(solution)/shard_map/ppermute | solution.py:52
  215.1 4.1 %collective-permute-start.44 = (f32[8,256]{1,0:T(8,128)S(1)}, f32[8,256]{1,0:T(8,128)S(1)}, u32[]{:S(2)}, u32[]{:S(2)}) collective-permute-start(f32[8,256]{1,0:T(8,128)S(1)} %fusion.41), channel_id=1, source_target_pairs={{0,16},{1,17},{2,18},{3,19},{4,20},{5,21},{6,22},{7,23},{8,24},{9,... | collective-permute-start | bytes 24584 | tf_op jit(solution)/shard_map/ppermute | solution.py:52
  216.5 4.5 %collective-permute-start.45 = (f32[8,256]{1,0:T(8,128)S(1)}, f32[8,256]{1,0:T(8,128)S(1)}, u32[]{:S(2)}, u32[]{:S(2)}) collective-permute-start(f32[8,256]{1,0:T(8,128)S(1)} %fusion.41), channel_id=1, source_target_pairs={{0,24},{1,25},{2,26},{3,27},{4,28},{5,29},{6,30},{7,31},{8,16},{9,... | collective-permute-start | bytes 24584 | tf_op jit(solution)/shard_map/ppermute | solution.py:52
  218.6 7.5 %collective-permute-start.56 = (bf16[16,512]{1,0:T(8,128)(2,1)S(1)}, bf16[16,512]{1,0:T(8,128)(2,1)S(1)}, u32[]{:S(2)}, u32[]{:S(2)}) collective-permute-start(bf16[16,512]{1,0:T(8,128)(2,1)S(1)} %copy-done.42), channel_id=1, source_target_pairs={{0,2},{1,3},{2,0},{3,1},{4,6},{5,7},{6,4},{7,5},{8,10},{9,11},{10,... | collective-permute-start | bytes 49160 | tf_op jit(solution)/shard_map/ppermute | solution.py:52
  221.6 5.5 %collective-permute-start.48 = (f32[8,256]{1,0:T(8,128)S(1)}, f32[8,256]{1,0:T(8,128)S(1)}, u32[]{:S(2)}, u32[]{:S(2)}) collective-permute-start(f32[8,256]{1,0:T(8,128)S(1)} %add_add_fusion.2.refs_0_), channel_id=1, source_target_pairs={{0,3},{1,2},{2,1},{3,0},{4,7},{5,6},{6,5},{7,4},{8,11},{9,10},{10,... | collective-permute-start | bytes 24584 | tf_op jit(solution)/shard_map/ppermute | solution.py:52
  223.5 4.5 %collective-permute-start.47 = (f32[8,256]{1,0:T(8,128)S(1)}, f32[8,256]{1,0:T(8,128)S(1)}, u32[]{:S(2)}, u32[]{:S(2)}) collective-permute-start(f32[8,256]{1,0:T(8,128)S(1)} %add_add_fusion.2.refs_0_), channel_id=1, source_target_pairs={{0,2},{1,3},{2,0},{3,1},{4,6},{5,7},{6,4},{7,5},{8,10},{9,11},{10,... | collective-permute-start | bytes 24584 | tf_op jit(solution)/shard_map/ppermute | solution.py:52
  223.5 4.5 %collective-permute-start.46 = (f32[8,256]{1,0:T(8,128)S(1)}, f32[8,256]{1,0:T(8,128)S(1)}, u32[]{:S(2)}, u32[]{:S(2)}) collective-permute-start(f32[8,256]{1,0:T(8,128)S(1)} %add_add_fusion.2.refs_0_), channel_id=1, source_target_pairs={{0,1},{1,0},{2,3},{3,2},{4,5},{5,4},{6,7},{7,6},{8,9},{9,8},{10,11... | collective-permute-start | bytes 24584 | tf_op jit(solution)/shard_map/ppermute | solution.py:52
  231.0 4.6 %collective-permute-start.52 = (f32[16,256]{1,0:T(8,128)S(1)}, f32[16,256]{1,0:T(8,128)S(1)}, u32[]{:S(2)}, u32[]{:S(2)}) collective-permute-start(f32[16,256]{1,0:T(8,128)S(1)} %add.282), channel_id=1, source_target_pairs={{0,24},{1,25},{2,26},{3,27},{4,28},{5,29},{6,30},{7,31},{8,16},{9,... | collective-permute-start | bytes 49160 | tf_op jit(solution)/shard_map/ppermute | solution.py:52
  236.9 5.6 %collective-permute-start.55 = (f32[16,256]{1,0:T(8,128)S(1)}, f32[16,256]{1,0:T(8,128)S(1)}, u32[]{:S(2)}, u32[]{:S(2)}) collective-permute-start(f32[16,256]{1,0:T(8,128)S(1)} %add_add_fusion.1.refs_0_), channel_id=1, source_target_pairs={{0,3},{1,2},{2,1},{3,0},{4,7},{5,6},{6,5},{7,4},{8,11},{9,10},{10,... | collective-permute-start | bytes 49160 | tf_op jit(solution)/shard_map/ppermute | solution.py:52
  239.0 4.8 %collective-permute-start.54 = (f32[16,256]{1,0:T(8,128)S(1)}, f32[16,256]{1,0:T(8,128)S(1)}, u32[]{:S(2)}, u32[]{:S(2)}) collective-permute-start(f32[16,256]{1,0:T(8,128)S(1)} %add_add_fusion.1.refs_0_), channel_id=1, source_target_pairs={{0,2},{1,3},{2,0},{3,1},{4,6},{5,7},{6,4},{7,5},{8,10},{9,11},{10,... | collective-permute-start | bytes 49160 | tf_op jit(solution)/shard_map/ppermute | solution.py:52
  246.0 35.3 %collective-permute-start.60 = (bf16[432,1024]{1,0:T(8,128)(2,1)S(1)}, bf16[432,1024]{1,0:T(8,128)(2,1)}, u32[]{:S(2)}, u32[]{:S(2)}) collective-permute-start(bf16[432,1024]{1,0:T(8,128)(2,1)S(1)} %get-tuple-element.121.refs_0_.refs_4_), channel_id=1, source_target_pairs={{0,4},{1,5},{2,6},{3,7},{4,0},{5,1},{6,2},{7,3},{8,12},{9,13},{10,... | collective-permute-start | bytes 2654216 | tf_op jit(solution)/shard_map/ppermute | solution.py:52
  246.1 31.6 %collective-permute-start.57 = (bf16[432,1024]{1,0:T(8,128)(2,1)S(1)}, bf16[432,1024]{1,0:T(8,128)(2,1)}, u32[]{:S(2)}, u32[]{:S(2)}) collective-permute-start(bf16[432,1024]{1,0:T(8,128)(2,1)S(1)} %get-tuple-element.121.refs_0_.refs_4_), channel_id=1, source_target_pairs={{0,1},{1,0},{2,3},{3,2},{4,5},{5,4},{6,7},{7,6},{8,9},{9,8},{10,11... | collective-permute-start | bytes 2654216 | tf_op jit(solution)/shard_map/ppermute | solution.py:52
  249.3 26.9 %collective-permute-start.58 = (bf16[432,512]{1,0:T(8,128)(2,1)S(1)}, bf16[432,512]{1,0:T(8,128)(2,1)}, u32[]{:S(2)}, u32[]{:S(2)}) collective-permute-start(bf16[432,512]{1,0:T(8,128)(2,1)S(1)} %get-tuple-element.122), channel_id=1, source_target_pairs={{0,2},{1,3},{2,0},{3,1},{4,6},{5,7},{6,4},{7,5},{8,10},{9,11},{10,... | collective-permute-start | bytes 1327112 | tf_op jit(solution)/shard_map/ppermute | solution.py:52
  279.6 23.0 %collective-permute-start.65 = (bf16[432,512]{1,0:T(8,128)(2,1)}, bf16[432,512]{1,0:T(8,128)(2,1)S(1)}, u32[]{:S(2)}, u32[]{:S(2)}) collective-permute-start(bf16[432,512]{1,0:T(8,128)(2,1)} %collective-permute-done.58.refs_8_), channel_id=1, source_target_pairs={{0,1},{1,0},{2,3},{3,2},{4,5},{5,4},{6,7},{7,6},{8,9},{9,8},{10,11... | collective-permute-start | bytes 1327112 | tf_op jit(solution)/shard_map/ppermute | solution.py:52
  281.3 22.6 %collective-permute-start.63 = (bf16[2,2,2,64,160]{4,3,2,1,0:T(8,128)(2,1)S(1)}, bf16[2,2,2,64,160]{4,3,2,1,0:T(8,128)(2,1)S(1)}, u32[]{:S(2)}, u32[]{:S(2)}) collective-permute-start(bf16[2,2,2,64,160]{4,3,2,1,0:T(8,128)(2,1)S(1)} %fusion.6), channel_id=1, source_target_pairs={{0,8},{1,9},{2,10},{3,11},{4,12},{5,13},{6,14},{7,15},{8,0},{9,1},... | collective-permute-start | bytes 491528 | tf_op jit(solution)/shard_map/ppermute | solution.py:52
  282.8 20.6 %collective-permute-start.66 = (bf16[432,512]{1,0:T(8,128)(2,1)}, bf16[432,512]{1,0:T(8,128)(2,1)S(1)}, u32[]{:S(2)}, u32[]{:S(2)}) collective-permute-start(bf16[432,512]{1,0:T(8,128)(2,1)} %get-tuple-element.135), channel_id=1, source_target_pairs={{0,3},{1,2},{2,1},{3,0},{4,7},{5,6},{6,5},{7,4},{8,11},{9,10},{10,... | collective-permute-start | bytes 1327112 | tf_op jit(solution)/shard_map/ppermute | solution.py:52
  302.5 25.1 %collective-permute-start.62 = (bf16[432,256]{1,0:T(8,128)(2,1)S(1)}, bf16[432,256]{1,0:T(8,128)(2,1)S(1)}, u32[]{:S(2)}, u32[]{:S(2)}) collective-permute-start(bf16[432,256]{1,0:T(8,128)(2,1)S(1)} %copy-done.30), channel_id=1, source_target_pairs={{0,6},{1,7},{2,4},{3,5},{4,2},{5,3},{6,0},{7,1},{8,14},{9,15},{10,... | collective-permute-start | bytes 663560 | tf_op jit(solution)/shard_map/ppermute | solution.py:52
  304.1 25.0 %collective-permute-start.64 = (bf16[1,2,2,64,160]{4,3,2,1,0:T(8,128)(2,1)S(1)}, bf16[1,2,2,64,160]{4,3,2,1,0:T(8,128)(2,1)S(1)}, u32[]{:S(2)}, u32[]{:S(2)}) collective-permute-start(bf16[1,2,2,64,160]{4,3,2,1,0:T(8,128)(2,1)S(1)} %select_bitcast_fusion.8), channel_id=1, source_target_pairs={{0,16},{1,17},{2,18},{3,19},{4,20},{5,21},{6,22},{7,23},{8,24},{9,... | collective-permute-start | bytes 245768 | tf_op jit(solution)/shard_map/ppermute | solution.py:52
  306.0 28.3 %collective-permute-start.69 = (bf16[432,512]{1,0:T(8,128)(2,1)}, bf16[432,512]{1,0:T(8,128)(2,1)}, u32[]{:S(2)}, u32[]{:S(2)}) collective-permute-start(bf16[432,512]{1,0:T(8,128)(2,1)} %get-tuple-element.138), channel_id=1, source_target_pairs={{0,2},{1,3},{2,0},{3,1},{4,6},{5,7},{6,4},{7,5},{8,10},{9,11},{10,... | collective-permute-start | bytes 1327112 | tf_op jit(solution)/shard_map/ppermute | solution.py:52
  307.9 26.4 %collective-permute-start.70 = (bf16[432,512]{1,0:T(8,128)(2,1)}, bf16[432,512]{1,0:T(8,128)(2,1)S(1)}, u32[]{:S(2)}, u32[]{:S(2)}) collective-permute-start(bf16[432,512]{1,0:T(8,128)(2,1)} %get-tuple-element.139), channel_id=1, source_target_pairs={{0,1},{1,0},{2,3},{3,2},{4,5},{5,4},{6,7},{7,6},{8,9},{9,8},{10,11... | collective-permute-start | bytes 1327112 | tf_op jit(solution)/shard_map/ppermute | solution.py:52
  326.2 12.6 %collective-permute-start.74 = (bf16[29,64,128]{2,1,0:T(8,128)(2,1)}, bf16[29,64,128]{2,1,0:T(8,128)(2,1)S(1)}, u32[]{:S(2)}, u32[]{:S(2)}) collective-permute-start(bf16[29,64,128]{2,1,0:T(8,128)(2,1)} %get-tuple-element.144), channel_id=1, source_target_pairs={{0,16},{1,17},{2,18},{3,19},{4,20},{5,21},{6,22},{7,23},{8,24},{9,... | collective-permute-start | bytes 1425416 | tf_op jit(solution)/shard_map/ppermute | solution.py:52
  327.7 12.2 %collective-permute-start.75 = (bf16[29,64,128]{2,1,0:T(8,128)(2,1)}, bf16[29,64,128]{2,1,0:T(8,128)(2,1)S(1)}, u32[]{:S(2)}, u32[]{:S(2)}) collective-permute-start(bf16[29,64,128]{2,1,0:T(8,128)(2,1)} %get-tuple-element.145), channel_id=1, source_target_pairs={{0,8},{1,9},{2,10},{3,11},{4,12},{5,13},{6,14},{7,15},{8,0},{9,1},... | collective-permute-start | bytes 1425416 | tf_op jit(solution)/shard_map/ppermute | solution.py:52
  334.3 14.6 %collective-permute-start.78 = (bf16[2,64,160]{2,1,0:T(8,128)(2,1)S(1)}, bf16[2,64,160]{2,1,0:T(8,128)(2,1)S(1)}, u32[]{:S(2)}, u32[]{:S(2)}) collective-permute-start(bf16[2,64,160]{2,1,0:T(8,128)(2,1)S(1)} %select_bitcast_fusion.11), channel_id=1, source_target_pairs={{0,2},{1,3},{2,0},{3,1},{4,6},{5,7},{6,4},{7,5},{8,10},{9,11},{10,... | collective-permute-start | bytes 122888 | tf_op jit(solution)/shard_map/ppermute | solution.py:52
  334.4 24.7 %collective-permute-start.71 = (bf16[432,512]{1,0:T(8,128)(2,1)}, bf16[432,512]{1,0:T(8,128)(2,1)S(1)}, u32[]{:S(2)}, u32[]{:S(2)}) collective-permute-start(bf16[432,512]{1,0:T(8,128)(2,1)} %get-tuple-element.140), channel_id=1, source_target_pairs={{0,2},{1,3},{2,0},{3,1},{4,6},{5,7},{6,4},{7,5},{8,10},{9,11},{10,... | collective-permute-start | bytes 1327112 | tf_op jit(solution)/shard_map/ppermute | solution.py:52
  337.3 21.9 %collective-permute-start.72 = (bf16[432,512]{1,0:T(8,128)(2,1)}, bf16[432,512]{1,0:T(8,128)(2,1)S(1)}, u32[]{:S(2)}, u32[]{:S(2)}) collective-permute-start(bf16[432,512]{1,0:T(8,128)(2,1)} %collective-permute-done.69), channel_id=1, source_target_pairs={{0,1},{1,0},{2,3},{3,2},{4,5},{5,4},{6,7},{7,6},{8,9},{9,8},{10,11... | collective-permute-start | bytes 1327112 | tf_op jit(solution)/shard_map/ppermute | solution.py:52
  341.2 21.3 %collective-permute-start.77 = (bf16[2,29,64,128]{3,2,1,0:T(8,128)(2,1)S(1)}, bf16[2,29,64,128]{3,2,1,0:T(8,128)(2,1)S(1)}, u32[]{:S(2)}, u32[]{:S(2)}) collective-permute-start(bf16[2,29,64,128]{3,2,1,0:T(8,128)(2,1)S(1)} %pad_maximum_fusion.2), channel_id=1, source_target_pairs={{0,16},{1,17},{2,18},{3,19},{4,20},{5,21},{6,22},{7,23},{8,24},{9,... | collective-permute-start | bytes 2850824 | tf_op jit(solution)/shard_map/ppermute | solution.py:52
  342.2 21.3 %collective-permute-start.76 = (bf16[2,29,64,128]{3,2,1,0:T(8,128)(2,1)S(1)}, bf16[2,29,64,128]{3,2,1,0:T(8,128)(2,1)S(1)}, u32[]{:S(2)}, u32[]{:S(2)}) collective-permute-start(bf16[2,29,64,128]{3,2,1,0:T(8,128)(2,1)S(1)} %pad_maximum_fusion.1), channel_id=1, source_target_pairs={{0,8},{1,9},{2,10},{3,11},{4,12},{5,13},{6,14},{7,15},{8,0},{9,1},... | collective-permute-start | bytes 2850824 | tf_op jit(solution)/shard_map/ppermute | solution.py:52
  359.5 6.1 %collective-permute-start.73 = (bf16[2,432,512]{2,1,0:T(8,128)(2,1)S(1)}, bf16[2,432,512]{2,1,0:T(8,128)(2,1)S(1)}, u32[]{:S(2)}, u32[]{:S(2)}) collective-permute-start(bf16[2,432,512]{2,1,0:T(8,128)(2,1)S(1)} %pad_maximum_fusion.4), channel_id=1, source_target_pairs={{0,4},{1,5},{2,6},{3,7},{4,0},{5,1},{6,2},{7,3},{8,12},{9,13},{10,... | collective-permute-start | bytes 2654216 | tf_op jit(solution)/shard_map/ppermute | solution.py:52
  364.2 11.6 %collective-permute-start.79 = (bf16[29,64,128]{2,1,0:T(8,128)(2,1)S(1)}, bf16[29,64,128]{2,1,0:T(8,128)(2,1)S(1)}, u32[]{:S(2)}, u32[]{:S(2)}) collective-permute-start(bf16[29,64,128]{2,1,0:T(8,128)(2,1)S(1)} %broadcast_select_fusion.7), channel_id=1, source_target_pairs={{0,1},{1,0},{2,3},{3,2},{4,5},{5,4},{6,7},{7,6},{8,9},{9,8},{10,11... | collective-permute-start | bytes 1425416 | tf_op jit(solution)/shard_map/ppermute | solution.py:52
  367.9 7.2 %collective-permute-start.81 = (bf16[1,64,160]{2,1,0:T(8,128)(2,1)S(1)}, bf16[1,64,160]{2,1,0:T(8,128)(2,1)S(1)}, u32[]{:S(2)}, u32[]{:S(2)}) collective-permute-start(bf16[1,64,160]{2,1,0:T(8,128)(2,1)S(1)} %select_bitcast_fusion.14), channel_id=1, source_target_pairs={{0,1},{1,0},{2,3},{3,2},{4,5},{5,4},{6,7},{7,6},{8,9},{9,8},{10,11... | collective-permute-start | bytes 61448 | tf_op jit(solution)/shard_map/ppermute | solution.py:52
  (75 other events, 414.9 us)

commit v3 on v2

--- a/solution.py
+++ b/solution.py
@@ -12,7 +12,7 @@
 AXES = ("dp", "rows")
 FULL, SHORT, PER_CHIP = 14, 13, 27
 SLOTS = FULL + 2 + SHORT
-FIRST = 14
+FIRST = 16
 CUT = 15
 NT = (((1,), (1,)), ((), ()))
 TN = (((0,), (0,)), ((), ()))
@@ -941,20 +941,21 @@
     keep, given, pooled, lifted = branch_sums(shape, info, areas, bands, weights)
     far_bands = [sent(1, k, first=ready) for k in range(nzl + 1)]
     projection = after(projection, ready)
+    projection = joined(place, projection, steps[-nd_bits - 2])
+    given = after(given, far_bands, projection)
+    projection = after(projection, given)
     for step in steps[: -nd_bits - 2]:
         projection = joined(place, projection, step)
-    given = after(given, far_bands, projection)
-    projection = joined(place, after(projection, given), steps[-nd_bits - 2])
     got, projection = after((place.swap(given, c=1), projection), projection)
     projection = joined(place, projection, steps[-nd_bits - 1])
     upstream_low = to_logical(place, after(cotangent.reshape(band, out), got))
     plane = [projection] + [place.swap(projection, m=k) for k in range(1, images // 2)]
     mine, others = given_on(keep, got)
-    mine, others = after((mine, others), plane, upstream_low)
+    projection = jnp.stack(by_xor(plane, place.m))
+    projection = projection.reshape((images // 2, 2, nzl, 2) + projection_weight.shape[::-1])
+    projection = jnp.transpose(projection, (3, 2, 4, 0, 1, 5)).reshape(out, -1)
+    mine, others = after((mine, others), projection, upstream_low)
     z, rows = branch_moments(shape, info, images, mine, others, lifted)
-    projection = jnp.stack(by_xor(plane, place.m))
-    projection = projection.reshape((place.nd, nr) + projection_weight.shape[::-1])
-    projection = jnp.transpose(projection, (1, 2, 0, 3)).reshape(out, -1)
     rows = exchanged(place, rows, lambda xs: merged(xs, 4))
     concat, proj_pre, rows, stats = projected(shape, info, images, rows, z, projection, norm_gain, norm_bias)
     pooled_far = place.swap(pooled, zh=1)

time: 384 us -> 381 us (level)
  local copies, waits for them, and re-layouts: 28.2 us -> 32.2 us
    unnamed x114 -> x110, local copies, waits for them, and re-layouts: 14.6 us -> 17.1 us
  transfers between devices with their start and end apart: 82 -> 82, of which waited for: 46 -> 48; matrix products, arithmetic and copies ran while one was open for 9% -> 10% of each run, Pallas kernels for 17% -> 17%
where the time goes in v3:
time: 381 us; the launch traced here: 377 us
  waiting for transfers between devices  152 us (40%)
  starting transfers between devices  90.9 us (24%)
  Pallas kernels  71.9 us (19%)
  local copies, waits for them, and re-layouts  32.2 us (8%)
  other arithmetic  26.3 us (7%)
    ppermute x82, waiting for transfers between devices, swap(): return lax.ppermute(x, AXES, pairs)  152 us
    ppermute x82, starting transfers between devices, swap(): return lax.ppermute(x, AXES, pairs)  90.9 us
    pallas_call x1, Pallas kernels, branch_sums(): pl.pallas_call(kernel, out_shape=half_shapes(shape, 4) + [jax.ShapeDtypeS...  18.4 us
    pallas_call x1, Pallas kernels, input_gradient(): pl.pallas_call(kernel, out_shape=[jax.ShapeDtypeStruct((shape.band, shape...  18 us
    pallas_call x1, Pallas kernels, weight_gradients(): pl.pallas_call(kernel, out_shape=out_shape, in_specs=[SMEM] + [ANY] * (4...  17.5 us
    unnamed x110, local copies, waits for them, and re-layouts  17.1 us
  transfers between devices with their start and end apart: 82, of which 48 were waited for; matrix products, arithmetic and copies ran while one was open for 10% of the time, Pallas kernels for 17%

profile of v3, /device:TPU:0, one launch (start us, length us, event | category | flops | bytes accessed | tf_op | source)
XLA Modules:
  0.0 377.1 jit_solution(7530409354162248581)
XLA Ops:
  5.0 2.9 collective-permute-start.4
  9.3 2.6 collective-permute-start.3
  14.1 1.5 collective-permute-done
  15.7 8.6 %collective-permute-done.3.first = bf16[16,64,128]{2,1,0:T(8,128)(2,1)S(1)} collective-permute-done((bf16[16,64,128]{2,1,0:T(8,128)(2,1)}, bf16[16,64,128]{2,1,0:T(8,128)(2,1)S(1)}, u32[]{:S(2)}, u32[]{:S(2)}) %collective-permute-start.3) | collective-permute-done | bytes 262176 | tf_op jit(solution)/shard_map/ppermute | solution.py:52
  26.0 1.6 collective-permute-start.8
  27.6 1.5 collective-permute-start.6
  29.1 3.2 collective-permute-start.5
  32.3 1.6 broadcast_select_fusion.2
  33.9 14.6 %collective-permute-done.8.refs_2_ = bf16[29,128,128]{2,1,0:T(8,128)(2,1)S(1)} collective-permute-done((bf16[29,128,128]{2,1,0:T(8,128)(2,1)S(1)}, bf16[29,128,128]{2,1,0:T(8,128)(2,1)S(1)}, u32[]{:S(2)}, u32[]{:S(2)}) %collective-permute-start.8) | collective-permute-done | bytes 950304 | tf_op jit(solution)/shard_map/ppermute | solution.py:52
  50.0 1.6 collective-permute-start.7
  53.4 8.1 %collective-permute-done.5.rest = bf16[42,64,128]{2,1,0:T(8,128)(2,1)S(1)} collective-permute-done((bf16[42,64,128]{2,1,0:T(8,128)(2,1)}, bf16[42,64,128]{2,1,0:T(8,128)(2,1)S(1)}, u32[]{:S(2)}, u32[]{:S(2)}) %collective-permute-start.5) | collective-permute-done | bytes 688160 | tf_op jit(solution)/shard_map/ppermute | solution.py:52
  63.5 3.2 collective-permute-start.12
  66.7 16.4 %collective-permute-done.12.refs_2_ = bf16[432,512]{1,0:T(8,128)(2,1)S(1)} collective-permute-done((bf16[432,512]{1,0:T(8,128)(2,1)S(1)}, bf16[432,512]{1,0:T(8,128)(2,1)S(1)}, u32[]{:S(2)}, u32[]{:S(2)}) %collective-permute-start.12) | collective-permute-done | bytes 442400 | tf_op jit(solution)/shard_map/ppermute | solution.py:52
  84.1 1.5 collective-permute-start.15
  87.6 3.6 collective-permute-start.14
  96.6 3.4 assembled_weights.2.refs_4_.refs_5_
  100.0 1.9 copy-done.2
  101.9 3.9 %assembled_weights.3.refs_5_.refs_6_ = bf16[29,128,512]{2,1,0:T(8,128)(2,1)S(1)} custom-call(s32[8]{0:T(128)S(1)} %stack.122.info, bf16[29,128,128]{2,1,0:T(8,128)(2,1)S(1)} %packed_far.1.refs_0_, bf16[29,128,128]{2,1,0:T(8,128)(2,1)S(1)} %collective-permute-done.10.refs_1_, bf16[29,128,128]{2,1,0:T(8,128)(2,1)S(1)} %copy-done.9, ...), custom_call_target="tpu_custom_call" | custom-call | tf_op jit(solution)/shard_map/assembled_weights/pallas_call | solution.py:378
  105.8 1.9 copy-done.3
  107.7 2.4 collective-permute-done.13.refs_1_
  110.1 1.7 collective-permute-start.17
  112.3 2.4 collective-permute-start.19
  116.0 18.4 %branch_sums.1 = (f32[864,1024]{1,0:T(8,128)}, bf16[864,1024]{1,0:T(8,128)(2,1)}, bf16[16,512]{1,0:T(8,128)(2,1)}, f32[16,256]{1,0:T(8,128)}) custom-call(s32[8]{0:T(128)} %copy-done.25, f32[1]{0:T(128)} %bitcast.11.area, bf16[432,512]{1,0:T(8,128)(2,1)} %bitcast.241, bf16[432,512]{1,0:T(8,128)(2,1)} %collective-permute-done.13.refs_1_, ...), custom_call_target="tpu_custom_call" | custom-call | tf_op jit(solution)/shard_map/branch_sums/pallas_call | solution.py:481
  135.1 4.1 %collective-permute-done.21 = bf16[2,64,160]{2,1,0:T(8,128)(2,1)S(1)} collective-permute-done((bf16[2,64,160]{2,1,0:T(8,128)(2,1)S(1)}, bf16[2,64,160]{2,1,0:T(8,128)(2,1)S(1)}, u32[]{:S(2)}, u32[]{:S(2)}) %collective-permute-start.21) | collective-permute-done | bytes 40992 | tf_op jit(solution)/shard_map/ppermute | solution.py:52
  139.9 3.5 fusion.2
  148.2 4.6 %collective-permute-done.27 = bf16[432,256]{1,0:T(8,128)(2,1)S(1)} collective-permute-done((bf16[432,256]{1,0:T(8,128)(2,1)}, bf16[432,256]{1,0:T(8,128)(2,1)S(1)}, u32[]{:S(2)}, u32[]{:S(2)}) %collective-permute-start.27) | collective-permute-done | bytes 221216 | tf_op jit(solution)/shard_map/ppermute | solution.py:52
  152.8 1.6 broadcast_select_fusion.24
  154.4 3.2 collective-permute-done.25
  157.6 1.6 collective-permute-done.24
  159.6 2.0 copy.22
  161.7 4.8 %reshape.325.projection = bf16[256,1280]{1,0:T(8,128)(2,1)} reshape(bf16[2,2,64,4,2,160]{5,4,3,2,1,0:T(2,128)(2,1)} %copy.22) | data formatting | bytes 1310720 | tf_op jit(solution)/shard_map/reshape | solution.py:956
  166.5 3.4 collective-permute-done.22.refs_0_
  176.1 1.6 collective-permute-start.30
  180.0 2.4 collective-permute-done.31
  182.6 1.9 collective-permute-start.34
  184.5 2.6 collective-permute-start.32
  190.9 1.6 projected.1
  201.7 2.1 collective-permute-start.40
  203.8 2.0 collective-permute-start.41
  206.4 2.9 collective-permute-done.41
  212.3 1.5 collective-permute-start.44
  216.2 2.2 collective-permute-done.45
  218.6 1.9 collective-permute-start.48
  220.4 2.5 collective-permute-start.46
  225.0 1.8 branch_gradients.1
  228.1 1.9 collective-permute-start.52
  234.2 2.0 collective-permute-start.55
  241.1 2.0 branch_deltas.1
  249.9 23.7 %collective-permute-done.58.refs_8_ = bf16[432,512]{1,0:T(8,128)(2,1)} collective-permute-done((bf16[432,512]{1,0:T(8,128)(2,1)S(1)}, bf16[432,512]{1,0:T(8,128)(2,1)}, u32[]{:S(2)}, u32[]{:S(2)}) %collective-permute-start.58) | collective-permute-done | bytes 442400 | tf_op jit(solution)/shard_map/ppermute | solution.py:52
  276.7 1.8 collective-permute-start.65
  279.7 1.9 collective-permute-start.66
  281.6 18.0 %input_gradient.1 = (bf16[432,512]{1,0:T(8,128)(2,1)}, bf16[432,512]{1,0:T(8,128)(2,1)}, bf16[432,512]{1,0:T(8,128)(2,1)}, bf16[432,512]{1,0:T(8,128)(2,1)}) custom-call(s32[8]{0:T(128)} %copy-done.25, f32[1]{0:T(128)} %bitcast.11.area, bf16[432,1024]{1,0:T(8,128)(2,1)} %copy-done.30, bf16[432,1024]{1,0:T(8,128)(2,1)} %collective-permute-done.57.refs_1_.refs_5_, ...), custom_call_target="tpu_custom_call" | custom-call | flops 9965666304 | bytes 16777216 | tf_op jit(solution)/shard_map/input_gradient/pallas_call | solution.py:736
  301.4 1.6 collective-permute-start.64
  303.4 1.6 collective-permute-start.69
  305.9 17.5 %weight_gradients.1 = (bf16[29,64,128]{2,1,0:T(8,128)(2,1)}, bf16[29,64,128]{2,1,0:T(8,128)(2,1)}, bf16[29,64,128]{2,1,0:T(8,128)(2,1)}, bf16[29,64,128]{2,1,0:T...) custom-call(s32[8]{0:T(128)} %copy-done.25, ...), custom_call_target="tpu_custom_call" | custom-call | flops 9965666304 | bytes 16777216 | tf_op jit(solution)/shard_map/weight_gradients/pallas_call | solution.py:848
  323.5 1.6 collective-permute-start.74
  326.4 4.9 %collective-permute-done.69 = bf16[432,512]{1,0:T(8,128)(2,1)} collective-permute-done((bf16[432,512]{1,0:T(8,128)(2,1)}, bf16[432,512]{1,0:T(8,128)(2,1)}, u32[]{:S(2)}, u32[]{:S(2)}) %collective-permute-start.69) | collective-permute-done | bytes 442400 | tf_op jit(solution)/shard_map/ppermute | solution.py:52
  331.4 2.9 collective-permute-start.71
  334.3 1.7 collective-permute-done.74
  340.6 5.4 %collective-permute-done.78 = bf16[2,64,160]{2,1,0:T(8,128)(2,1)S(1)} collective-permute-done((bf16[2,64,160]{2,1,0:T(8,128)(2,1)S(1)}, bf16[2,64,160]{2,1,0:T(8,128)(2,1)S(1)}, u32[]{:S(2)}, u32[]{:S(2)}) %collective-permute-start.78) | collective-permute-done | bytes 40992 | tf_op jit(solution)/shard_map/ppermute | solution.py:52
  346.0 10.1 %collective-permute-done.71 = bf16[432,512]{1,0:T(8,128)(2,1)S(1)} collective-permute-done((bf16[432,512]{1,0:T(8,128)(2,1)}, bf16[432,512]{1,0:T(8,128)(2,1)S(1)}, u32[]{:S(2)}, u32[]{:S(2)}) %collective-permute-start.71) | collective-permute-done | bytes 442400 | tf_op jit(solution)/shard_map/ppermute | solution.py:52
  356.6 3.3 collective-permute-done.77
  362.7 2.3 join_features.1
  366.7 5.8 %collective-permute-done.81 = bf16[1,64,160]{2,1,0:T(8,128)(2,1)S(1)} collective-permute-done((bf16[1,64,160]{2,1,0:T(8,128)(2,1)S(1)}, bf16[1,64,160]{2,1,0:T(8,128)(2,1)S(1)}, u32[]{:S(2)}, u32[]{:S(2)}) %collective-permute-start.81) | collective-permute-done | bytes 20512 | tf_op jit(solution)/shard_map/ppermute | solution.py:52
  (358 shorter events, 99.2 us)
Async XLA Ops:
  5.0 20.0 %collective-permute-start.4 = (bf16[29,64,128]{2,1,0:T(8,128)(2,1)}, bf16[29,64,128]{2,1,0:T(8,128)(2,1)S(1)}, u32[]{:S(2)}, u32[]{:S(2)}) collective-permute-start(bf16[29,64,128]{2,1,0:T(8,128)(2,1)} %get-tuple-element.183), channel_id=1, source_target_pairs={{0,1},{1,0},{2,3},{3,2},{4,5},{5,4},{6,7},{7,6},{8,9},{9,8},{10,11... | collective-permute-start | bytes 1425416 | tf_op jit(solution)/shard_map/ppermute | solution.py:52
  9.3 15.0 %collective-permute-start.3 = (bf16[16,64,128]{2,1,0:T(8,128)(2,1)}, bf16[16,64,128]{2,1,0:T(8,128)(2,1)S(1)}, u32[]{:S(2)}, u32[]{:S(2)}) collective-permute-start(bf16[16,64,128]{2,1,0:T(8,128)(2,1)} %slice.502), channel_id=1, source_target_pairs={{0,2},{1,3},{2,0},{3,1},{4,6},{5,7},{6,4},{7,5},{8,10},{9,11},{10,... | collective-permute-start | bytes 786440 | tf_op jit(solution)/shard_map/ppermute | solution.py:52
  13.6 18.7 %collective-permute-start.1 = (bf16[2,432,512]{2,1,0:T(8,128)(2,1)}, bf16[2,432,512]{2,1,0:T(8,128)(2,1)}, u32[]{:S(2)}, u32[]{:S(2)}) collective-permute-start(bf16[2,432,512]{2,1,0:T(8,128)(2,1)} %get-tuple-element.84), channel_id=1, source_target_pairs={{0,4},{1,5},{2,6},{3,7},{4,0},{5,1},{6,2},{7,3},{8,12},{9,13},{10,... | collective-permute-start | bytes 2654216 | tf_op jit(solution)/shard_map/ppermute | solution.py:52
  26.0 22.5 %collective-permute-start.8 = (bf16[29,128,128]{2,1,0:T(8,128)(2,1)S(1)}, bf16[29,128,128]{2,1,0:T(8,128)(2,1)S(1)}, u32[]{:S(2)}, u32[]{:S(2)}) collective-permute-start(bf16[29,128,128]{2,1,0:T(8,128)(2,1)S(1)} %get-tuple-element.87.refs_0_), channel_id=1, source_target_pairs={{0,16},{1,17},{2,18},{3,19},{4,20},{5,21},{6,22},{7,23},{8,24},{9,... | collective-permute-start | bytes 2850824 | tf_op jit(solution)/shard_map/ppermute | solution.py:52
  27.6 22.3 %collective-permute-start.6 = (bf16[29,128,128]{2,1,0:T(8,128)(2,1)S(1)}, bf16[29,128,128]{2,1,0:T(8,128)(2,1)S(1)}, u32[]{:S(2)}, u32[]{:S(2)}) collective-permute-start(bf16[29,128,128]{2,1,0:T(8,128)(2,1)S(1)} %get-tuple-element.87.refs_0_), channel_id=1, source_target_pairs={{0,8},{1,9},{2,10},{3,11},{4,12},{5,13},{6,14},{7,15},{8,0},{9,1},... | collective-permute-start | bytes 2850824 | tf_op jit(solution)/shard_map/ppermute | solution.py:52
  29.1 32.5 %collective-permute-start.5 = (bf16[42,64,128]{2,1,0:T(8,128)(2,1)}, bf16[42,64,128]{2,1,0:T(8,128)(2,1)S(1)}, u32[]{:S(2)}, u32[]{:S(2)}) collective-permute-start(bf16[42,64,128]{2,1,0:T(8,128)(2,1)} %copy-done.31), channel_id=1, source_target_pairs={{0,2},{1,3},{2,0},{3,1},{4,6},{5,7},{6,4},{7,5},{8,10},{9,11},{10,... | collective-permute-start | bytes 2064392 | tf_op jit(solution)/shard_map/ppermute | solution.py:52
  48.5 13.1 %collective-permute-start.9 = (bf16[14,128,128]{2,1,0:T(8,128)(2,1)S(1)}, bf16[14,128,128]{2,1,0:T(8,128)(2,1)S(1)}, u32[]{:S(2)}, u32[]{:S(2)}) collective-permute-start(bf16[14,128,128]{2,1,0:T(8,128)(2,1)S(1)} %slice.504), channel_id=1, source_target_pairs={{0,8},{1,9},{2,10},{3,11},{4,12},{5,13},{6,14},{7,15},{8,0},{9,1},... | collective-permute-start | bytes 1376264 | tf_op jit(solution)/shard_map/ppermute | solution.py:52
  50.0 11.6 %collective-permute-start.7 = (bf16[15,128,128]{2,1,0:T(8,128)(2,1)S(1)}, bf16[15,128,128]{2,1,0:T(8,128)(2,1)S(1)}, u32[]{:S(2)}, u32[]{:S(2)}) collective-permute-start(bf16[15,128,128]{2,1,0:T(8,128)(2,1)S(1)} %slice.503), channel_id=1, source_target_pairs={{0,16},{1,17},{2,18},{3,19},{4,20},{5,21},{6,22},{7,23},{8,24},{9,... | collective-permute-start | bytes 1474568 | tf_op jit(solution)/shard_map/ppermute | solution.py:52
  61.7 21.4 %collective-permute-start.11 = (bf16[29,128,128]{2,1,0:T(8,128)(2,1)S(1)}, bf16[29,128,128]{2,1,0:T(8,128)(2,1)S(1)}, u32[]{:S(2)}, u32[]{:S(2)}) collective-permute-start(bf16[29,128,128]{2,1,0:T(8,128)(2,1)S(1)} %packed_far.1.refs_0_), channel_id=1, source_target_pairs={{0,16},{1,17},{2,18},{3,19},{4,20},{5,21},{6,22},{7,23},{8,24},{9,... | collective-permute-start | bytes 2850824 | tf_op jit(solution)/shard_map/ppermute | solution.py:52
  62.9 20.2 %collective-permute-start.10 = (bf16[29,128,128]{2,1,0:T(8,128)(2,1)S(1)}, bf16[29,128,128]{2,1,0:T(8,128)(2,1)S(1)}, u32[]{:S(2)}, u32[]{:S(2)}) collective-permute-start(bf16[29,128,128]{2,1,0:T(8,128)(2,1)S(1)} %packed_far.1.refs_0_), channel_id=1, source_target_pairs={{0,8},{1,9},{2,10},{3,11},{4,12},{5,13},{6,14},{7,15},{8,0},{9,1},... | collective-permute-start | bytes 2850824 | tf_op jit(solution)/shard_map/ppermute | solution.py:52
  63.5 19.6 %collective-permute-start.12 = (bf16[432,512]{1,0:T(8,128)(2,1)S(1)}, bf16[432,512]{1,0:T(8,128)(2,1)S(1)}, u32[]{:S(2)}, u32[]{:S(2)}) collective-permute-start(bf16[432,512]{1,0:T(8,128)(2,1)S(1)} %bitcast.248), channel_id=1, source_target_pairs={{0,2},{1,3},{2,0},{3,1},{4,6},{5,7},{6,4},{7,5},{8,10},{9,11},{10,... | collective-permute-start | bytes 1327112 | tf_op jit(solution)/shard_map/ppermute | solution.py:52
  84.1 17.9 %collective-permute-start.15 = (bf16[15,128,128]{2,1,0:T(8,128)(2,1)}, bf16[15,128,128]{2,1,0:T(8,128)(2,1)}, u32[]{:S(2)}, u32[]{:S(2)}) collective-permute-start(bf16[15,128,128]{2,1,0:T(8,128)(2,1)} %slice.404), channel_id=1, source_target_pairs={{0,16},{1,17},{2,18},{3,19},{4,20},{5,21},{6,22},{7,23},{8,24},{9,... | collective-permute-start | bytes 1474568 | tf_op jit(solution)/shard_map/ppermute | solution.py:52
  86.4 15.5 %collective-permute-start.16 = (bf16[14,128,128]{2,1,0:T(8,128)(2,1)}, bf16[14,128,128]{2,1,0:T(8,128)(2,1)}, u32[]{:S(2)}, u32[]{:S(2)}) collective-permute-start(bf16[14,128,128]{2,1,0:T(8,128)(2,1)} %slice.405), channel_id=1, source_target_pairs={{0,8},{1,9},{2,10},{3,11},{4,12},{5,13},{6,14},{7,15},{8,0},{9,1},... | collective-permute-start | bytes 1376264 | tf_op jit(solution)/shard_map/ppermute | solution.py:52
  87.6 20.1 %collective-permute-start.14 = (bf16[432,512]{1,0:T(8,128)(2,1)}, bf16[432,512]{1,0:T(8,128)(2,1)}, u32[]{:S(2)}, u32[]{:S(2)}) collective-permute-start(bf16[432,512]{1,0:T(8,128)(2,1)} %get-tuple-element.98), channel_id=1, source_target_pairs={{0,3},{1,2},{2,1},{3,0},{4,7},{5,6},{6,5},{7,4},{8,11},{9,10},{10,... | collective-permute-start | bytes 1327112 | tf_op jit(solution)/shard_map/ppermute | solution.py:52
  91.2 18.9 %collective-permute-start.13 = (bf16[432,512]{1,0:T(8,128)(2,1)}, bf16[432,512]{1,0:T(8,128)(2,1)}, u32[]{:S(2)}, u32[]{:S(2)}) collective-permute-start(bf16[432,512]{1,0:T(8,128)(2,1)} %get-tuple-element.135), channel_id=1, source_target_pairs={{0,1},{1,0},{2,3},{3,2},{4,5},{5,4},{6,7},{7,6},{8,9},{9,8},{10,11... | collective-permute-start | bytes 1327112 | tf_op jit(solution)/shard_map/ppermute | solution.py:52
  110.1 24.4 %collective-permute-start.17 = (bf16[432,512]{1,0:T(8,128)(2,1)}, bf16[432,512]{1,0:T(8,128)(2,1)S(1)}, u32[]{:S(2)}, u32[]{:S(2)}) collective-permute-start(bf16[432,512]{1,0:T(8,128)(2,1)} %get-tuple-element.98), channel_id=1, source_target_pairs={{0,1},{1,0},{2,3},{3,2},{4,5},{5,4},{6,7},{7,6},{8,9},{9,8},{10,11... | collective-permute-start | bytes 1327112 | tf_op jit(solution)/shard_map/ppermute | solution.py:52
  111.8 22.7 %collective-permute-start.18 = (bf16[432,512]{1,0:T(8,128)(2,1)S(1)}, bf16[432,512]{1,0:T(8,128)(2,1)S(1)}, u32[]{:S(2)}, u32[]{:S(2)}) collective-permute-start(bf16[432,512]{1,0:T(8,128)(2,1)S(1)} %bitcast.243), channel_id=1, source_target_pairs={{0,2},{1,3},{2,0},{3,1},{4,6},{5,7},{6,4},{7,5},{8,10},{9,11},{10,... | collective-permute-start | bytes 1327112 | tf_op jit(solution)/shard_map/ppermute | solution.py:52
  112.3 22.1 %collective-permute-start.19 = (bf16[64,160]{1,0:T(8,128)(2,1)S(1)}, bf16[64,160]{1,0:T(8,128)(2,1)S(1)}, u32[]{:S(2)}, u32[]{:S(2)}) collective-permute-start(bf16[64,160]{1,0:T(8,128)(2,1)S(1)} %bitcast.252), channel_id=1, source_target_pairs={{0,2},{1,3},{2,0},{3,1},{4,6},{5,7},{6,4},{7,5},{8,10},{9,11},{10,... | collective-permute-start | bytes 61448 | tf_op jit(solution)/shard_map/ppermute | solution.py:52
  134.6 4.6 %collective-permute-start.20 = (bf16[864,1024]{1,0:T(8,128)(2,1)}, bf16[864,1024]{1,0:T(8,128)(2,1)S(1)}, u32[]{:S(2)}, u32[]{:S(2)}) collective-permute-start(bf16[864,1024]{1,0:T(8,128)(2,1)} %get-tuple-element.101), channel_id=1, source_target_pairs={{0,4},{1,5},{2,6},{3,7},{4,0},{5,1},{6,2},{7,3},{8,12},{9,13},{10,... | collective-permute-start | bytes 5308424 | tf_op jit(solution)/shard_map/ppermute | solution.py:52
  134.6 4.5 %collective-permute-start.21 = (bf16[2,64,160]{2,1,0:T(8,128)(2,1)S(1)}, bf16[2,64,160]{2,1,0:T(8,128)(2,1)S(1)}, u32[]{:S(2)}, u32[]{:S(2)}) collective-permute-start(bf16[2,64,160]{2,1,0:T(8,128)(2,1)S(1)} %pad_maximum_fusion.10), channel_id=1, source_target_pairs={{0,1},{1,0},{2,3},{3,2},{4,5},{5,4},{6,7},{7,6},{8,9},{9,8},{10,11... | collective-permute-start | bytes 122888 | tf_op jit(solution)/shard_map/ppermute | solution.py:52
  139.2 5.3 %collective-permute-start.23 = (bf16[2,2,64,160]{3,2,1,0:T(8,128)(2,1)S(1)}, bf16[2,2,64,160]{3,2,1,0:T(8,128)(2,1)S(1)}, u32[]{:S(2)}, u32[]{:S(2)}) collective-permute-start(bf16[2,2,64,160]{3,2,1,0:T(8,128)(2,1)S(1)} %pad_maximum_fusion.9), channel_id=1, source_target_pairs={{0,4},{1,5},{2,6},{3,7},{4,0},{5,1},{6,2},{7,3},{8,12},{9,13},{10,... | collective-permute-start | bytes 245768 | tf_op jit(solution)/shard_map/ppermute | solution.py:52
  139.3 13.5 %collective-permute-start.27 = (bf16[432,256]{1,0:T(8,128)(2,1)}, bf16[432,256]{1,0:T(8,128)(2,1)S(1)}, u32[]{:S(2)}, u32[]{:S(2)}) collective-permute-start(bf16[432,256]{1,0:T(8,128)(2,1)} %bitcast.41), channel_id=1, source_target_pairs={{0,6},{1,7},{2,4},{3,5},{4,2},{5,3},{6,0},{7,1},{8,14},{9,15},{10,... | collective-permute-start | bytes 663560 | tf_op jit(solution)/shard_map/ppermute | solution.py:52
  143.5 26.5 %collective-permute-start.22 = (bf16[432,1024]{1,0:T(8,128)(2,1)}, bf16[432,1024]{1,0:T(8,128)(2,1)S(1)}, u32[]{:S(2)}, u32[]{:S(2)}) collective-permute-start(bf16[432,1024]{1,0:T(8,128)(2,1)} %get-tuple-element.171), channel_id=1, source_target_pairs={{0,1},{1,0},{2,3},{3,2},{4,5},{5,4},{6,7},{7,6},{8,9},{9,8},{10,11... | collective-permute-start | bytes 2654216 | tf_op jit(solution)/shard_map/ppermute | solution.py:52
  144.6 9.8 %collective-permute-start.26 = (bf16[2,2,2,64,160]{4,3,2,1,0:T(8,128)(2,1)S(1)}, bf16[2,2,2,64,160]{4,3,2,1,0:T(8,128)(2,1)S(1)}, u32[]{:S(2)}, u32[]{:S(2)}) collective-permute-start(bf16[2,2,2,64,160]{4,3,2,1,0:T(8,128)(2,1)S(1)} %pad_maximum_fusion.8), channel_id=1, source_target_pairs={{0,8},{1,9},{2,10},{3,11},{4,12},{5,13},{6,14},{7,15},{8,0},{9,1},... | collective-permute-start | bytes 491528 | tf_op jit(solution)/shard_map/ppermute | solution.py:52
  145.7 11.9 %collective-permute-start.25 = (bf16[2,2,2,64,160]{4,3,2,1,0:T(8,128)(2,1)S(1)}, bf16[2,2,2,64,160]{4,3,2,1,0:T(8,128)(2,1)S(1)}, u32[]{:S(2)}, u32[]{:S(2)}) collective-permute-start(bf16[2,2,2,64,160]{4,3,2,1,0:T(8,128)(2,1)S(1)} %pad_maximum_fusion.8), channel_id=1, source_target_pairs={{0,16},{1,17},{2,18},{3,19},{4,20},{5,21},{6,22},{7,23},{8,24},{9,... | collective-permute-start | bytes 491528 | tf_op jit(solution)/shard_map/ppermute | solution.py:52
  146.7 12.5 %collective-permute-start.24 = (bf16[2,2,2,64,160]{4,3,2,1,0:T(8,128)(2,1)S(1)}, bf16[2,2,2,64,160]{4,3,2,1,0:T(8,128)(2,1)S(1)}, u32[]{:S(2)}, u32[]{:S(2)}) collective-permute-start(bf16[2,2,2,64,160]{4,3,2,1,0:T(8,128)(2,1)S(1)} %pad_maximum_fusion.8), channel_id=1, source_target_pairs={{0,24},{1,25},{2,26},{3,27},{4,28},{5,29},{6,30},{7,31},{8,16},{9,... | collective-permute-start | bytes 491528 | tf_op jit(solution)/shard_map/ppermute | solution.py:52
  176.1 3.9 %collective-permute-start.30 = (f32[24,256]{1,0:T(8,128)S(1)}, f32[24,256]{1,0:T(8,128)S(1)}, u32[]{:S(2)}, u32[]{:S(2)}) collective-permute-start(f32[24,256]{1,0:T(8,128)S(1)} %pad_maximum_fusion.11), channel_id=1, source_target_pairs={{0,16},{1,17},{2,18},{3,19},{4,20},{5,21},{6,22},{7,23},{8,24},{9,... | collective-permute-start | bytes 73736 | tf_op jit(solution)/shard_map/ppermute | solution.py:52
  177.7 4.7 %collective-permute-start.31 = (f32[24,256]{1,0:T(8,128)S(1)}, f32[24,256]{1,0:T(8,128)S(1)}, u32[]{:S(2)}, u32[]{:S(2)}) collective-permute-start(f32[24,256]{1,0:T(8,128)S(1)} %pad_maximum_fusion.11), channel_id=1, source_target_pairs={{0,24},{1,25},{2,26},{3,27},{4,28},{5,29},{6,30},{7,31},{8,16},{9,... | collective-permute-start | bytes 73736 | tf_op jit(solution)/shard_map/ppermute | solution.py:52
  182.6 5.7 %collective-permute-start.34 = (f32[24,256]{1,0:T(8,128)S(1)}, f32[24,256]{1,0:T(8,128)S(1)}, u32[]{:S(2)}, u32[]{:S(2)}) collective-permute-start(f32[24,256]{1,0:T(8,128)S(1)} %pad_maximum_fusion.12.refs_0_), channel_id=1, source_target_pairs={{0,3},{1,2},{2,1},{3,0},{4,7},{5,6},{6,5},{7,4},{8,11},{9,10},{10,... | collective-permute-start | bytes 73736 | tf_op jit(solution)/shard_map/ppermute | solution.py:52
  184.5 4.7 %collective-permute-start.33 = (f32[24,256]{1,0:T(8,128)S(1)}, f32[24,256]{1,0:T(8,128)S(1)}, u32[]{:S(2)}, u32[]{:S(2)}) collective-permute-start(f32[24,256]{1,0:T(8,128)S(1)} %pad_maximum_fusion.12.refs_0_), channel_id=1, source_target_pairs={{0,2},{1,3},{2,0},{3,1},{4,6},{5,7},{6,4},{7,5},{8,10},{9,11},{10,... | collective-permute-start | bytes 73736 | tf_op jit(solution)/shard_map/ppermute | solution.py:52
  184.5 4.7 %collective-permute-start.32 = (f32[24,256]{1,0:T(8,128)S(1)}, f32[24,256]{1,0:T(8,128)S(1)}, u32[]{:S(2)}, u32[]{:S(2)}) collective-permute-start(f32[24,256]{1,0:T(8,128)S(1)} %pad_maximum_fusion.12.refs_0_), channel_id=1, source_target_pairs={{0,1},{1,0},{2,3},{3,2},{4,5},{5,4},{6,7},{7,6},{8,9},{9,8},{10,11... | collective-permute-start | bytes 73736 | tf_op jit(solution)/shard_map/ppermute | solution.py:52
  195.5 4.2 %collective-permute-start.37 = (f32[8,256]{1,0:T(8,128)S(1)}, f32[8,256]{1,0:T(8,128)S(1)}, u32[]{:S(2)}, u32[]{:S(2)}) collective-permute-start(f32[8,256]{1,0:T(8,128)S(1)} %pad_maximum_fusion.13), channel_id=1, source_target_pairs={{0,16},{1,17},{2,18},{3,19},{4,20},{5,21},{6,22},{7,23},{8,24},{9,... | collective-permute-start | bytes 24584 | tf_op jit(solution)/shard_map/ppermute | solution.py:52
  196.6 4.5 %collective-permute-start.38 = (f32[8,256]{1,0:T(8,128)S(1)}, f32[8,256]{1,0:T(8,128)S(1)}, u32[]{:S(2)}, u32[]{:S(2)}) collective-permute-start(f32[8,256]{1,0:T(8,128)S(1)} %pad_maximum_fusion.13), channel_id=1, source_target_pairs={{0,24},{1,25},{2,26},{3,27},{4,28},{5,29},{6,30},{7,31},{8,16},{9,... | collective-permute-start | bytes 24584 | tf_op jit(solution)/shard_map/ppermute | solution.py:52
  201.7 4.6 %collective-permute-start.40 = (f32[8,256]{1,0:T(8,128)S(1)}, f32[8,256]{1,0:T(8,128)S(1)}, u32[]{:S(2)}, u32[]{:S(2)}) collective-permute-start(f32[8,256]{1,0:T(8,128)S(1)} %pad_maximum_fusion.14), channel_id=1, source_target_pairs={{0,2},{1,3},{2,0},{3,1},{4,6},{5,7},{6,4},{7,5},{8,10},{9,11},{10,... | collective-permute-start | bytes 24584 | tf_op jit(solution)/shard_map/ppermute | solution.py:52
  203.8 5.4 %collective-permute-start.41 = (f32[8,256]{1,0:T(8,128)S(1)}, f32[8,256]{1,0:T(8,128)S(1)}, u32[]{:S(2)}, u32[]{:S(2)}) collective-permute-start(f32[8,256]{1,0:T(8,128)S(1)} %pad_maximum_fusion.14), channel_id=1, source_target_pairs={{0,3},{1,2},{2,1},{3,0},{4,7},{5,6},{6,5},{7,4},{8,11},{9,10},{10,... | collective-permute-start | bytes 24584 | tf_op jit(solution)/shard_map/ppermute | solution.py:52
  212.3 3.9 %collective-permute-start.44 = (f32[8,256]{1,0:T(8,128)S(1)}, f32[8,256]{1,0:T(8,128)S(1)}, u32[]{:S(2)}, u32[]{:S(2)}) collective-permute-start(f32[8,256]{1,0:T(8,128)S(1)} %fusion.41), channel_id=1, source_target_pairs={{0,16},{1,17},{2,18},{3,19},{4,20},{5,21},{6,22},{7,23},{8,24},{9,... | collective-permute-start | bytes 24584 | tf_op jit(solution)/shard_map/ppermute | solution.py:52
  213.8 4.5 %collective-permute-start.45 = (f32[8,256]{1,0:T(8,128)S(1)}, f32[8,256]{1,0:T(8,128)S(1)}, u32[]{:S(2)}, u32[]{:S(2)}) collective-permute-start(f32[8,256]{1,0:T(8,128)S(1)} %fusion.41), channel_id=1, source_target_pairs={{0,24},{1,25},{2,26},{3,27},{4,28},{5,29},{6,30},{7,31},{8,16},{9,... | collective-permute-start | bytes 24584 | tf_op jit(solution)/shard_map/ppermute | solution.py:52
  215.8 7.2 %collective-permute-start.56 = (bf16[16,512]{1,0:T(8,128)(2,1)S(1)}, bf16[16,512]{1,0:T(8,128)(2,1)S(1)}, u32[]{:S(2)}, u32[]{:S(2)}) collective-permute-start(bf16[16,512]{1,0:T(8,128)(2,1)S(1)} %copy-done.45), channel_id=1, source_target_pairs={{0,2},{1,3},{2,0},{3,1},{4,6},{5,7},{6,4},{7,5},{8,10},{9,11},{10,... | collective-permute-start | bytes 49160 | tf_op jit(solution)/shard_map/ppermute | solution.py:52
  218.6 5.5 %collective-permute-start.48 = (f32[8,256]{1,0:T(8,128)S(1)}, f32[8,256]{1,0:T(8,128)S(1)}, u32[]{:S(2)}, u32[]{:S(2)}) collective-permute-start(f32[8,256]{1,0:T(8,128)S(1)} %add_add_fusion.2.refs_0_), channel_id=1, source_target_pairs={{0,3},{1,2},{2,1},{3,0},{4,7},{5,6},{6,5},{7,4},{8,11},{9,10},{10,... | collective-permute-start | bytes 24584 | tf_op jit(solution)/shard_map/ppermute | solution.py:52
  220.4 4.5 %collective-permute-start.47 = (f32[8,256]{1,0:T(8,128)S(1)}, f32[8,256]{1,0:T(8,128)S(1)}, u32[]{:S(2)}, u32[]{:S(2)}) collective-permute-start(f32[8,256]{1,0:T(8,128)S(1)} %add_add_fusion.2.refs_0_), channel_id=1, source_target_pairs={{0,2},{1,3},{2,0},{3,1},{4,6},{5,7},{6,4},{7,5},{8,10},{9,11},{10,... | collective-permute-start | bytes 24584 | tf_op jit(solution)/shard_map/ppermute | solution.py:52
  220.4 4.5 %collective-permute-start.46 = (f32[8,256]{1,0:T(8,128)S(1)}, f32[8,256]{1,0:T(8,128)S(1)}, u32[]{:S(2)}, u32[]{:S(2)}) collective-permute-start(f32[8,256]{1,0:T(8,128)S(1)} %add_add_fusion.2.refs_0_), channel_id=1, source_target_pairs={{0,1},{1,0},{2,3},{3,2},{4,5},{5,4},{6,7},{7,6},{8,9},{9,8},{10,11... | collective-permute-start | bytes 24584 | tf_op jit(solution)/shard_map/ppermute | solution.py:52
  228.1 4.7 %collective-permute-start.52 = (f32[16,256]{1,0:T(8,128)S(1)}, f32[16,256]{1,0:T(8,128)S(1)}, u32[]{:S(2)}, u32[]{:S(2)}) collective-permute-start(f32[16,256]{1,0:T(8,128)S(1)} %add.282), channel_id=1, source_target_pairs={{0,24},{1,25},{2,26},{3,27},{4,28},{5,29},{6,30},{7,31},{8,16},{9,... | collective-permute-start | bytes 49160 | tf_op jit(solution)/shard_map/ppermute | solution.py:52
  234.2 5.6 %collective-permute-start.55 = (f32[16,256]{1,0:T(8,128)S(1)}, f32[16,256]{1,0:T(8,128)S(1)}, u32[]{:S(2)}, u32[]{:S(2)}) collective-permute-start(f32[16,256]{1,0:T(8,128)S(1)} %add_add_fusion.1.refs_0_), channel_id=1, source_target_pairs={{0,3},{1,2},{2,1},{3,0},{4,7},{5,6},{6,5},{7,4},{8,11},{9,10},{10,... | collective-permute-start | bytes 49160 | tf_op jit(solution)/shard_map/ppermute | solution.py:52
  236.2 4.8 %collective-permute-start.54 = (f32[16,256]{1,0:T(8,128)S(1)}, f32[16,256]{1,0:T(8,128)S(1)}, u32[]{:S(2)}, u32[]{:S(2)}) collective-permute-start(f32[16,256]{1,0:T(8,128)S(1)} %add_add_fusion.1.refs_0_), channel_id=1, source_target_pairs={{0,2},{1,3},{2,0},{3,1},{4,6},{5,7},{6,4},{7,5},{8,10},{9,11},{10,... | collective-permute-start | bytes 49160 | tf_op jit(solution)/shard_map/ppermute | solution.py:52
  243.1 35.4 %collective-permute-start.60 = (bf16[432,1024]{1,0:T(8,128)(2,1)S(1)}, bf16[432,1024]{1,0:T(8,128)(2,1)}, u32[]{:S(2)}, u32[]{:S(2)}) collective-permute-start(bf16[432,1024]{1,0:T(8,128)(2,1)S(1)} %get-tuple-element.121.refs_0_.refs_4_), channel_id=1, source_target_pairs={{0,4},{1,5},{2,6},{3,7},{4,0},{5,1},{6,2},{7,3},{8,12},{9,13},{10,... | collective-permute-start | bytes 2654216 | tf_op jit(solution)/shard_map/ppermute | solution.py:52
  243.2 31.6 %collective-permute-start.57 = (bf16[432,1024]{1,0:T(8,128)(2,1)S(1)}, bf16[432,1024]{1,0:T(8,128)(2,1)}, u32[]{:S(2)}, u32[]{:S(2)}) collective-permute-start(bf16[432,1024]{1,0:T(8,128)(2,1)S(1)} %get-tuple-element.121.refs_0_.refs_4_), channel_id=1, source_target_pairs={{0,1},{1,0},{2,3},{3,2},{4,5},{5,4},{6,7},{7,6},{8,9},{9,8},{10,11... | collective-permute-start | bytes 2654216 | tf_op jit(solution)/shard_map/ppermute | solution.py:52
  246.7 26.9 %collective-permute-start.58 = (bf16[432,512]{1,0:T(8,128)(2,1)S(1)}, bf16[432,512]{1,0:T(8,128)(2,1)}, u32[]{:S(2)}, u32[]{:S(2)}) collective-permute-start(bf16[432,512]{1,0:T(8,128)(2,1)S(1)} %get-tuple-element.122), channel_id=1, source_target_pairs={{0,2},{1,3},{2,0},{3,1},{4,6},{5,7},{6,4},{7,5},{8,10},{9,11},{10,... | collective-permute-start | bytes 1327112 | tf_op jit(solution)/shard_map/ppermute | solution.py:52
  276.7 22.9 %collective-permute-start.65 = (bf16[432,512]{1,0:T(8,128)(2,1)}, bf16[432,512]{1,0:T(8,128)(2,1)S(1)}, u32[]{:S(2)}, u32[]{:S(2)}) collective-permute-start(bf16[432,512]{1,0:T(8,128)(2,1)} %collective-permute-done.58.refs_8_), channel_id=1, source_target_pairs={{0,1},{1,0},{2,3},{3,2},{4,5},{5,4},{6,7},{7,6},{8,9},{9,8},{10,11... | collective-permute-start | bytes 1327112 | tf_op jit(solution)/shard_map/ppermute | solution.py:52
  278.6 22.7 %collective-permute-start.63 = (bf16[2,2,2,64,160]{4,3,2,1,0:T(8,128)(2,1)S(1)}, bf16[2,2,2,64,160]{4,3,2,1,0:T(8,128)(2,1)S(1)}, u32[]{:S(2)}, u32[]{:S(2)}) collective-permute-start(bf16[2,2,2,64,160]{4,3,2,1,0:T(8,128)(2,1)S(1)} %fusion.6), channel_id=1, source_target_pairs={{0,8},{1,9},{2,10},{3,11},{4,12},{5,13},{6,14},{7,15},{8,0},{9,1},... | collective-permute-start | bytes 491528 | tf_op jit(solution)/shard_map/ppermute | solution.py:52
  279.7 21.0 %collective-permute-start.66 = (bf16[432,512]{1,0:T(8,128)(2,1)}, bf16[432,512]{1,0:T(8,128)(2,1)S(1)}, u32[]{:S(2)}, u32[]{:S(2)}) collective-permute-start(bf16[432,512]{1,0:T(8,128)(2,1)} %get-tuple-element.135), channel_id=1, source_target_pairs={{0,3},{1,2},{2,1},{3,0},{4,7},{5,6},{6,5},{7,4},{8,11},{9,10},{10,... | collective-permute-start | bytes 1327112 | tf_op jit(solution)/shard_map/ppermute | solution.py:52
  299.6 25.5 %collective-permute-start.62 = (bf16[432,256]{1,0:T(8,128)(2,1)S(1)}, bf16[432,256]{1,0:T(8,128)(2,1)S(1)}, u32[]{:S(2)}, u32[]{:S(2)}) collective-permute-start(bf16[432,256]{1,0:T(8,128)(2,1)S(1)} %copy-done.33), channel_id=1, source_target_pairs={{0,6},{1,7},{2,4},{3,5},{4,2},{5,3},{6,0},{7,1},{8,14},{9,15},{10,... | collective-permute-start | bytes 663560 | tf_op jit(solution)/shard_map/ppermute | solution.py:52
  301.4 24.9 %collective-permute-start.64 = (bf16[1,2,2,64,160]{4,3,2,1,0:T(8,128)(2,1)S(1)}, bf16[1,2,2,64,160]{4,3,2,1,0:T(8,128)(2,1)S(1)}, u32[]{:S(2)}, u32[]{:S(2)}) collective-permute-start(bf16[1,2,2,64,160]{4,3,2,1,0:T(8,128)(2,1)S(1)} %select_bitcast_fusion.8), channel_id=1, source_target_pairs={{0,16},{1,17},{2,18},{3,19},{4,20},{5,21},{6,22},{7,23},{8,24},{9,... | collective-permute-start | bytes 245768 | tf_op jit(solution)/shard_map/ppermute | solution.py:52
  303.4 28.0 %collective-permute-start.69 = (bf16[432,512]{1,0:T(8,128)(2,1)}, bf16[432,512]{1,0:T(8,128)(2,1)}, u32[]{:S(2)}, u32[]{:S(2)}) collective-permute-start(bf16[432,512]{1,0:T(8,128)(2,1)} %get-tuple-element.138), channel_id=1, source_target_pairs={{0,2},{1,3},{2,0},{3,1},{4,6},{5,7},{6,4},{7,5},{8,10},{9,11},{10,... | collective-permute-start | bytes 1327112 | tf_op jit(solution)/shard_map/ppermute | solution.py:52
  304.9 26.4 %collective-permute-start.70 = (bf16[432,512]{1,0:T(8,128)(2,1)}, bf16[432,512]{1,0:T(8,128)(2,1)S(1)}, u32[]{:S(2)}, u32[]{:S(2)}) collective-permute-start(bf16[432,512]{1,0:T(8,128)(2,1)} %get-tuple-element.139), channel_id=1, source_target_pairs={{0,1},{1,0},{2,3},{3,2},{4,5},{5,4},{6,7},{7,6},{8,9},{9,8},{10,11... | collective-permute-start | bytes 1327112 | tf_op jit(solution)/shard_map/ppermute | solution.py:52
  323.5 12.6 %collective-permute-start.74 = (bf16[29,64,128]{2,1,0:T(8,128)(2,1)}, bf16[29,64,128]{2,1,0:T(8,128)(2,1)S(1)}, u32[]{:S(2)}, u32[]{:S(2)}) collective-permute-start(bf16[29,64,128]{2,1,0:T(8,128)(2,1)} %get-tuple-element.144), channel_id=1, source_target_pairs={{0,16},{1,17},{2,18},{3,19},{4,20},{5,21},{6,22},{7,23},{8,24},{9,... | collective-permute-start | bytes 1425416 | tf_op jit(solution)/shard_map/ppermute | solution.py:52
  325.1 12.2 %collective-permute-start.75 = (bf16[29,64,128]{2,1,0:T(8,128)(2,1)}, bf16[29,64,128]{2,1,0:T(8,128)(2,1)S(1)}, u32[]{:S(2)}, u32[]{:S(2)}) collective-permute-start(bf16[29,64,128]{2,1,0:T(8,128)(2,1)} %get-tuple-element.145), channel_id=1, source_target_pairs={{0,8},{1,9},{2,10},{3,11},{4,12},{5,13},{6,14},{7,15},{8,0},{9,1},... | collective-permute-start | bytes 1425416 | tf_op jit(solution)/shard_map/ppermute | solution.py:52
  331.4 14.6 %collective-permute-start.78 = (bf16[2,64,160]{2,1,0:T(8,128)(2,1)S(1)}, bf16[2,64,160]{2,1,0:T(8,128)(2,1)S(1)}, u32[]{:S(2)}, u32[]{:S(2)}) collective-permute-start(bf16[2,64,160]{2,1,0:T(8,128)(2,1)S(1)} %select_bitcast_fusion.11), channel_id=1, source_target_pairs={{0,2},{1,3},{2,0},{3,1},{4,6},{5,7},{6,4},{7,5},{8,10},{9,11},{10,... | collective-permute-start | bytes 122888 | tf_op jit(solution)/shard_map/ppermute | solution.py:52
  331.4 24.7 %collective-permute-start.71 = (bf16[432,512]{1,0:T(8,128)(2,1)}, bf16[432,512]{1,0:T(8,128)(2,1)S(1)}, u32[]{:S(2)}, u32[]{:S(2)}) collective-permute-start(bf16[432,512]{1,0:T(8,128)(2,1)} %get-tuple-element.140), channel_id=1, source_target_pairs={{0,2},{1,3},{2,0},{3,1},{4,6},{5,7},{6,4},{7,5},{8,10},{9,11},{10,... | collective-permute-start | bytes 1327112 | tf_op jit(solution)/shard_map/ppermute | solution.py:52
  334.3 21.9 %collective-permute-start.72 = (bf16[432,512]{1,0:T(8,128)(2,1)}, bf16[432,512]{1,0:T(8,128)(2,1)S(1)}, u32[]{:S(2)}, u32[]{:S(2)}) collective-permute-start(bf16[432,512]{1,0:T(8,128)(2,1)} %collective-permute-done.69), channel_id=1, source_target_pairs={{0,1},{1,0},{2,3},{3,2},{4,5},{5,4},{6,7},{7,6},{8,9},{9,8},{10,11... | collective-permute-start | bytes 1327112 | tf_op jit(solution)/shard_map/ppermute | solution.py:52
  338.6 21.3 %collective-permute-start.77 = (bf16[2,29,64,128]{3,2,1,0:T(8,128)(2,1)S(1)}, bf16[2,29,64,128]{3,2,1,0:T(8,128)(2,1)S(1)}, u32[]{:S(2)}, u32[]{:S(2)}) collective-permute-start(bf16[2,29,64,128]{3,2,1,0:T(8,128)(2,1)S(1)} %pad_maximum_fusion.1), channel_id=1, source_target_pairs={{0,16},{1,17},{2,18},{3,19},{4,20},{5,21},{6,22},{7,23},{8,24},{9,... | collective-permute-start | bytes 2850824 | tf_op jit(solution)/shard_map/ppermute | solution.py:52
  339.6 21.3 %collective-permute-start.76 = (bf16[2,29,64,128]{3,2,1,0:T(8,128)(2,1)S(1)}, bf16[2,29,64,128]{3,2,1,0:T(8,128)(2,1)S(1)}, u32[]{:S(2)}, u32[]{:S(2)}) collective-permute-start(bf16[2,29,64,128]{3,2,1,0:T(8,128)(2,1)S(1)} %pad_maximum_fusion), channel_id=1, source_target_pairs={{0,8},{1,9},{2,10},{3,11},{4,12},{5,13},{6,14},{7,15},{8,0},{9,1},... | collective-permute-start | bytes 2850824 | tf_op jit(solution)/shard_map/ppermute | solution.py:52
  356.4 6.2 %collective-permute-start.73 = (bf16[2,432,512]{2,1,0:T(8,128)(2,1)S(1)}, bf16[2,432,512]{2,1,0:T(8,128)(2,1)S(1)}, u32[]{:S(2)}, u32[]{:S(2)}) collective-permute-start(bf16[2,432,512]{2,1,0:T(8,128)(2,1)S(1)} %pad_maximum_fusion.3), channel_id=1, source_target_pairs={{0,4},{1,5},{2,6},{3,7},{4,0},{5,1},{6,2},{7,3},{8,12},{9,13},{10,... | collective-permute-start | bytes 2654216 | tf_op jit(solution)/shard_map/ppermute | solution.py:52
  361.6 11.6 %collective-permute-start.79 = (bf16[29,64,128]{2,1,0:T(8,128)(2,1)S(1)}, bf16[29,64,128]{2,1,0:T(8,128)(2,1)S(1)}, u32[]{:S(2)}, u32[]{:S(2)}) collective-permute-start(bf16[29,64,128]{2,1,0:T(8,128)(2,1)S(1)} %broadcast_select_fusion.7), channel_id=1, source_target_pairs={{0,1},{1,0},{2,3},{3,2},{4,5},{5,4},{6,7},{7,6},{8,9},{9,8},{10,11... | collective-permute-start | bytes 1425416 | tf_op jit(solution)/shard_map/ppermute | solution.py:52
  364.9 7.5 %collective-permute-start.81 = (bf16[1,64,160]{2,1,0:T(8,128)(2,1)S(1)}, bf16[1,64,160]{2,1,0:T(8,128)(2,1)S(1)}, u32[]{:S(2)}, u32[]{:S(2)}) collective-permute-start(bf16[1,64,160]{2,1,0:T(8,128)(2,1)S(1)} %select_bitcast_fusion.14), channel_id=1, source_target_pairs={{0,1},{1,0},{2,3},{3,2},{4,5},{5,4},{6,7},{7,6},{8,9},{9,8},{10,11... | collective-permute-start | bytes 61448 | tf_op jit(solution)/shard_map/ppermute | solution.py:52
  (73 other events, 448.0 us)

commit v4 on v3

--- a/solution.py
+++ b/solution.py
@@ -228,7 +228,7 @@
 VMEM = pl.BlockSpec(memory_space=pltpu.VMEM)
 PARAMS = pltpu.CompilerParams(vmem_limit_bytes=58 * 2**20)
 TINY = pltpu.CompilerParams(vmem_limit_bytes=8 * 2**20)
-SMALL = pltpu.CompilerParams(vmem_limit_bytes=12 * 2**20)
+SMALL = pltpu.CompilerParams(vmem_limit_bytes=8 * 2**20)
 
 
 LIGHT = pl.CostEstimate(flops=0, bytes_accessed=0, transcendentals=0)

time: 381 us -> 381 us (level)
  no operation moved by 1% of the time
where the time goes in v4:
time: 381 us; the launch traced here: 377 us
  waiting for transfers between devices  152 us (40%)
  starting transfers between devices  90.9 us (24%)
  Pallas kernels  71.9 us (19%)
  local copies, waits for them, and re-layouts  32.2 us (8%)
  other arithmetic  26.3 us (7%)
    ppermute x82, waiting for transfers between devices, swap(): return lax.ppermute(x, AXES, pairs)  152 us
    ppermute x82, starting transfers between devices, swap(): return lax.ppermute(x, AXES, pairs)  90.9 us
    pallas_call x1, Pallas kernels, branch_sums(): pl.pallas_call(kernel, out_shape=half_shapes(shape, 4) + [jax.ShapeDtypeS...  18.4 us
    pallas_call x1, Pallas kernels, input_gradient(): pl.pallas_call(kernel, out_shape=[jax.ShapeDtypeStruct((shape.band, shape...  18 us
    pallas_call x1, Pallas kernels, weight_gradients(): pl.pallas_call(kernel, out_shape=out_shape, in_specs=[SMEM] + [ANY] * (4...  17.5 us
    unnamed x110, local copies, waits for them, and re-layouts  17.1 us
  transfers between devices with their start and end apart: 82, of which 48 were waited for; matrix products, arithmetic and copies ran while one was open for 10% of the time, Pallas kernels for 17%

profile of v4, /device:TPU:0, one launch (start us, length us, event | category | flops | bytes accessed | tf_op | source)
XLA Modules:
  0.0 377.1 jit_solution(17950361514906470821)
XLA Ops:
  5.0 2.9 collective-permute-start.4
  9.3 2.6 collective-permute-start.3
  14.1 1.5 collective-permute-done
  15.7 8.6 %collective-permute-done.3.first = bf16[16,64,128]{2,1,0:T(8,128)(2,1)S(1)} collective-permute-done((bf16[16,64,128]{2,1,0:T(8,128)(2,1)}, bf16[16,64,128]{2,1,0:T(8,128)(2,1)S(1)}, u32[]{:S(2)}, u32[]{:S(2)}) %collective-permute-start.3) | collective-permute-done | bytes 262176 | tf_op jit(solution)/shard_map/ppermute | solution.py:52
  26.0 1.6 collective-permute-start.8
  27.6 1.5 collective-permute-start.6
  29.1 3.2 collective-permute-start.5
  32.3 1.6 broadcast_select_fusion.2
  33.9 14.6 %collective-permute-done.8.refs_2_ = bf16[29,128,128]{2,1,0:T(8,128)(2,1)S(1)} collective-permute-done((bf16[29,128,128]{2,1,0:T(8,128)(2,1)S(1)}, bf16[29,128,128]{2,1,0:T(8,128)(2,1)S(1)}, u32[]{:S(2)}, u32[]{:S(2)}) %collective-permute-start.8) | collective-permute-done | bytes 950304 | tf_op jit(solution)/shard_map/ppermute | solution.py:52
  50.0 1.6 collective-permute-start.7
  53.4 8.1 %collective-permute-done.5.rest = bf16[42,64,128]{2,1,0:T(8,128)(2,1)S(1)} collective-permute-done((bf16[42,64,128]{2,1,0:T(8,128)(2,1)}, bf16[42,64,128]{2,1,0:T(8,128)(2,1)S(1)}, u32[]{:S(2)}, u32[]{:S(2)}) %collective-permute-start.5) | collective-permute-done | bytes 688160 | tf_op jit(solution)/shard_map/ppermute | solution.py:52
  63.5 3.2 collective-permute-start.12
  66.7 16.4 %collective-permute-done.12.refs_2_ = bf16[432,512]{1,0:T(8,128)(2,1)S(1)} collective-permute-done((bf16[432,512]{1,0:T(8,128)(2,1)S(1)}, bf16[432,512]{1,0:T(8,128)(2,1)S(1)}, u32[]{:S(2)}, u32[]{:S(2)}) %collective-permute-start.12) | collective-permute-done | bytes 442400 | tf_op jit(solution)/shard_map/ppermute | solution.py:52
  84.1 1.5 collective-permute-start.15
  87.6 3.6 collective-permute-start.14
  96.6 3.4 assembled_weights.2.refs_4_.refs_5_
  100.0 1.9 copy-done.2
  101.9 3.9 %assembled_weights.3.refs_5_.refs_6_ = bf16[29,128,512]{2,1,0:T(8,128)(2,1)S(1)} custom-call(s32[8]{0:T(128)S(1)} %stack.122.info, bf16[29,128,128]{2,1,0:T(8,128)(2,1)S(1)} %packed_far.1.refs_0_, bf16[29,128,128]{2,1,0:T(8,128)(2,1)S(1)} %collective-permute-done.10.refs_1_, bf16[29,128,128]{2,1,0:T(8,128)(2,1)S(1)} %copy-done.9, ...), custom_call_target="tpu_custom_call" | custom-call | tf_op jit(solution)/shard_map/assembled_weights/pallas_call | solution.py:378
  105.8 1.9 copy-done.3
  107.7 2.4 collective-permute-done.13.refs_1_
  110.1 1.7 collective-permute-start.17
  112.3 2.4 collective-permute-start.19
  116.0 18.4 %branch_sums.1 = (f32[864,1024]{1,0:T(8,128)}, bf16[864,1024]{1,0:T(8,128)(2,1)}, bf16[16,512]{1,0:T(8,128)(2,1)}, f32[16,256]{1,0:T(8,128)}) custom-call(s32[8]{0:T(128)} %copy-done.25, f32[1]{0:T(128)} %bitcast.11.area, bf16[432,512]{1,0:T(8,128)(2,1)} %bitcast.241, bf16[432,512]{1,0:T(8,128)(2,1)} %collective-permute-done.13.refs_1_, ...), custom_call_target="tpu_custom_call" | custom-call | tf_op jit(solution)/shard_map/branch_sums/pallas_call | solution.py:481
  135.1 4.1 %collective-permute-done.21 = bf16[2,64,160]{2,1,0:T(8,128)(2,1)S(1)} collective-permute-done((bf16[2,64,160]{2,1,0:T(8,128)(2,1)S(1)}, bf16[2,64,160]{2,1,0:T(8,128)(2,1)S(1)}, u32[]{:S(2)}, u32[]{:S(2)}) %collective-permute-start.21) | collective-permute-done | bytes 40992 | tf_op jit(solution)/shard_map/ppermute | solution.py:52
  139.9 3.5 fusion.2
  148.2 4.6 %collective-permute-done.27 = bf16[432,256]{1,0:T(8,128)(2,1)S(1)} collective-permute-done((bf16[432,256]{1,0:T(8,128)(2,1)}, bf16[432,256]{1,0:T(8,128)(2,1)S(1)}, u32[]{:S(2)}, u32[]{:S(2)}) %collective-permute-start.27) | collective-permute-done | bytes 221216 | tf_op jit(solution)/shard_map/ppermute | solution.py:52
  152.8 1.6 broadcast_select_fusion.24
  154.4 3.2 collective-permute-done.25
  157.6 1.6 collective-permute-done.24
  159.6 2.0 copy.22
  161.7 4.8 %reshape.325.projection = bf16[256,1280]{1,0:T(8,128)(2,1)} reshape(bf16[2,2,64,4,2,160]{5,4,3,2,1,0:T(2,128)(2,1)} %copy.22) | data formatting | bytes 1310720 | tf_op jit(solution)/shard_map/reshape | solution.py:956
  166.5 3.4 collective-permute-done.22.refs_0_
  176.1 1.6 collective-permute-start.30
  180.0 2.4 collective-permute-done.31
  182.6 1.9 collective-permute-start.34
  184.5 2.6 collective-permute-start.32
  190.9 1.6 projected.1
  201.7 2.1 collective-permute-start.40
  203.8 2.0 collective-permute-start.41
  206.4 2.9 collective-permute-done.41
  212.3 1.5 collective-permute-start.44
  216.2 2.2 collective-permute-done.45
  218.6 1.9 collective-permute-start.48
  220.4 2.5 collective-permute-start.46
  225.0 1.8 branch_gradients.1
  228.1 1.9 collective-permute-start.52
  234.2 2.0 collective-permute-start.55
  241.1 2.0 branch_deltas.1
  249.9 23.7 %collective-permute-done.58.refs_8_ = bf16[432,512]{1,0:T(8,128)(2,1)} collective-permute-done((bf16[432,512]{1,0:T(8,128)(2,1)S(1)}, bf16[432,512]{1,0:T(8,128)(2,1)}, u32[]{:S(2)}, u32[]{:S(2)}) %collective-permute-start.58) | collective-permute-done | bytes 442400 | tf_op jit(solution)/shard_map/ppermute | solution.py:52
  276.7 1.8 collective-permute-start.65
  279.7 1.9 collective-permute-start.66
  281.6 18.0 %input_gradient.1 = (bf16[432,512]{1,0:T(8,128)(2,1)}, bf16[432,512]{1,0:T(8,128)(2,1)}, bf16[432,512]{1,0:T(8,128)(2,1)}, bf16[432,512]{1,0:T(8,128)(2,1)}) custom-call(s32[8]{0:T(128)} %copy-done.25, f32[1]{0:T(128)} %bitcast.11.area, bf16[432,1024]{1,0:T(8,128)(2,1)} %copy-done.30, bf16[432,1024]{1,0:T(8,128)(2,1)} %collective-permute-done.57.refs_1_.refs_5_, ...), custom_call_target="tpu_custom_call" | custom-call | flops 9965666304 | bytes 16777216 | tf_op jit(solution)/shard_map/input_gradient/pallas_call | solution.py:736
  301.4 1.6 collective-permute-start.64
  303.4 1.6 collective-permute-start.69
  305.9 17.5 %weight_gradients.1 = (bf16[29,64,128]{2,1,0:T(8,128)(2,1)}, bf16[29,64,128]{2,1,0:T(8,128)(2,1)}, bf16[29,64,128]{2,1,0:T(8,128)(2,1)}, bf16[29,64,128]{2,1,0:T...) custom-call(s32[8]{0:T(128)} %copy-done.25, ...), custom_call_target="tpu_custom_call" | custom-call | flops 9965666304 | bytes 16777216 | tf_op jit(solution)/shard_map/weight_gradients/pallas_call | solution.py:848
  323.5 1.6 collective-permute-start.74
  326.4 4.9 %collective-permute-done.69 = bf16[432,512]{1,0:T(8,128)(2,1)} collective-permute-done((bf16[432,512]{1,0:T(8,128)(2,1)}, bf16[432,512]{1,0:T(8,128)(2,1)}, u32[]{:S(2)}, u32[]{:S(2)}) %collective-permute-start.69) | collective-permute-done | bytes 442400 | tf_op jit(solution)/shard_map/ppermute | solution.py:52
  331.4 2.9 collective-permute-start.71
  334.3 1.7 collective-permute-done.74
  340.6 5.4 %collective-permute-done.78 = bf16[2,64,160]{2,1,0:T(8,128)(2,1)S(1)} collective-permute-done((bf16[2,64,160]{2,1,0:T(8,128)(2,1)S(1)}, bf16[2,64,160]{2,1,0:T(8,128)(2,1)S(1)}, u32[]{:S(2)}, u32[]{:S(2)}) %collective-permute-start.78) | collective-permute-done | bytes 40992 | tf_op jit(solution)/shard_map/ppermute | solution.py:52
  346.0 10.1 %collective-permute-done.71 = bf16[432,512]{1,0:T(8,128)(2,1)S(1)} collective-permute-done((bf16[432,512]{1,0:T(8,128)(2,1)}, bf16[432,512]{1,0:T(8,128)(2,1)S(1)}, u32[]{:S(2)}, u32[]{:S(2)}) %collective-permute-start.71) | collective-permute-done | bytes 442400 | tf_op jit(solution)/shard_map/ppermute | solution.py:52
  356.6 3.3 collective-permute-done.77
  362.7 2.3 join_features.1
  366.7 5.8 %collective-permute-done.81 = bf16[1,64,160]{2,1,0:T(8,128)(2,1)S(1)} collective-permute-done((bf16[1,64,160]{2,1,0:T(8,128)(2,1)S(1)}, bf16[1,64,160]{2,1,0:T(8,128)(2,1)S(1)}, u32[]{:S(2)}, u32[]{:S(2)}) %collective-permute-start.81) | collective-permute-done | bytes 20512 | tf_op jit(solution)/shard_map/ppermute | solution.py:52
  (358 shorter events, 99.2 us)
Async XLA Ops:
  5.0 20.0 %collective-permute-start.4 = (bf16[29,64,128]{2,1,0:T(8,128)(2,1)}, bf16[29,64,128]{2,1,0:T(8,128)(2,1)S(1)}, u32[]{:S(2)}, u32[]{:S(2)}) collective-permute-start(bf16[29,64,128]{2,1,0:T(8,128)(2,1)} %get-tuple-element.183), channel_id=1, source_target_pairs={{0,1},{1,0},{2,3},{3,2},{4,5},{5,4},{6,7},{7,6},{8,9},{9,8},{10,11... | collective-permute-start | bytes 1425416 | tf_op jit(solution)/shard_map/ppermute | solution.py:52
  9.3 15.0 %collective-permute-start.3 = (bf16[16,64,128]{2,1,0:T(8,128)(2,1)}, bf16[16,64,128]{2,1,0:T(8,128)(2,1)S(1)}, u32[]{:S(2)}, u32[]{:S(2)}) collective-permute-start(bf16[16,64,128]{2,1,0:T(8,128)(2,1)} %slice.502), channel_id=1, source_target_pairs={{0,2},{1,3},{2,0},{3,1},{4,6},{5,7},{6,4},{7,5},{8,10},{9,11},{10,... | collective-permute-start | bytes 786440 | tf_op jit(solution)/shard_map/ppermute | solution.py:52
  13.6 18.7 %collective-permute-start.1 = (bf16[2,432,512]{2,1,0:T(8,128)(2,1)}, bf16[2,432,512]{2,1,0:T(8,128)(2,1)}, u32[]{:S(2)}, u32[]{:S(2)}) collective-permute-start(bf16[2,432,512]{2,1,0:T(8,128)(2,1)} %get-tuple-element.84), channel_id=1, source_target_pairs={{0,4},{1,5},{2,6},{3,7},{4,0},{5,1},{6,2},{7,3},{8,12},{9,13},{10,... | collective-permute-start | bytes 2654216 | tf_op jit(solution)/shard_map/ppermute | solution.py:52
  26.0 22.5 %collective-permute-start.8 = (bf16[29,128,128]{2,1,0:T(8,128)(2,1)S(1)}, bf16[29,128,128]{2,1,0:T(8,128)(2,1)S(1)}, u32[]{:S(2)}, u32[]{:S(2)}) collective-permute-start(bf16[29,128,128]{2,1,0:T(8,128)(2,1)S(1)} %get-tuple-element.87.refs_0_), channel_id=1, source_target_pairs={{0,16},{1,17},{2,18},{3,19},{4,20},{5,21},{6,22},{7,23},{8,24},{9,... | collective-permute-start | bytes 2850824 | tf_op jit(solution)/shard_map/ppermute | solution.py:52
  27.6 22.3 %collective-permute-start.6 = (bf16[29,128,128]{2,1,0:T(8,128)(2,1)S(1)}, bf16[29,128,128]{2,1,0:T(8,128)(2,1)S(1)}, u32[]{:S(2)}, u32[]{:S(2)}) collective-permute-start(bf16[29,128,128]{2,1,0:T(8,128)(2,1)S(1)} %get-tuple-element.87.refs_0_), channel_id=1, source_target_pairs={{0,8},{1,9},{2,10},{3,11},{4,12},{5,13},{6,14},{7,15},{8,0},{9,1},... | collective-permute-start | bytes 2850824 | tf_op jit(solution)/shard_map/ppermute | solution.py:52
  29.1 32.5 %collective-permute-start.5 = (bf16[42,64,128]{2,1,0:T(8,128)(2,1)}, bf16[42,64,128]{2,1,0:T(8,128)(2,1)S(1)}, u32[]{:S(2)}, u32[]{:S(2)}) collective-permute-start(bf16[42,64,128]{2,1,0:T(8,128)(2,1)} %copy-done.31), channel_id=1, source_target_pairs={{0,2},{1,3},{2,0},{3,1},{4,6},{5,7},{6,4},{7,5},{8,10},{9,11},{10,... | collective-permute-start | bytes 2064392 | tf_op jit(solution)/shard_map/ppermute | solution.py:52
  48.5 13.1 %collective-permute-start.9 = (bf16[14,128,128]{2,1,0:T(8,128)(2,1)S(1)}, bf16[14,128,128]{2,1,0:T(8,128)(2,1)S(1)}, u32[]{:S(2)}, u32[]{:S(2)}) collective-permute-start(bf16[14,128,128]{2,1,0:T(8,128)(2,1)S(1)} %slice.504), channel_id=1, source_target_pairs={{0,8},{1,9},{2,10},{3,11},{4,12},{5,13},{6,14},{7,15},{8,0},{9,1},... | collective-permute-start | bytes 1376264 | tf_op jit(solution)/shard_map/ppermute | solution.py:52
  50.0 11.6 %collective-permute-start.7 = (bf16[15,128,128]{2,1,0:T(8,128)(2,1)S(1)}, bf16[15,128,128]{2,1,0:T(8,128)(2,1)S(1)}, u32[]{:S(2)}, u32[]{:S(2)}) collective-permute-start(bf16[15,128,128]{2,1,0:T(8,128)(2,1)S(1)} %slice.503), channel_id=1, source_target_pairs={{0,16},{1,17},{2,18},{3,19},{4,20},{5,21},{6,22},{7,23},{8,24},{9,... | collective-permute-start | bytes 1474568 | tf_op jit(solution)/shard_map/ppermute | solution.py:52
  61.7 21.4 %collective-permute-start.11 = (bf16[29,128,128]{2,1,0:T(8,128)(2,1)S(1)}, bf16[29,128,128]{2,1,0:T(8,128)(2,1)S(1)}, u32[]{:S(2)}, u32[]{:S(2)}) collective-permute-start(bf16[29,128,128]{2,1,0:T(8,128)(2,1)S(1)} %packed_far.1.refs_0_), channel_id=1, source_target_pairs={{0,16},{1,17},{2,18},{3,19},{4,20},{5,21},{6,22},{7,23},{8,24},{9,... | collective-permute-start | bytes 2850824 | tf_op jit(solution)/shard_map/ppermute | solution.py:52
  62.9 20.2 %collective-permute-start.10 = (bf16[29,128,128]{2,1,0:T(8,128)(2,1)S(1)}, bf16[29,128,128]{2,1,0:T(8,128)(2,1)S(1)}, u32[]{:S(2)}, u32[]{:S(2)}) collective-permute-start(bf16[29,128,128]{2,1,0:T(8,128)(2,1)S(1)} %packed_far.1.refs_0_), channel_id=1, source_target_pairs={{0,8},{1,9},{2,10},{3,11},{4,12},{5,13},{6,14},{7,15},{8,0},{9,1},... | collective-permute-start | bytes 2850824 | tf_op jit(solution)/shard_map/ppermute | solution.py:52
  63.5 19.6 %collective-permute-start.12 = (bf16[432,512]{1,0:T(8,128)(2,1)S(1)}, bf16[432,512]{1,0:T(8,128)(2,1)S(1)}, u32[]{:S(2)}, u32[]{:S(2)}) collective-permute-start(bf16[432,512]{1,0:T(8,128)(2,1)S(1)} %bitcast.248), channel_id=1, source_target_pairs={{0,2},{1,3},{2,0},{3,1},{4,6},{5,7},{6,4},{7,5},{8,10},{9,11},{10,... | collective-permute-start | bytes 1327112 | tf_op jit(solution)/shard_map/ppermute | solution.py:52
  84.1 17.9 %collective-permute-start.15 = (bf16[15,128,128]{2,1,0:T(8,128)(2,1)}, bf16[15,128,128]{2,1,0:T(8,128)(2,1)}, u32[]{:S(2)}, u32[]{:S(2)}) collective-permute-start(bf16[15,128,128]{2,1,0:T(8,128)(2,1)} %slice.404), channel_id=1, source_target_pairs={{0,16},{1,17},{2,18},{3,19},{4,20},{5,21},{6,22},{7,23},{8,24},{9,... | collective-permute-start | bytes 1474568 | tf_op jit(solution)/shard_map/ppermute | solution.py:52
  86.4 15.5 %collective-permute-start.16 = (bf16[14,128,128]{2,1,0:T(8,128)(2,1)}, bf16[14,128,128]{2,1,0:T(8,128)(2,1)}, u32[]{:S(2)}, u32[]{:S(2)}) collective-permute-start(bf16[14,128,128]{2,1,0:T(8,128)(2,1)} %slice.405), channel_id=1, source_target_pairs={{0,8},{1,9},{2,10},{3,11},{4,12},{5,13},{6,14},{7,15},{8,0},{9,1},... | collective-permute-start | bytes 1376264 | tf_op jit(solution)/shard_map/ppermute | solution.py:52
  87.6 20.1 %collective-permute-start.14 = (bf16[432,512]{1,0:T(8,128)(2,1)}, bf16[432,512]{1,0:T(8,128)(2,1)}, u32[]{:S(2)}, u32[]{:S(2)}) collective-permute-start(bf16[432,512]{1,0:T(8,128)(2,1)} %get-tuple-element.98), channel_id=1, source_target_pairs={{0,3},{1,2},{2,1},{3,0},{4,7},{5,6},{6,5},{7,4},{8,11},{9,10},{10,... | collective-permute-start | bytes 1327112 | tf_op jit(solution)/shard_map/ppermute | solution.py:52
  91.2 18.9 %collective-permute-start.13 = (bf16[432,512]{1,0:T(8,128)(2,1)}, bf16[432,512]{1,0:T(8,128)(2,1)}, u32[]{:S(2)}, u32[]{:S(2)}) collective-permute-start(bf16[432,512]{1,0:T(8,128)(2,1)} %get-tuple-element.135), channel_id=1, source_target_pairs={{0,1},{1,0},{2,3},{3,2},{4,5},{5,4},{6,7},{7,6},{8,9},{9,8},{10,11... | collective-permute-start | bytes 1327112 | tf_op jit(solution)/shard_map/ppermute | solution.py:52
  110.1 24.4 %collective-permute-start.17 = (bf16[432,512]{1,0:T(8,128)(2,1)}, bf16[432,512]{1,0:T(8,128)(2,1)S(1)}, u32[]{:S(2)}, u32[]{:S(2)}) collective-permute-start(bf16[432,512]{1,0:T(8,128)(2,1)} %get-tuple-element.98), channel_id=1, source_target_pairs={{0,1},{1,0},{2,3},{3,2},{4,5},{5,4},{6,7},{7,6},{8,9},{9,8},{10,11... | collective-permute-start | bytes 1327112 | tf_op jit(solution)/shard_map/ppermute | solution.py:52
  111.8 22.7 %collective-permute-start.18 = (bf16[432,512]{1,0:T(8,128)(2,1)S(1)}, bf16[432,512]{1,0:T(8,128)(2,1)S(1)}, u32[]{:S(2)}, u32[]{:S(2)}) collective-permute-start(bf16[432,512]{1,0:T(8,128)(2,1)S(1)} %bitcast.243), channel_id=1, source_target_pairs={{0,2},{1,3},{2,0},{3,1},{4,6},{5,7},{6,4},{7,5},{8,10},{9,11},{10,... | collective-permute-start | bytes 1327112 | tf_op jit(solution)/shard_map/ppermute | solution.py:52
  112.3 22.1 %collective-permute-start.19 = (bf16[64,160]{1,0:T(8,128)(2,1)S(1)}, bf16[64,160]{1,0:T(8,128)(2,1)S(1)}, u32[]{:S(2)}, u32[]{:S(2)}) collective-permute-start(bf16[64,160]{1,0:T(8,128)(2,1)S(1)} %bitcast.252), channel_id=1, source_target_pairs={{0,2},{1,3},{2,0},{3,1},{4,6},{5,7},{6,4},{7,5},{8,10},{9,11},{10,... | collective-permute-start | bytes 61448 | tf_op jit(solution)/shard_map/ppermute | solution.py:52
  134.6 4.6 %collective-permute-start.20 = (bf16[864,1024]{1,0:T(8,128)(2,1)}, bf16[864,1024]{1,0:T(8,128)(2,1)S(1)}, u32[]{:S(2)}, u32[]{:S(2)}) collective-permute-start(bf16[864,1024]{1,0:T(8,128)(2,1)} %get-tuple-element.101), channel_id=1, source_target_pairs={{0,4},{1,5},{2,6},{3,7},{4,0},{5,1},{6,2},{7,3},{8,12},{9,13},{10,... | collective-permute-start | bytes 5308424 | tf_op jit(solution)/shard_map/ppermute | solution.py:52
  134.6 4.5 %collective-permute-start.21 = (bf16[2,64,160]{2,1,0:T(8,128)(2,1)S(1)}, bf16[2,64,160]{2,1,0:T(8,128)(2,1)S(1)}, u32[]{:S(2)}, u32[]{:S(2)}) collective-permute-start(bf16[2,64,160]{2,1,0:T(8,128)(2,1)S(1)} %pad_maximum_fusion.10), channel_id=1, source_target_pairs={{0,1},{1,0},{2,3},{3,2},{4,5},{5,4},{6,7},{7,6},{8,9},{9,8},{10,11... | collective-permute-start | bytes 122888 | tf_op jit(solution)/shard_map/ppermute | solution.py:52
  139.2 5.3 %collective-permute-start.23 = (bf16[2,2,64,160]{3,2,1,0:T(8,128)(2,1)S(1)}, bf16[2,2,64,160]{3,2,1,0:T(8,128)(2,1)S(1)}, u32[]{:S(2)}, u32[]{:S(2)}) collective-permute-start(bf16[2,2,64,160]{3,2,1,0:T(8,128)(2,1)S(1)} %pad_maximum_fusion.9), channel_id=1, source_target_pairs={{0,4},{1,5},{2,6},{3,7},{4,0},{5,1},{6,2},{7,3},{8,12},{9,13},{10,... | collective-permute-start | bytes 245768 | tf_op jit(solution)/shard_map/ppermute | solution.py:52
  139.3 13.5 %collective-permute-start.27 = (bf16[432,256]{1,0:T(8,128)(2,1)}, bf16[432,256]{1,0:T(8,128)(2,1)S(1)}, u32[]{:S(2)}, u32[]{:S(2)}) collective-permute-start(bf16[432,256]{1,0:T(8,128)(2,1)} %bitcast.41), channel_id=1, source_target_pairs={{0,6},{1,7},{2,4},{3,5},{4,2},{5,3},{6,0},{7,1},{8,14},{9,15},{10,... | collective-permute-start | bytes 663560 | tf_op jit(solution)/shard_map/ppermute | solution.py:52
  143.5 26.5 %collective-permute-start.22 = (bf16[432,1024]{1,0:T(8,128)(2,1)}, bf16[432,1024]{1,0:T(8,128)(2,1)S(1)}, u32[]{:S(2)}, u32[]{:S(2)}) collective-permute-start(bf16[432,1024]{1,0:T(8,128)(2,1)} %get-tuple-element.171), channel_id=1, source_target_pairs={{0,1},{1,0},{2,3},{3,2},{4,5},{5,4},{6,7},{7,6},{8,9},{9,8},{10,11... | collective-permute-start | bytes 2654216 | tf_op jit(solution)/shard_map/ppermute | solution.py:52
  144.6 9.8 %collective-permute-start.26 = (bf16[2,2,2,64,160]{4,3,2,1,0:T(8,128)(2,1)S(1)}, bf16[2,2,2,64,160]{4,3,2,1,0:T(8,128)(2,1)S(1)}, u32[]{:S(2)}, u32[]{:S(2)}) collective-permute-start(bf16[2,2,2,64,160]{4,3,2,1,0:T(8,128)(2,1)S(1)} %pad_maximum_fusion.8), channel_id=1, source_target_pairs={{0,8},{1,9},{2,10},{3,11},{4,12},{5,13},{6,14},{7,15},{8,0},{9,1},... | collective-permute-start | bytes 491528 | tf_op jit(solution)/shard_map/ppermute | solution.py:52
  145.7 11.9 %collective-permute-start.25 = (bf16[2,2,2,64,160]{4,3,2,1,0:T(8,128)(2,1)S(1)}, bf16[2,2,2,64,160]{4,3,2,1,0:T(8,128)(2,1)S(1)}, u32[]{:S(2)}, u32[]{:S(2)}) collective-permute-start(bf16[2,2,2,64,160]{4,3,2,1,0:T(8,128)(2,1)S(1)} %pad_maximum_fusion.8), channel_id=1, source_target_pairs={{0,16},{1,17},{2,18},{3,19},{4,20},{5,21},{6,22},{7,23},{8,24},{9,... | collective-permute-start | bytes 491528 | tf_op jit(solution)/shard_map/ppermute | solution.py:52
  146.7 12.5 %collective-permute-start.24 = (bf16[2,2,2,64,160]{4,3,2,1,0:T(8,128)(2,1)S(1)}, bf16[2,2,2,64,160]{4,3,2,1,0:T(8,128)(2,1)S(1)}, u32[]{:S(2)}, u32[]{:S(2)}) collective-permute-start(bf16[2,2,2,64,160]{4,3,2,1,0:T(8,128)(2,1)S(1)} %pad_maximum_fusion.8), channel_id=1, source_target_pairs={{0,24},{1,25},{2,26},{3,27},{4,28},{5,29},{6,30},{7,31},{8,16},{9,... | collective-permute-start | bytes 491528 | tf_op jit(solution)/shard_map/ppermute | solution.py:52
  176.1 3.9 %collective-permute-start.30 = (f32[24,256]{1,0:T(8,128)S(1)}, f32[24,256]{1,0:T(8,128)S(1)}, u32[]{:S(2)}, u32[]{:S(2)}) collective-permute-start(f32[24,256]{1,0:T(8,128)S(1)} %pad_maximum_fusion.11), channel_id=1, source_target_pairs={{0,16},{1,17},{2,18},{3,19},{4,20},{5,21},{6,22},{7,23},{8,24},{9,... | collective-permute-start | bytes 73736 | tf_op jit(solution)/shard_map/ppermute | solution.py:52
  177.7 4.7 %collective-permute-start.31 = (f32[24,256]{1,0:T(8,128)S(1)}, f32[24,256]{1,0:T(8,128)S(1)}, u32[]{:S(2)}, u32[]{:S(2)}) collective-permute-start(f32[24,256]{1,0:T(8,128)S(1)} %pad_maximum_fusion.11), channel_id=1, source_target_pairs={{0,24},{1,25},{2,26},{3,27},{4,28},{5,29},{6,30},{7,31},{8,16},{9,... | collective-permute-start | bytes 73736 | tf_op jit(solution)/shard_map/ppermute | solution.py:52
  182.6 5.7 %collective-permute-start.34 = (f32[24,256]{1,0:T(8,128)S(1)}, f32[24,256]{1,0:T(8,128)S(1)}, u32[]{:S(2)}, u32[]{:S(2)}) collective-permute-start(f32[24,256]{1,0:T(8,128)S(1)} %pad_maximum_fusion.12.refs_0_), channel_id=1, source_target_pairs={{0,3},{1,2},{2,1},{3,0},{4,7},{5,6},{6,5},{7,4},{8,11},{9,10},{10,... | collective-permute-start | bytes 73736 | tf_op jit(solution)/shard_map/ppermute | solution.py:52
  184.5 4.7 %collective-permute-start.33 = (f32[24,256]{1,0:T(8,128)S(1)}, f32[24,256]{1,0:T(8,128)S(1)}, u32[]{:S(2)}, u32[]{:S(2)}) collective-permute-start(f32[24,256]{1,0:T(8,128)S(1)} %pad_maximum_fusion.12.refs_0_), channel_id=1, source_target_pairs={{0,2},{1,3},{2,0},{3,1},{4,6},{5,7},{6,4},{7,5},{8,10},{9,11},{10,... | collective-permute-start | bytes 73736 | tf_op jit(solution)/shard_map/ppermute | solution.py:52
  184.5 4.7 %collective-permute-start.32 = (f32[24,256]{1,0:T(8,128)S(1)}, f32[24,256]{1,0:T(8,128)S(1)}, u32[]{:S(2)}, u32[]{:S(2)}) collective-permute-start(f32[24,256]{1,0:T(8,128)S(1)} %pad_maximum_fusion.12.refs_0_), channel_id=1, source_target_pairs={{0,1},{1,0},{2,3},{3,2},{4,5},{5,4},{6,7},{7,6},{8,9},{9,8},{10,11... | collective-permute-start | bytes 73736 | tf_op jit(solution)/shard_map/ppermute | solution.py:52
  195.5 4.2 %collective-permute-start.37 = (f32[8,256]{1,0:T(8,128)S(1)}, f32[8,256]{1,0:T(8,128)S(1)}, u32[]{:S(2)}, u32[]{:S(2)}) collective-permute-start(f32[8,256]{1,0:T(8,128)S(1)} %pad_maximum_fusion.13), channel_id=1, source_target_pairs={{0,16},{1,17},{2,18},{3,19},{4,20},{5,21},{6,22},{7,23},{8,24},{9,... | collective-permute-start | bytes 24584 | tf_op jit(solution)/shard_map/ppermute | solution.py:52
  196.6 4.5 %collective-permute-start.38 = (f32[8,256]{1,0:T(8,128)S(1)}, f32[8,256]{1,0:T(8,128)S(1)}, u32[]{:S(2)}, u32[]{:S(2)}) collective-permute-start(f32[8,256]{1,0:T(8,128)S(1)} %pad_maximum_fusion.13), channel_id=1, source_target_pairs={{0,24},{1,25},{2,26},{3,27},{4,28},{5,29},{6,30},{7,31},{8,16},{9,... | collective-permute-start | bytes 24584 | tf_op jit(solution)/shard_map/ppermute | solution.py:52
  201.7 4.6 %collective-permute-start.40 = (f32[8,256]{1,0:T(8,128)S(1)}, f32[8,256]{1,0:T(8,128)S(1)}, u32[]{:S(2)}, u32[]{:S(2)}) collective-permute-start(f32[8,256]{1,0:T(8,128)S(1)} %pad_maximum_fusion.14), channel_id=1, source_target_pairs={{0,2},{1,3},{2,0},{3,1},{4,6},{5,7},{6,4},{7,5},{8,10},{9,11},{10,... | collective-permute-start | bytes 24584 | tf_op jit(solution)/shard_map/ppermute | solution.py:52
  203.8 5.4 %collective-permute-start.41 = (f32[8,256]{1,0:T(8,128)S(1)}, f32[8,256]{1,0:T(8,128)S(1)}, u32[]{:S(2)}, u32[]{:S(2)}) collective-permute-start(f32[8,256]{1,0:T(8,128)S(1)} %pad_maximum_fusion.14), channel_id=1, source_target_pairs={{0,3},{1,2},{2,1},{3,0},{4,7},{5,6},{6,5},{7,4},{8,11},{9,10},{10,... | collective-permute-start | bytes 24584 | tf_op jit(solution)/shard_map/ppermute | solution.py:52
  212.3 3.9 %collective-permute-start.44 = (f32[8,256]{1,0:T(8,128)S(1)}, f32[8,256]{1,0:T(8,128)S(1)}, u32[]{:S(2)}, u32[]{:S(2)}) collective-permute-start(f32[8,256]{1,0:T(8,128)S(1)} %fusion.41), channel_id=1, source_target_pairs={{0,16},{1,17},{2,18},{3,19},{4,20},{5,21},{6,22},{7,23},{8,24},{9,... | collective-permute-start | bytes 24584 | tf_op jit(solution)/shard_map/ppermute | solution.py:52
  213.8 4.5 %collective-permute-start.45 = (f32[8,256]{1,0:T(8,128)S(1)}, f32[8,256]{1,0:T(8,128)S(1)}, u32[]{:S(2)}, u32[]{:S(2)}) collective-permute-start(f32[8,256]{1,0:T(8,128)S(1)} %fusion.41), channel_id=1, source_target_pairs={{0,24},{1,25},{2,26},{3,27},{4,28},{5,29},{6,30},{7,31},{8,16},{9,... | collective-permute-start | bytes 24584 | tf_op jit(solution)/shard_map/ppermute | solution.py:52
  215.8 7.2 %collective-permute-start.56 = (bf16[16,512]{1,0:T(8,128)(2,1)S(1)}, bf16[16,512]{1,0:T(8,128)(2,1)S(1)}, u32[]{:S(2)}, u32[]{:S(2)}) collective-permute-start(bf16[16,512]{1,0:T(8,128)(2,1)S(1)} %copy-done.45), channel_id=1, source_target_pairs={{0,2},{1,3},{2,0},{3,1},{4,6},{5,7},{6,4},{7,5},{8,10},{9,11},{10,... | collective-permute-start | bytes 49160 | tf_op jit(solution)/shard_map/ppermute | solution.py:52
  218.6 5.5 %collective-permute-start.48 = (f32[8,256]{1,0:T(8,128)S(1)}, f32[8,256]{1,0:T(8,128)S(1)}, u32[]{:S(2)}, u32[]{:S(2)}) collective-permute-start(f32[8,256]{1,0:T(8,128)S(1)} %add_add_fusion.2.refs_0_), channel_id=1, source_target_pairs={{0,3},{1,2},{2,1},{3,0},{4,7},{5,6},{6,5},{7,4},{8,11},{9,10},{10,... | collective-permute-start | bytes 24584 | tf_op jit(solution)/shard_map/ppermute | solution.py:52
  220.4 4.5 %collective-permute-start.47 = (f32[8,256]{1,0:T(8,128)S(1)}, f32[8,256]{1,0:T(8,128)S(1)}, u32[]{:S(2)}, u32[]{:S(2)}) collective-permute-start(f32[8,256]{1,0:T(8,128)S(1)} %add_add_fusion.2.refs_0_), channel_id=1, source_target_pairs={{0,2},{1,3},{2,0},{3,1},{4,6},{5,7},{6,4},{7,5},{8,10},{9,11},{10,... | collective-permute-start | bytes 24584 | tf_op jit(solution)/shard_map/ppermute | solution.py:52
  220.4 4.5 %collective-permute-start.46 = (f32[8,256]{1,0:T(8,128)S(1)}, f32[8,256]{1,0:T(8,128)S(1)}, u32[]{:S(2)}, u32[]{:S(2)}) collective-permute-start(f32[8,256]{1,0:T(8,128)S(1)} %add_add_fusion.2.refs_0_), channel_id=1, source_target_pairs={{0,1},{1,0},{2,3},{3,2},{4,5},{5,4},{6,7},{7,6},{8,9},{9,8},{10,11... | collective-permute-start | bytes 24584 | tf_op jit(solution)/shard_map/ppermute | solution.py:52
  228.1 4.7 %collective-permute-start.52 = (f32[16,256]{1,0:T(8,128)S(1)}, f32[16,256]{1,0:T(8,128)S(1)}, u32[]{:S(2)}, u32[]{:S(2)}) collective-permute-start(f32[16,256]{1,0:T(8,128)S(1)} %add.282), channel_id=1, source_target_pairs={{0,24},{1,25},{2,26},{3,27},{4,28},{5,29},{6,30},{7,31},{8,16},{9,... | collective-permute-start | bytes 49160 | tf_op jit(solution)/shard_map/ppermute | solution.py:52
  234.2 5.6 %collective-permute-start.55 = (f32[16,256]{1,0:T(8,128)S(1)}, f32[16,256]{1,0:T(8,128)S(1)}, u32[]{:S(2)}, u32[]{:S(2)}) collective-permute-start(f32[16,256]{1,0:T(8,128)S(1)} %add_add_fusion.1.refs_0_), channel_id=1, source_target_pairs={{0,3},{1,2},{2,1},{3,0},{4,7},{5,6},{6,5},{7,4},{8,11},{9,10},{10,... | collective-permute-start | bytes 49160 | tf_op jit(solution)/shard_map/ppermute | solution.py:52
  236.2 4.8 %collective-permute-start.54 = (f32[16,256]{1,0:T(8,128)S(1)}, f32[16,256]{1,0:T(8,128)S(1)}, u32[]{:S(2)}, u32[]{:S(2)}) collective-permute-start(f32[16,256]{1,0:T(8,128)S(1)} %add_add_fusion.1.refs_0_), channel_id=1, source_target_pairs={{0,2},{1,3},{2,0},{3,1},{4,6},{5,7},{6,4},{7,5},{8,10},{9,11},{10,... | collective-permute-start | bytes 49160 | tf_op jit(solution)/shard_map/ppermute | solution.py:52
  243.1 35.4 %collective-permute-start.60 = (bf16[432,1024]{1,0:T(8,128)(2,1)S(1)}, bf16[432,1024]{1,0:T(8,128)(2,1)}, u32[]{:S(2)}, u32[]{:S(2)}) collective-permute-start(bf16[432,1024]{1,0:T(8,128)(2,1)S(1)} %get-tuple-element.121.refs_0_.refs_4_), channel_id=1, source_target_pairs={{0,4},{1,5},{2,6},{3,7},{4,0},{5,1},{6,2},{7,3},{8,12},{9,13},{10,... | collective-permute-start | bytes 2654216 | tf_op jit(solution)/shard_map/ppermute | solution.py:52
  243.2 31.6 %collective-permute-start.57 = (bf16[432,1024]{1,0:T(8,128)(2,1)S(1)}, bf16[432,1024]{1,0:T(8,128)(2,1)}, u32[]{:S(2)}, u32[]{:S(2)}) collective-permute-start(bf16[432,1024]{1,0:T(8,128)(2,1)S(1)} %get-tuple-element.121.refs_0_.refs_4_), channel_id=1, source_target_pairs={{0,1},{1,0},{2,3},{3,2},{4,5},{5,4},{6,7},{7,6},{8,9},{9,8},{10,11... | collective-permute-start | bytes 2654216 | tf_op jit(solution)/shard_map/ppermute | solution.py:52
  246.7 26.9 %collective-permute-start.58 = (bf16[432,512]{1,0:T(8,128)(2,1)S(1)}, bf16[432,512]{1,0:T(8,128)(2,1)}, u32[]{:S(2)}, u32[]{:S(2)}) collective-permute-start(bf16[432,512]{1,0:T(8,128)(2,1)S(1)} %get-tuple-element.122), channel_id=1, source_target_pairs={{0,2},{1,3},{2,0},{3,1},{4,6},{5,7},{6,4},{7,5},{8,10},{9,11},{10,... | collective-permute-start | bytes 1327112 | tf_op jit(solution)/shard_map/ppermute | solution.py:52
  276.7 22.9 %collective-permute-start.65 = (bf16[432,512]{1,0:T(8,128)(2,1)}, bf16[432,512]{1,0:T(8,128)(2,1)S(1)}, u32[]{:S(2)}, u32[]{:S(2)}) collective-permute-start(bf16[432,512]{1,0:T(8,128)(2,1)} %collective-permute-done.58.refs_8_), channel_id=1, source_target_pairs={{0,1},{1,0},{2,3},{3,2},{4,5},{5,4},{6,7},{7,6},{8,9},{9,8},{10,11... | collective-permute-start | bytes 1327112 | tf_op jit(solution)/shard_map/ppermute | solution.py:52
  278.6 22.7 %collective-permute-start.63 = (bf16[2,2,2,64,160]{4,3,2,1,0:T(8,128)(2,1)S(1)}, bf16[2,2,2,64,160]{4,3,2,1,0:T(8,128)(2,1)S(1)}, u32[]{:S(2)}, u32[]{:S(2)}) collective-permute-start(bf16[2,2,2,64,160]{4,3,2,1,0:T(8,128)(2,1)S(1)} %fusion.6), channel_id=1, source_target_pairs={{0,8},{1,9},{2,10},{3,11},{4,12},{5,13},{6,14},{7,15},{8,0},{9,1},... | collective-permute-start | bytes 491528 | tf_op jit(solution)/shard_map/ppermute | solution.py:52
  279.7 21.0 %collective-permute-start.66 = (bf16[432,512]{1,0:T(8,128)(2,1)}, bf16[432,512]{1,0:T(8,128)(2,1)S(1)}, u32[]{:S(2)}, u32[]{:S(2)}) collective-permute-start(bf16[432,512]{1,0:T(8,128)(2,1)} %get-tuple-element.135), channel_id=1, source_target_pairs={{0,3},{1,2},{2,1},{3,0},{4,7},{5,6},{6,5},{7,4},{8,11},{9,10},{10,... | collective-permute-start | bytes 1327112 | tf_op jit(solution)/shard_map/ppermute | solution.py:52
  299.6 25.5 %collective-permute-start.62 = (bf16[432,256]{1,0:T(8,128)(2,1)S(1)}, bf16[432,256]{1,0:T(8,128)(2,1)S(1)}, u32[]{:S(2)}, u32[]{:S(2)}) collective-permute-start(bf16[432,256]{1,0:T(8,128)(2,1)S(1)} %copy-done.33), channel_id=1, source_target_pairs={{0,6},{1,7},{2,4},{3,5},{4,2},{5,3},{6,0},{7,1},{8,14},{9,15},{10,... | collective-permute-start | bytes 663560 | tf_op jit(solution)/shard_map/ppermute | solution.py:52
  301.4 24.9 %collective-permute-start.64 = (bf16[1,2,2,64,160]{4,3,2,1,0:T(8,128)(2,1)S(1)}, bf16[1,2,2,64,160]{4,3,2,1,0:T(8,128)(2,1)S(1)}, u32[]{:S(2)}, u32[]{:S(2)}) collective-permute-start(bf16[1,2,2,64,160]{4,3,2,1,0:T(8,128)(2,1)S(1)} %select_bitcast_fusion.8), channel_id=1, source_target_pairs={{0,16},{1,17},{2,18},{3,19},{4,20},{5,21},{6,22},{7,23},{8,24},{9,... | collective-permute-start | bytes 245768 | tf_op jit(solution)/shard_map/ppermute | solution.py:52
  303.4 28.0 %collective-permute-start.69 = (bf16[432,512]{1,0:T(8,128)(2,1)}, bf16[432,512]{1,0:T(8,128)(2,1)}, u32[]{:S(2)}, u32[]{:S(2)}) collective-permute-start(bf16[432,512]{1,0:T(8,128)(2,1)} %get-tuple-element.138), channel_id=1, source_target_pairs={{0,2},{1,3},{2,0},{3,1},{4,6},{5,7},{6,4},{7,5},{8,10},{9,11},{10,... | collective-permute-start | bytes 1327112 | tf_op jit(solution)/shard_map/ppermute | solution.py:52
  304.9 26.4 %collective-permute-start.70 = (bf16[432,512]{1,0:T(8,128)(2,1)}, bf16[432,512]{1,0:T(8,128)(2,1)S(1)}, u32[]{:S(2)}, u32[]{:S(2)}) collective-permute-start(bf16[432,512]{1,0:T(8,128)(2,1)} %get-tuple-element.139), channel_id=1, source_target_pairs={{0,1},{1,0},{2,3},{3,2},{4,5},{5,4},{6,7},{7,6},{8,9},{9,8},{10,11... | collective-permute-start | bytes 1327112 | tf_op jit(solution)/shard_map/ppermute | solution.py:52
  323.5 12.6 %collective-permute-start.74 = (bf16[29,64,128]{2,1,0:T(8,128)(2,1)}, bf16[29,64,128]{2,1,0:T(8,128)(2,1)S(1)}, u32[]{:S(2)}, u32[]{:S(2)}) collective-permute-start(bf16[29,64,128]{2,1,0:T(8,128)(2,1)} %get-tuple-element.144), channel_id=1, source_target_pairs={{0,16},{1,17},{2,18},{3,19},{4,20},{5,21},{6,22},{7,23},{8,24},{9,... | collective-permute-start | bytes 1425416 | tf_op jit(solution)/shard_map/ppermute | solution.py:52
  325.1 12.2 %collective-permute-start.75 = (bf16[29,64,128]{2,1,0:T(8,128)(2,1)}, bf16[29,64,128]{2,1,0:T(8,128)(2,1)S(1)}, u32[]{:S(2)}, u32[]{:S(2)}) collective-permute-start(bf16[29,64,128]{2,1,0:T(8,128)(2,1)} %get-tuple-element.145), channel_id=1, source_target_pairs={{0,8},{1,9},{2,10},{3,11},{4,12},{5,13},{6,14},{7,15},{8,0},{9,1},... | collective-permute-start | bytes 1425416 | tf_op jit(solution)/shard_map/ppermute | solution.py:52
  331.4 14.6 %collective-permute-start.78 = (bf16[2,64,160]{2,1,0:T(8,128)(2,1)S(1)}, bf16[2,64,160]{2,1,0:T(8,128)(2,1)S(1)}, u32[]{:S(2)}, u32[]{:S(2)}) collective-permute-start(bf16[2,64,160]{2,1,0:T(8,128)(2,1)S(1)} %select_bitcast_fusion.11), channel_id=1, source_target_pairs={{0,2},{1,3},{2,0},{3,1},{4,6},{5,7},{6,4},{7,5},{8,10},{9,11},{10,... | collective-permute-start | bytes 122888 | tf_op jit(solution)/shard_map/ppermute | solution.py:52
  331.4 24.7 %collective-permute-start.71 = (bf16[432,512]{1,0:T(8,128)(2,1)}, bf16[432,512]{1,0:T(8,128)(2,1)S(1)}, u32[]{:S(2)}, u32[]{:S(2)}) collective-permute-start(bf16[432,512]{1,0:T(8,128)(2,1)} %get-tuple-element.140), channel_id=1, source_target_pairs={{0,2},{1,3},{2,0},{3,1},{4,6},{5,7},{6,4},{7,5},{8,10},{9,11},{10,... | collective-permute-start | bytes 1327112 | tf_op jit(solution)/shard_map/ppermute | solution.py:52
  334.3 21.9 %collective-permute-start.72 = (bf16[432,512]{1,0:T(8,128)(2,1)}, bf16[432,512]{1,0:T(8,128)(2,1)S(1)}, u32[]{:S(2)}, u32[]{:S(2)}) collective-permute-start(bf16[432,512]{1,0:T(8,128)(2,1)} %collective-permute-done.69), channel_id=1, source_target_pairs={{0,1},{1,0},{2,3},{3,2},{4,5},{5,4},{6,7},{7,6},{8,9},{9,8},{10,11... | collective-permute-start | bytes 1327112 | tf_op jit(solution)/shard_map/ppermute | solution.py:52
  338.6 21.3 %collective-permute-start.77 = (bf16[2,29,64,128]{3,2,1,0:T(8,128)(2,1)S(1)}, bf16[2,29,64,128]{3,2,1,0:T(8,128)(2,1)S(1)}, u32[]{:S(2)}, u32[]{:S(2)}) collective-permute-start(bf16[2,29,64,128]{3,2,1,0:T(8,128)(2,1)S(1)} %pad_maximum_fusion.1), channel_id=1, source_target_pairs={{0,16},{1,17},{2,18},{3,19},{4,20},{5,21},{6,22},{7,23},{8,24},{9,... | collective-permute-start | bytes 2850824 | tf_op jit(solution)/shard_map/ppermute | solution.py:52
  339.6 21.3 %collective-permute-start.76 = (bf16[2,29,64,128]{3,2,1,0:T(8,128)(2,1)S(1)}, bf16[2,29,64,128]{3,2,1,0:T(8,128)(2,1)S(1)}, u32[]{:S(2)}, u32[]{:S(2)}) collective-permute-start(bf16[2,29,64,128]{3,2,1,0:T(8,128)(2,1)S(1)} %pad_maximum_fusion), channel_id=1, source_target_pairs={{0,8},{1,9},{2,10},{3,11},{4,12},{5,13},{6,14},{7,15},{8,0},{9,1},... | collective-permute-start | bytes 2850824 | tf_op jit(solution)/shard_map/ppermute | solution.py:52
  356.4 6.2 %collective-permute-start.73 = (bf16[2,432,512]{2,1,0:T(8,128)(2,1)S(1)}, bf16[2,432,512]{2,1,0:T(8,128)(2,1)S(1)}, u32[]{:S(2)}, u32[]{:S(2)}) collective-permute-start(bf16[2,432,512]{2,1,0:T(8,128)(2,1)S(1)} %pad_maximum_fusion.3), channel_id=1, source_target_pairs={{0,4},{1,5},{2,6},{3,7},{4,0},{5,1},{6,2},{7,3},{8,12},{9,13},{10,... | collective-permute-start | bytes 2654216 | tf_op jit(solution)/shard_map/ppermute | solution.py:52
  361.6 11.6 %collective-permute-start.79 = (bf16[29,64,128]{2,1,0:T(8,128)(2,1)S(1)}, bf16[29,64,128]{2,1,0:T(8,128)(2,1)S(1)}, u32[]{:S(2)}, u32[]{:S(2)}) collective-permute-start(bf16[29,64,128]{2,1,0:T(8,128)(2,1)S(1)} %broadcast_select_fusion.7), channel_id=1, source_target_pairs={{0,1},{1,0},{2,3},{3,2},{4,5},{5,4},{6,7},{7,6},{8,9},{9,8},{10,11... | collective-permute-start | bytes 1425416 | tf_op jit(solution)/shard_map/ppermute | solution.py:52
  364.9 7.5 %collective-permute-start.81 = (bf16[1,64,160]{2,1,0:T(8,128)(2,1)S(1)}, bf16[1,64,160]{2,1,0:T(8,128)(2,1)S(1)}, u32[]{:S(2)}, u32[]{:S(2)}) collective-permute-start(bf16[1,64,160]{2,1,0:T(8,128)(2,1)S(1)} %select_bitcast_fusion.14), channel_id=1, source_target_pairs={{0,1},{1,0},{2,3},{3,2},{4,5},{5,4},{6,7},{7,6},{8,9},{9,8},{10,11... | collective-permute-start | bytes 61448 | tf_op jit(solution)/shard_map/ppermute | solution.py:52
  (73 other events, 448.0 us)
